TPU v7x, 512 devices: a whole 4x4x16 slice. The times are simulated.
512 devices in a mesh: col: 16 (over y, x_hi, core), blk: 32 (over z, x_lo).
Axes of the slice: x: 4 (x_hi: 2, x_lo: 2; x = x_hi * 2 + x_lo), y: 4, z: 16, core: 2. Of those that a mesh axis runs over, the one named last changes fastest.
Arguments:
- tokens: bfloat16 [2048, 6144], P('blk', 'col'), may hold values from -6 to 6
- route_ids: int32 [2048, 2], P('blk'), may hold values from 0 to 7, as said below
- route_gates: float32 [2048, 2], P('blk'), may hold values from 0.2 to 1
- gate_weight: bfloat16 [2, 6144, 16384], P(None, 'col', 'blk'), may hold values from -0.078125 to 0.078125
- up_weight: bfloat16 [2, 6144, 16384], P(None, 'col', 'blk'), may hold values from -0.078125 to 0.078125
- gate_scale: float32 [2, 48, 128], P(None, 'col', 'blk'), may hold values from 0.5 to 2
- up_scale: float32 [2, 48, 128], P(None, 'col', 'blk'), may hold values from 0.5 to 2
- down_weight: bfloat16 [2, 16384, 6144], P(None, 'blk', 'col'), may hold values from -0.046875 to 0.046875
- down_scale: float32 [2, 128, 48], P(None, 'blk', 'col'), may hold values from 0.5 to 2
Outputs:
- mixed: bfloat16 [2048, 6144], P('blk', 'col')
Inputs may be any that keep to these rules, and one draw needn't show every extreme that they name: `route_ids`: in each aligned block of 64 rows the two ids of a row differ, and each expert below 2 is named by at most 20 rows of the block; in every block one of them is named by exactly 20 rows.
All inputs are finite; a program needn't handle non-finite values.
Results may differ from a plain program's by a relative error of at most 0.0049.
Values may be sent and summed in bfloat16 or wider, within the bound.
No kernel may reach another device: no remote copies, remote signals or barrier semaphores. Data moves between devices by JAX's collectives and lax.ppermute only.
A program may use at most 64 MiB of HBM per device.

v0:
```python
import jax
import jax.numpy as jnp
from jax import lax
from jax.sharding import PartitionSpec as P

EXPW = 2
CAP = 20


def dispatch(route_ids, route_gates):
    expert_ids = jnp.arange(EXPW, dtype=jnp.int32)
    matches = route_ids[:, :, None] == expert_ids[None, None, :]
    chosen = jnp.any(matches, axis=1)
    combine_weights = jnp.sum(
        jnp.where(matches, route_gates[:, :, None], jnp.zeros((), route_gates.dtype)), axis=1
    )
    slot_index = jnp.cumsum(chosen.astype(jnp.int32), axis=0) - 1
    onehot = chosen[:, :, None] & (
        slot_index[:, :, None] == jnp.arange(CAP, dtype=jnp.int32)[None, None, :]
    )
    return (onehot, combine_weights)


def blocked(row_block, weight, scale):
    square = weight.shape[1] // scale.shape[1]
    running = jnp.zeros(row_block.shape[:2] + (weight.shape[2],), jnp.float32)
    for position in range(scale.shape[1]):
        offset = position * square
        product = jnp.einsum(
            "rek,ekf->ref",
            row_block[:, :, offset : offset + square],
            weight[:, offset : offset + square, :],
            preferred_element_type=jnp.float32,
        )
        running = running + product * jnp.repeat(scale[:, position, :], square, axis=-1)[None, :, :]
    return running


def activate(summed, hidden_width):
    return (jax.nn.silu(summed[:, :, :hidden_width]) * summed[:, :, hidden_width:]).astype(
        jnp.bfloat16
    )


def shards(
    tokens,
    route_ids,
    route_gates,
    gate_weight,
    up_weight,
    gate_scale,
    up_scale,
    down_weight,
    down_scale,
):
    onehot, combine_weights = dispatch(route_ids, route_gates)
    slot_rows = jnp.einsum(
        "tec,td->ced", onehot.astype(jnp.bfloat16), tokens, preferred_element_type=jnp.float32
    ).astype(jnp.bfloat16)
    portion = lax.all_gather(slot_rows, "blk", axis=0, tiled=True)
    partial_sums = jnp.concatenate(
        [blocked(portion, gate_weight, gate_scale), blocked(portion, up_weight, up_scale)], axis=-1
    )
    hidden_width = gate_weight.shape[2]
    summed = lax.psum(partial_sums, "col")
    hidden = activate(summed, hidden_width)
    expert_out = lax.psum_scatter(
        blocked(hidden, down_weight, down_scale), "blk", scatter_dimension=0, tiled=True
    )
    combine = onehot.astype(jnp.float32) * combine_weights[:, :, None]
    mixed = jnp.einsum("tec,ced->td", combine, expert_out, precision=lax.Precision.HIGHEST)
    return mixed.astype(jnp.bfloat16)


def solution(mesh):
    in_specs = (
        P("blk", "col"),
        P("blk", None),
        P("blk", None),
        P(None, "col", "blk"),
        P(None, "col", "blk"),
        P(None, "col", "blk"),
        P(None, "col", "blk"),
        P(None, "blk", "col"),
        P(None, "blk", "col"),
    )
    out_specs = P("blk", "col")
    return jax.shard_map(shards, mesh=mesh, in_specs=in_specs, out_specs=out_specs, check_vma=False)
```

profile of v0, /device:TPU:16, one launch (start us, length us, event | category | flops | bytes accessed | tf_op | source)
XLA Modules:
  0.0 550.4 jit_solution(4307508778404087508)
XLA Ops:
  6.5 0.8 fusion.42
  7.3 0.1 copy.62
  7.4 0.1 reduce_window_sum.11
  7.5 0.1 copy.63
  7.6 0.1 fusion.2
  7.8 74.2 %all_gather.3 = bf16[640,2,384]{2,1,0:T(2,128)(2,1)S(1)} all-gather(bf16[20,2,384]{2,1,0:T(2,128)(2,1)S(1)} %copy.64), channel_id=1, replica_groups=mesh['col'=16,'blk'=32] {'blk'}, dimensions={0}, use_global_device_ids=true | all-gather | bytes 1013760 | tf_op jit(solution)/shard_map/all_gather | solution.py:60
  82.0 0.7 fusion.44
  82.7 0.6 fusion.14
  83.3 0.6 fusion.18
  83.9 0.5 fusion.12
  84.4 0.6 fusion.16
  85.0 0.1 broadcast_bitcast_fusion.7
  85.3 0.9 add_bitcast_fusion.1
  86.2 0.9 add_bitcast_fusion
  87.2 2.7 pad_maximum_fusion
  89.9 0.6 copy-done.4
  90.5 0.1 fusion.45
  90.6 0.1 copy.81
  90.7 0.1 copy.79
  90.8 0.1 copy.77
  90.9 0.1 copy.75
  91.3 163.7 %all-reduce.4.cloned.1.call-done = f32[640,2,1024]{0,2,1:T(8,128)} async-done(((f32[640,2,1024]{0,2,1:T(8,128)}), f32[640,2,1024]{0,2,1:T(8,128)}) %all-reduce.4.cloned.1.call-update) | async-done | bytes 5242896 | tf_op jit(solution)/shard_map/psum | solution.py:65
  255.0 3.2 fusion
  258.3 0.5 fusion.4
  258.8 0.5 fusion.6
  259.2 0.5 fusion.8
  259.7 0.7 add_bitcast_fusion.2
  260.5 2.8 copy.82
  263.3 1.3 dynamic-slice
  265.2 276.6 %all-reduce.6.cloned.1.call-done = f32[640,2,384]{2,1,0:T(2,128)} async-done(((f32[640,2,384]{2,1,0:T(2,128)}), f32[640,2,384]{2,1,0:T(2,128)}) %all-reduce.6.cloned.1.call-update) | async-done | bytes 1966096
  541.8 0.8 constant_dynamic-slice_fusion
  542.7 0.9 fusion.1
  (42 shorter events, 0.7 us)
Async XLA Ops:
  6.5 1.1 copy-start
  6.5 76.1 %copy-start.1 = (bf16[2,384,512]{2,1,0:T(8,128)(2,1)S(1)}, bf16[2,384,512]{2,1,0:T(8,128)(2,1)}, u32[]{:S(2)}) copy-start(bf16[2,384,512]{2,1,0:T(8,128)(2,1)} %param.12) | copy-start | bytes 2359300
  6.5 248.5 %all-reduce.4.cloned.1.call-start = ((), (), s32[]{:S(2)}) async-start(), calls=%async_computation | async-start | bytes 10485760 | tf_op jit(solution)/shard_map/psum | solution.py:65
  82.7 1.1 copy-start.2
  83.8 1.1 copy-start.5
  83.8 1.3 copy-start.6
  89.8 0.7 copy-start.4
  89.9 451.9 %all-reduce.6.cloned.1.call-start = ((), (), s32[]{:S(2)}) async-start(), calls=%async_computation.1 | async-start | bytes 3932160
  91.3 167.0 %copy-start.3 = (bf16[2,512,384]{2,1,0:T(8,128)(2,1)S(1)}, bf16[2,512,384]{2,1,0:T(8,128)(2,1)}, u32[]{:S(2)}) copy-start(bf16[2,512,384]{2,1,0:T(8,128)(2,1)} %param.16) | copy-start | bytes 2359300
  260.4 4.8 copy-start.7
  260.5 4.8 copy-start.8
Sparse Core Ops, SparseCore 0:
  90.0 165.0 all-reduce.3
  263.4 278.3 all-reduce.5
where the time goes:
time: 551 us; the launch traced here: 550 us
  waiting for transfers between devices  440 us (80%)
  blocking collectives  74.2 us (13%)
  between operations  14.3 us (3%)
  local copies, waits for them, and re-layouts  7.5 us (1%)
  matrix products  7.24 us (1%)
  other arithmetic  6.81 us (1%)
    unnamed x3, waiting for transfers between devices  277 us
    psum x1, waiting for transfers between devices, shards(): summed = lax.psum(partial_sums, 'col')  164 us
    all_gather x1, blocking collectives, shards(): portion = lax.all_gather(slot_rows, 'blk', axis=0, tiled=True)  74.2 us
  transfers between devices with their start and end apart: 2, of which 2 were waited for; matrix products, arithmetic and copies ran while one was open for 0% of the time, Pallas kernels for 0%

commit v1 on v0

v1 whole, which is shorter than its diff:
```python
import jax
import jax.numpy as jnp
from jax import lax
from jax.sharding import Mesh, PartitionSpec as P

EXPW = 2
CAP = 20
SB = 128
COL = ("y", "xh", "core")
BLK = ("zh", "zl", "xl")
SIZES = {"y": 4, "xh": 2, "core": 2, "zh": 4, "zl": 4, "xl": 2}
F32 = jnp.float32
BF16 = jnp.bfloat16


def dispatch(route_ids, route_gates):
    expert_ids = jnp.arange(EXPW, dtype=jnp.int32)
    matches = route_ids[:, :, None] == expert_ids[None, None, :]
    chosen = jnp.any(matches, axis=1)
    combine_weights = jnp.sum(
        jnp.where(matches, route_gates[:, :, None], jnp.zeros((), route_gates.dtype)), axis=1
    )
    slot_index = jnp.cumsum(chosen.astype(jnp.int32), axis=0) - 1
    onehot = chosen[:, :, None] & (
        slot_index[:, :, None] == jnp.arange(CAP, dtype=jnp.int32)[None, None, :]
    )
    return (onehot, combine_weights)


def swap(value):
    return lax.ppermute(value, "core", [(0, 1), (1, 0)])


def gather(value, axes, count):
    return lax.all_to_all(
        jnp.broadcast_to(value[None], (count,) + value.shape), axes, 0, 0, tiled=True
    )


def exchange_sum(value, axes):
    received = lax.all_to_all(value, axes, 0, 0, tiled=True)
    return jnp.sum(received.astype(F32), axis=0)


def blocked(rows, weight, scale):
    running = jnp.zeros((rows.shape[0], weight.shape[1]), F32)
    for position in range(scale.shape[0]):
        cut = slice(position * SB, (position + 1) * SB)
        product = jnp.dot(rows[:, cut], weight[cut], preferred_element_type=F32)
        running = running + product * jnp.repeat(scale[position], SB)[None, :]
    return running


def both_cores(array, core, axis):
    own = lax.dynamic_index_in_dim(array, core, 0, keepdims=False)
    other = swap(lax.dynamic_index_in_dim(array, 1 - core, 0, keepdims=False))
    first = jnp.where(core == 0, own, other)
    second = jnp.where(core == 0, other, own)
    return jnp.concatenate([first, second], axis=axis)


def shards(
    tokens,
    route_ids,
    route_gates,
    gate_weight,
    up_weight,
    gate_scale,
    up_scale,
    down_weight,
    down_scale,
):
    core = lax.axis_index("core")
    width = tokens.shape[1]
    hidden_width = gate_weight.shape[2]
    other_tokens = swap(tokens)
    tokens2 = jnp.concatenate(
        [
            jnp.where(core == 0, tokens, other_tokens),
            jnp.where(core == 0, other_tokens, tokens),
        ],
        axis=1,
    )
    onehot, combine_weights = dispatch(route_ids, route_gates)
    mine = lax.dynamic_index_in_dim(onehot, core, 1, keepdims=False)
    slot_rows = jnp.einsum(
        "tc,td->cd", mine.astype(BF16), tokens2, preferred_element_type=F32
    ).astype(BF16)
    portion = gather(slot_rows, "zh", 4).reshape(4 * CAP, 2 * width)
    portion = gather(portion, ("zl", "xl"), 8).reshape(32 * CAP, 2 * width)

    gate_up_weight = both_cores(jnp.concatenate([gate_weight, up_weight], axis=2), core, 0)
    gate_up_scale = both_cores(jnp.concatenate([gate_scale, up_scale], axis=2), core, 0)
    down_both = both_cores(down_weight, core, 1)
    down_scale_both = both_cores(down_scale, core, 1)

    partial_sums = blocked(portion, gate_up_weight, gate_up_scale).astype(BF16)
    summed = exchange_sum(partial_sums.reshape(8, 4 * CAP, 2 * hidden_width), ("y", "xh"))
    hidden = (jax.nn.silu(summed[:, :hidden_width]) * summed[:, hidden_width:]).astype(BF16)
    hidden = gather(hidden, ("y", "xh"), 8).reshape(32 * CAP, hidden_width)
    down = blocked(hidden, down_both, down_scale_both).astype(BF16)
    down = exchange_sum(down.reshape(8, 4 * CAP, 2 * width), ("zl", "xl")).astype(BF16)
    expert_out = exchange_sum(down.reshape(4, CAP, 2 * width), "zh")

    kept = lax.dynamic_slice_in_dim(expert_out, core * width, width, 1)
    given = swap(lax.dynamic_slice_in_dim(expert_out, (1 - core) * width, width, 1))
    first = jnp.where(core == 0, kept, given)
    second = jnp.where(core == 0, given, kept)
    combine = onehot.astype(F32) * combine_weights[:, :, None]
    mixed = jnp.dot(combine[:, 0], first, precision=lax.Precision.HIGHEST) + jnp.dot(
        combine[:, 1], second, precision=lax.Precision.HIGHEST
    )
    return mixed.astype(BF16)


def solution(mesh):
    parts = Mesh(mesh.devices.reshape(tuple(SIZES.values())), tuple(SIZES))
    in_specs = (
        P(BLK, COL),
        P(BLK, None),
        P(BLK, None),
        P(None, COL, BLK),
        P(None, COL, BLK),
        P(None, COL, BLK),
        P(None, COL, BLK),
        P(None, BLK, COL),
        P(None, BLK, COL),
    )
    return jax.shard_map(
        shards, mesh=parts, in_specs=in_specs, out_specs=P(BLK, COL), check_vma=False
    )
```

time: 551 us -> 166 us (0.30)
  the two profiles are of different devices: /device:TPU:16 before, /device:TPU:1 now
where the time goes in v1:
time: 166 us; the launch traced here: 165 us
  starting transfers between devices  51.8 us (31%)
  blocking collectives  51.8 us (31%)
  waiting for transfers between devices  47 us (28%)
  matrix products  7.86 us (5%)
  local copies, waits for them, and re-layouts  3.91 us (2%)
  other arithmetic  2.44 us (1%)
    ppermute x6, starting transfers between devices, swap(): return lax.ppermute(value, 'core', [(0, 1), (1, 0)])  29.9 us
    all_to_all x1, blocking collectives, exchange_sum(): received = lax.all_to_all(value, axes, 0, 0, tiled=True)  29.8 us
    all_to_all x2, waiting for transfers between devices, gather(): lax.all_to_all(jnp.broadcast_to(value[None], (count,) + value.shape), axe...  22.5 us
    all_to_all x1, blocking collectives, gather(): lax.all_to_all(jnp.broadcast_to(value[None], (count,) + value.shape), axe...  22 us
    all_to_all x2, waiting for transfers between devices, exchange_sum(): received = lax.all_to_all(value, axes, 0, 0, tiled=True)  20.8 us
    all_to_all x2, starting transfers between devices, exchange_sum(): received = lax.all_to_all(value, axes, 0, 0, tiled=True)  12.3 us
    all_to_all x2, starting transfers between devices, gather(): lax.all_to_all(jnp.broadcast_to(value[None], (count,) + value.shape), axe...  9.6 us
    dot_general x10, matrix products, blocked(): product = jnp.dot(rows[:, cut], weight[cut], preferred_element_type=F32)  6.51 us
  transfers between devices with their start and end apart: 10, of which 8 were waited for; matrix products, arithmetic and copies ran while one was open for 2% of the time, Pallas kernels for 0%

profile of v1, /device:TPU:1, one launch (start us, length us, event | category | flops | bytes accessed | tf_op | source)
XLA Modules:
  0.0 165.1 jit_solution(12461560433462234007)
XLA Ops:
  0.0 8.9 %collective-permute-start = (bf16[64,384]{1,0:T(8,128)(2,1)}, bf16[64,384]{1,0:T(8,128)(2,1)S(1)}, u32[]{:S(2)}, u32[]{:S(2)}) collective-permute-start(bf16[64,384]{1,0:T(8,128)(2,1)} %param.9), channel_id=1, source_target_pairs={{0,32},{32,0},{1,33},{33,1},{2,34},{34,2},{3,35},{35,3},{4,36},{36... | collective-permute-start | bytes 147464 | tf_op jit(solution)/shard_map/ppermute | solution.py:31
  8.9 0.7 fusion.49
  10.0 0.8 broadcast_select_fusion.1
  11.0 22.0 %all_to_all.30 = bf16[4,20,768]{2,1,0:T(8,128)(2,1)S(1)} all-to-all(bf16[4,20,768]{2,1,0:T(8,128)(2,1)S(1)} %broadcast_in_dim.70), channel_id=1, replica_groups=mesh['y'=4,'xh'=2,'core'=2,'zh'=4,'zl'=4,'xl'=2] {'zh'}, dimensions={0} | all-to-all | bytes 245760 | tf_op jit(solution)/shard_map/all_to_all | solution.py:35
  33.0 1.0 broadcast_in_dim.72
  34.0 5.5 %all-to-all-start.1 = ((bf16[8,80,768]{2,1,0:T(8,128)(2,1)}), bf16[8,80,768]{2,1,0:T(8,128)(2,1)S(1)}, u32[]{:S(2)}, u32[]{:S(2)}) async-start(bf16[8,80,768]{2,1,0:T(8,128)(2,1)} %broadcast_in_dim.72), calls=%async_computation.1 | async-start | bytes 1966080 | tf_op jit(solution)/shard_map/all_to_all | solution.py:35
  39.6 5.1 %collective-permute-start.2 = (f32[3,8]{1,0:T(4,128)S(1)}, f32[3,8]{1,0:T(4,128)S(1)}, u32[]{:S(2)}, u32[]{:S(2)}) collective-permute-start(f32[3,8]{1,0:T(4,128)S(1)} %bitcast.84), channel_id=1, source_target_pairs={{0,32},{32,0},{1,33},{33,1},{2,34},{34,2},{3,35},{35,3},{4,36},{36... | collective-permute-start | bytes 296 | tf_op jit(solution)/shard_map/ppermute | solution.py:31
  45.0 1.9 %collective-permute-start.1 = (bf16[384,1024]{1,0:T(8,128)(2,1)S(1)}, bf16[384,1024]{1,0:T(8,128)(2,1)S(1)}, u32[]{:S(2)}, u32[]{:S(2)}) collective-permute-start(bf16[384,1024]{1,0:T(8,128)(2,1)S(1)} %dynamic-slice_bitcast_fusion), channel_id=1, source_target_pairs={{0,32},{32,0},{1,33},{33,1},{2,34},{34,2},{3,35},{35,3},{4,36},{36... | collective-permute-start | bytes 2359304 | tf_op jit(solution)/shard_map/ppermute | solution.py:31
  47.4 1.8 %collective-permute-done.1 = bf16[384,1024]{1,0:T(8,128)(2,1)S(1)} collective-permute-done((bf16[384,1024]{1,0:T(8,128)(2,1)S(1)}, bf16[384,1024]{1,0:T(8,128)(2,1)S(1)}, u32[]{:S(2)}, u32[]{:S(2)}) %collective-permute-start.1) | collective-permute-done | bytes 786464 | tf_op jit(solution)/shard_map/ppermute | solution.py:31
  49.3 12.8 %all-to-all-done.1 = bf16[8,80,768]{2,1,0:T(8,128)(2,1)S(1)} async-done(((bf16[8,80,768]{2,1,0:T(8,128)(2,1)}), bf16[8,80,768]{2,1,0:T(8,128)(2,1)S(1)}, u32[]{:S(2)}, u32[]{:S(2)}) %all-to-all-start.1) | async-done | bytes 983072 | tf_op jit(solution)/shard_map/all_to_all | solution.py:35
  62.1 0.5 fusion.10
  62.6 0.5 fusion.6
  63.1 0.5 fusion.8
  63.5 0.5 fusion.4
  64.0 0.5 fusion.2
  64.5 2.2 %add_convert_fusion = bf16[640,1024]{1,0:T(8,128)(2,1)} fusion(f32[640,1024]{1,0:T(8,128)S(1)} %fusion.2, f32[640,1024]{1,0:T(8,128)S(1)} %fusion.4, f32[640,1024]{1,0:T(8,128)S(1)} %fusion.6, f32[640,1024]{1,0:T(8,128)S(1)} %fusion.8, f32[640,1024]{1,0:T(8,128)S(1)} %fusion.10, f32[1024]{0:T(1024)S(1)} %broadcast_bitcast_fusion.4, ...), kind=kOutput, calls=%fused_computation.1 | convolution fusion | flops 175636480 | bytes 14868480 | tf_op jit(solution)/shard_map/dot_general | solution.py:49
  66.8 6.5 %all-to-all-start.2 = ((bf16[8,80,1024]{2,1,0:T(8,128)(2,1)}), bf16[8,80,1024]{2,1,0:T(8,128)(2,1)S(1)}, u32[]{:S(2)}, u32[]{:S(2)}) async-start(bf16[8,80,1024]{2,1,0:T(8,128)(2,1)} %bitcast.17), calls=%async_computation.2 | async-start | bytes 2621440 | tf_op jit(solution)/shard_map/all_to_all | solution.py:41
  73.3 5.2 %collective-permute-start.3 = (bf16[512,384]{1,0:T(8,128)(2,1)S(1)}, bf16[512,384]{1,0:T(8,128)(2,1)S(1)}, u32[]{:S(2)}, u32[]{:S(2)}) collective-permute-start(bf16[512,384]{1,0:T(8,128)(2,1)S(1)} %dynamic-slice_bitcast_fusion.1), channel_id=1, source_target_pairs={{0,32},{32,0},{1,33},{33,1},{2,34},{34,2},{3,35},{35,3},{4,36},{36... | collective-permute-start | bytes 1179656 | tf_op jit(solution)/shard_map/ppermute | solution.py:31
  78.6 1.9 %collective-permute-start.4 = (f32[4,3]{1,0:T(4,128)S(1)}, f32[4,3]{1,0:T(4,128)S(1)}, u32[]{:S(2)}, u32[]{:S(2)}) collective-permute-start(f32[4,3]{1,0:T(4,128)S(1)} %bitcast.85), channel_id=1, source_target_pairs={{0,32},{32,0},{1,33},{33,1},{2,34},{34,2},{3,35},{35,3},{4,36},{36... | collective-permute-start | bytes 152 | tf_op jit(solution)/shard_map/ppermute | solution.py:31
  80.6 1.0 collective-permute-done.4
  81.7 8.3 %all-to-all-done.2 = bf16[8,80,1024]{2,1,0:T(8,128)(2,1)S(1)} async-done(((bf16[8,80,1024]{2,1,0:T(8,128)(2,1)}), bf16[8,80,1024]{2,1,0:T(8,128)(2,1)S(1)}, u32[]{:S(2)}, u32[]{:S(2)}) %all-to-all-start.2) | async-done | bytes 1310752 | tf_op jit(solution)/shard_map/all_to_all | solution.py:41
  90.3 0.9 broadcast_in_dim.79
  91.2 4.1 %all-to-all-start.3 = ((bf16[8,80,512]{2,1,0:T(8,128)(2,1)}), bf16[8,80,512]{2,1,0:T(8,128)(2,1)S(1)}, u32[]{:S(2)}, u32[]{:S(2)}) async-start(bf16[8,80,512]{2,1,0:T(8,128)(2,1)} %broadcast_in_dim.79), calls=%async_computation.3 | async-start | bytes 1310720 | tf_op jit(solution)/shard_map/all_to_all | solution.py:35
  95.5 9.7 %all-to-all-done.3 = bf16[8,80,512]{2,1,0:T(8,128)(2,1)S(1)} async-done(((bf16[8,80,512]{2,1,0:T(8,128)(2,1)}), bf16[8,80,512]{2,1,0:T(8,128)(2,1)S(1)}, u32[]{:S(2)}, u32[]{:S(2)}) %all-to-all-start.3) | async-done | bytes 655392 | tf_op jit(solution)/shard_map/all_to_all | solution.py:35
  106.4 0.7 add_convert_fusion.1
  107.1 29.8 %all_to_all.31 = bf16[8,80,768]{2,1,0:T(8,128)(2,1)S(1)} all-to-all(bf16[8,80,768]{2,1,0:T(8,128)(2,1)S(1)} %bitcast.79), channel_id=1, replica_groups=mesh['y'=4,'xh'=2,'core'=2,'zh'=4,'zl'=4,'xl'=2] {'zl','xl'}, dimensions={0} | all-to-all | bytes 1966080 | tf_op jit(solution)/shard_map/all_to_all | solution.py:41
  137.0 0.7 reshape.45
  137.7 5.8 %all-to-all-start.5 = ((bf16[4,20,768]{2,1,0:T(8,128)(2,1)}), bf16[4,20,768]{2,1,0:T(8,128)(2,1)S(1)}, u32[]{:S(2)}, u32[]{:S(2)}) async-start(bf16[4,20,768]{2,1,0:T(8,128)(2,1)} %reshape.45), calls=%async_computation.5 | async-start | bytes 294912 | tf_op jit(solution)/shard_map/all_to_all | solution.py:41
  143.5 12.6 %all-to-all-done.5 = bf16[4,20,768]{2,1,0:T(8,128)(2,1)S(1)} async-done(((bf16[4,20,768]{2,1,0:T(8,128)(2,1)}), bf16[4,20,768]{2,1,0:T(8,128)(2,1)S(1)}, u32[]{:S(2)}, u32[]{:S(2)}) %all-to-all-start.5) | async-done | bytes 122912 | tf_op jit(solution)/shard_map/all_to_all | solution.py:41
  156.1 6.9 %collective-permute-start.5 = (f32[20,384]{1,0:T(8,128)S(1)}, f32[20,384]{1,0:T(8,128)S(1)}, u32[]{:S(2)}, u32[]{:S(2)}) collective-permute-start(f32[20,384]{1,0:T(8,128)S(1)} %constant_dynamic-slice_fusion.2), channel_id=1, source_target_pairs={{0,32},{32,0},{1,33},{33,1},{2,34},{34,2},{3,35},{35,3},{4,36},{36... | collective-permute-start | bytes 92168 | tf_op jit(solution)/shard_map/ppermute | solution.py:31
  163.0 0.8 collective-permute-done.5
  164.2 0.9 fusion
  (63 shorter events, 3.9 us)
Async XLA Ops:
  0.0 39.5 %copy-start.5 = (f32[2,3,4]{2,0,1:T(2,128)S(1)}, f32[2,3,4]{2,0,1:T(2,128)}, u32[]{:S(2)}) copy-start(f32[2,3,4]{2,0,1:T(2,128)} %param.14) | copy-start | bytes 292
  0.0 39.5 %copy-start.4 = (f32[2,3,4]{2,0,1:T(2,128)S(1)}, f32[2,3,4]{2,0,1:T(2,128)}, u32[]{:S(2)}) copy-start(f32[2,3,4]{2,0,1:T(2,128)} %param.15) | copy-start | bytes 292
  0.0 44.7 %copy-start = (bf16[2,384,512]{2,1,0:T(8,128)(2,1)S(1)}, bf16[2,384,512]{2,1,0:T(8,128)(2,1)}, u32[]{:S(2)}) copy-start(bf16[2,384,512]{2,1,0:T(8,128)(2,1)} %param.12) | copy-start | bytes 2359300
  0.0 10.0 %collective-permute-start = (bf16[64,384]{1,0:T(8,128)(2,1)}, bf16[64,384]{1,0:T(8,128)(2,1)S(1)}, u32[]{:S(2)}, u32[]{:S(2)}) collective-permute-start(bf16[64,384]{1,0:T(8,128)(2,1)} %param.9), channel_id=1, source_target_pairs={{0,32},{32,0},{1,33},{33,1},{2,34},{34,2},{3,35},{35,3},{4,36},{36... | collective-permute-start | bytes 147464 | tf_op jit(solution)/shard_map/ppermute | solution.py:31
  11.0 33.8 %copy-start.1 = (bf16[2,384,512]{2,1,0:T(8,128)(2,1)S(1)}, bf16[2,384,512]{2,1,0:T(8,128)(2,1)}, u32[]{:S(2)}) copy-start(bf16[2,384,512]{2,1,0:T(8,128)(2,1)} %param.13) | copy-start | bytes 2359300
  34.0 28.1 %all-to-all-start.1 = ((bf16[8,80,768]{2,1,0:T(8,128)(2,1)}), bf16[8,80,768]{2,1,0:T(8,128)(2,1)S(1)}, u32[]{:S(2)}, u32[]{:S(2)}) async-start(bf16[8,80,768]{2,1,0:T(8,128)(2,1)} %broadcast_in_dim.72), calls=%async_computation.1 | async-start | bytes 1966080 | tf_op jit(solution)/shard_map/all_to_all | solution.py:35
  39.6 7.3 %collective-permute-start.2 = (f32[3,8]{1,0:T(4,128)S(1)}, f32[3,8]{1,0:T(4,128)S(1)}, u32[]{:S(2)}, u32[]{:S(2)}) collective-permute-start(f32[3,8]{1,0:T(4,128)S(1)} %bitcast.84), channel_id=1, source_target_pairs={{0,32},{32,0},{1,33},{33,1},{2,34},{34,2},{3,35},{35,3},{4,36},{36... | collective-permute-start | bytes 296 | tf_op jit(solution)/shard_map/ppermute | solution.py:31
  45.0 4.2 %collective-permute-start.1 = (bf16[384,1024]{1,0:T(8,128)(2,1)S(1)}, bf16[384,1024]{1,0:T(8,128)(2,1)S(1)}, u32[]{:S(2)}, u32[]{:S(2)}) collective-permute-start(bf16[384,1024]{1,0:T(8,128)(2,1)S(1)} %dynamic-slice_bitcast_fusion), channel_id=1, source_target_pairs={{0,32},{32,0},{1,33},{33,1},{2,34},{34,2},{3,35},{35,3},{4,36},{36... | collective-permute-start | bytes 2359304 | tf_op jit(solution)/shard_map/ppermute | solution.py:31
  66.8 6.5 %copy-start.2 = (bf16[2,512,384]{2,1,0:T(8,128)(2,1)S(1)}, bf16[2,512,384]{2,1,0:T(8,128)(2,1)}, u32[]{:S(2)}) copy-start(bf16[2,512,384]{2,1,0:T(8,128)(2,1)} %param.16) | copy-start | bytes 2359300
  66.8 11.7 %copy-start.3 = (f32[2,4,3]{1,0,2:T(2,128)S(1)}, f32[2,4,3]{1,0,2:T(2,128)}, u32[]{:S(2)}) copy-start(f32[2,4,3]{1,0,2:T(2,128)} %param.17) | copy-start | bytes 292
  66.8 23.3 %all-to-all-start.2 = ((bf16[8,80,1024]{2,1,0:T(8,128)(2,1)}), bf16[8,80,1024]{2,1,0:T(8,128)(2,1)S(1)}, u32[]{:S(2)}, u32[]{:S(2)}) async-start(bf16[8,80,1024]{2,1,0:T(8,128)(2,1)} %bitcast.17), calls=%async_computation.2 | async-start | bytes 2621440 | tf_op jit(solution)/shard_map/all_to_all | solution.py:41
  73.3 22.1 %collective-permute-start.3 = (bf16[512,384]{1,0:T(8,128)(2,1)S(1)}, bf16[512,384]{1,0:T(8,128)(2,1)S(1)}, u32[]{:S(2)}, u32[]{:S(2)}) collective-permute-start(bf16[512,384]{1,0:T(8,128)(2,1)S(1)} %dynamic-slice_bitcast_fusion.1), channel_id=1, source_target_pairs={{0,32},{32,0},{1,33},{33,1},{2,34},{34,2},{3,35},{35,3},{4,36},{36... | collective-permute-start | bytes 1179656 | tf_op jit(solution)/shard_map/ppermute | solution.py:31
  78.6 3.0 %collective-permute-start.4 = (f32[4,3]{1,0:T(4,128)S(1)}, f32[4,3]{1,0:T(4,128)S(1)}, u32[]{:S(2)}, u32[]{:S(2)}) collective-permute-start(f32[4,3]{1,0:T(4,128)S(1)} %bitcast.85), channel_id=1, source_target_pairs={{0,32},{32,0},{1,33},{33,1},{2,34},{34,2},{3,35},{35,3},{4,36},{36... | collective-permute-start | bytes 152 | tf_op jit(solution)/shard_map/ppermute | solution.py:31
  91.2 14.0 %all-to-all-start.3 = ((bf16[8,80,512]{2,1,0:T(8,128)(2,1)}), bf16[8,80,512]{2,1,0:T(8,128)(2,1)S(1)}, u32[]{:S(2)}, u32[]{:S(2)}) async-start(bf16[8,80,512]{2,1,0:T(8,128)(2,1)} %broadcast_in_dim.79), calls=%async_computation.3 | async-start | bytes 1310720 | tf_op jit(solution)/shard_map/all_to_all | solution.py:35
  107.0 36.5 %copy-start.6 = (s32[64,2]{0,1:T(2,128)S(1)}, s32[64,2]{0,1:T(2,128)}, u32[]{:S(2)}) copy-start(s32[64,2]{0,1:T(2,128)} %param.10) | copy-start | bytes 1540
  107.0 36.5 %copy-start.7 = (f32[64,2]{0,1:T(2,128)S(1)}, f32[64,2]{0,1:T(2,128)}, u32[]{:S(2)}) copy-start(f32[64,2]{0,1:T(2,128)} %param.11) | copy-start | bytes 1540
  137.7 18.4 %all-to-all-start.5 = ((bf16[4,20,768]{2,1,0:T(8,128)(2,1)}), bf16[4,20,768]{2,1,0:T(8,128)(2,1)S(1)}, u32[]{:S(2)}, u32[]{:S(2)}) async-start(bf16[4,20,768]{2,1,0:T(8,128)(2,1)} %reshape.45), calls=%async_computation.5 | async-start | bytes 294912 | tf_op jit(solution)/shard_map/all_to_all | solution.py:41
  156.1 7.8 %collective-permute-start.5 = (f32[20,384]{1,0:T(8,128)S(1)}, f32[20,384]{1,0:T(8,128)S(1)}, u32[]{:S(2)}, u32[]{:S(2)}) collective-permute-start(f32[20,384]{1,0:T(8,128)S(1)} %constant_dynamic-slice_fusion.2), channel_id=1, source_target_pairs={{0,32},{32,0},{1,33},{33,1},{2,34},{34,2},{3,35},{35,3},{4,36},{36... | collective-permute-start | bytes 92168 | tf_op jit(solution)/shard_map/ppermute | solution.py:31

commit v2 on v1

--- a/solution.py
+++ b/solution.py
@@ -8,9 +8,13 @@
 SB = 128
 COL = ("y", "xh", "core")
 BLK = ("zh", "zl", "xl")
-SIZES = {"y": 4, "xh": 2, "core": 2, "zh": 4, "zl": 4, "xl": 2}
+SIZES = {"y": 4, "xh": 2, "core": 2, "zh": 8, "zl": 2, "xl": 2}
+ZH = SIZES["zh"]
+NEAR = SIZES["zl"] * SIZES["xl"]
+GROUP = SIZES["y"] * SIZES["xh"]
 F32 = jnp.float32
 BF16 = jnp.bfloat16
+SHIFT = 64.0
 
 
 def dispatch(route_ids, route_gates):
@@ -31,15 +35,12 @@
     return lax.ppermute(value, "core", [(0, 1), (1, 0)])
 
 
-def gather(value, axes, count):
-    return lax.all_to_all(
-        jnp.broadcast_to(value[None], (count,) + value.shape), axes, 0, 0, tiled=True
-    )
+def trade(value, axes):
+    return lax.all_to_all(value, axes, 0, 0, tiled=True)
 
 
-def exchange_sum(value, axes):
-    received = lax.all_to_all(value, axes, 0, 0, tiled=True)
-    return jnp.sum(received.astype(F32), axis=0)
+def gather(value, axes, count):
+    return trade(jnp.broadcast_to(value[None], (count,) + value.shape), axes)
 
 
 def blocked(rows, weight, scale):
@@ -73,43 +74,36 @@
     core = lax.axis_index("core")
     width = tokens.shape[1]
     hidden_width = gate_weight.shape[2]
-    other_tokens = swap(tokens)
-    tokens2 = jnp.concatenate(
-        [
-            jnp.where(core == 0, tokens, other_tokens),
-            jnp.where(core == 0, other_tokens, tokens),
-        ],
-        axis=1,
-    )
+    near_rows = ZH * CAP
+    rows = NEAR * near_rows
     onehot, combine_weights = dispatch(route_ids, route_gates)
-    mine = lax.dynamic_index_in_dim(onehot, core, 1, keepdims=False)
     slot_rows = jnp.einsum(
-        "tc,td->cd", mine.astype(BF16), tokens2, preferred_element_type=F32
+        "tec,td->ecd", onehot.astype(BF16), tokens, preferred_element_type=F32
     ).astype(BF16)
-    portion = gather(slot_rows, "zh", 4).reshape(4 * CAP, 2 * width)
-    portion = gather(portion, ("zl", "xl"), 8).reshape(32 * CAP, 2 * width)
+    far = jnp.broadcast_to(slot_rows[None], (ZH, 2, CAP, width)).reshape(2 * ZH, CAP, width)
+    far = trade(far, ("zh", "core")).reshape(ZH, 2, CAP, width)
+    far = far.transpose(0, 2, 1, 3).reshape(near_rows, 2 * width)
+    portion = gather(far, ("zl", "xl"), NEAR).reshape(rows, 2 * width)
 
     gate_up_weight = both_cores(jnp.concatenate([gate_weight, up_weight], axis=2), core, 0)
     gate_up_scale = both_cores(jnp.concatenate([gate_scale, up_scale], axis=2), core, 0)
     down_both = both_cores(down_weight, core, 1)
     down_scale_both = both_cores(down_scale, core, 1)
 
-    partial_sums = blocked(portion, gate_up_weight, gate_up_scale).astype(BF16)
-    summed = exchange_sum(partial_sums.reshape(8, 4 * CAP, 2 * hidden_width), ("y", "xh"))
+    partial_sums = (blocked(portion, gate_up_weight, gate_up_scale) * SHIFT).astype(jnp.float16)
+    received = trade(partial_sums.reshape(GROUP, rows // GROUP, 2 * hidden_width), ("y", "xh"))
+    summed = jnp.sum(received.astype(F32), axis=0) * (1.0 / SHIFT)
     hidden = (jax.nn.silu(summed[:, :hidden_width]) * summed[:, hidden_width:]).astype(BF16)
-    hidden = gather(hidden, ("y", "xh"), 8).reshape(32 * CAP, hidden_width)
+    hidden = gather(hidden, ("y", "xh"), GROUP).reshape(rows, hidden_width)
     down = blocked(hidden, down_both, down_scale_both).astype(BF16)
-    down = exchange_sum(down.reshape(8, 4 * CAP, 2 * width), ("zl", "xl")).astype(BF16)
-    expert_out = exchange_sum(down.reshape(4, CAP, 2 * width), "zh")
+    down = trade(down.reshape(NEAR, near_rows, 2 * width), ("zl", "xl"))
+    down = jnp.sum(down.astype(F32), axis=0).astype(BF16)
+    down = down.reshape(ZH, CAP, 2, width).transpose(0, 2, 1, 3).reshape(2 * ZH, CAP, width)
+    down = trade(down, ("zh", "core")).reshape(ZH, 2, CAP, width)
+    expert_out = jnp.sum(down.astype(F32), axis=0)
 
-    kept = lax.dynamic_slice_in_dim(expert_out, core * width, width, 1)
-    given = swap(lax.dynamic_slice_in_dim(expert_out, (1 - core) * width, width, 1))
-    first = jnp.where(core == 0, kept, given)
-    second = jnp.where(core == 0, given, kept)
     combine = onehot.astype(F32) * combine_weights[:, :, None]
-    mixed = jnp.dot(combine[:, 0], first, precision=lax.Precision.HIGHEST) + jnp.dot(
-        combine[:, 1], second, precision=lax.Precision.HIGHEST
-    )
+    mixed = jnp.einsum("tec,ecd->td", combine, expert_out, precision=lax.Precision.HIGHEST)
     return mixed.astype(BF16)
 
 

time: 166 us -> 154 us (0.928)
  starting transfers between devices: 51.8 us -> 29.5 us
  waiting for transfers between devices: 47 us -> 53.3 us
    ppermute x6 -> x4, starting transfers between devices: 29.9 us -> 8.63 us  [swap(): return lax.ppermute(value, 'core', [(0, 1), (1, 0)])]
    all_to_all x4, waiting for transfers between devices: 43.3 us -> 51 us  [trade(): return lax.all_to_all(value, axes, 0, 0, tiled=True)]
    select_n x3, other arithmetic: 0.12 us -> 2.18 us  [both_cores(): first = jnp.where(core == 0, own, other)]
    ppermute x6 -> x4, waiting for transfers between devices: 3.72 us -> 2.27 us  [swap(): return lax.ppermute(value, 'core', [(0, 1), (1, 0)])]
  transfers between devices with their start and end apart: 10 -> 8, of which waited for: 8 -> 6; matrix products, arithmetic and copies ran while one was open for 2% -> 4% of each run, Pallas kernels for 0% -> 0%
where the time goes in v2:
time: 154 us; the launch traced here: 153 us
  waiting for transfers between devices  53.3 us (35%)
  blocking collectives  52.2 us (34%)
  starting transfers between devices  29.5 us (19%)
  matrix products  8.7 us (6%)
  local copies, waits for them, and re-layouts  5.42 us (4%)
  other arithmetic  3.81 us (2%)
    all_to_all x2, blocking collectives, trade(): return lax.all_to_all(value, axes, 0, 0, tiled=True)  52.2 us
    all_to_all x4, waiting for transfers between devices, trade(): return lax.all_to_all(value, axes, 0, 0, tiled=True)  51 us
    all_to_all x4, starting transfers between devices, trade(): return lax.all_to_all(value, axes, 0, 0, tiled=True)  20.9 us
    ppermute x4, starting transfers between devices, swap(): return lax.ppermute(value, 'core', [(0, 1), (1, 0)])  8.63 us
    dot_general x10, matrix products, blocked(): product = jnp.dot(rows[:, cut], weight[cut], preferred_element_type=F32)  7.63 us
  transfers between devices with their start and end apart: 8, of which 6 were waited for; matrix products, arithmetic and copies ran while one was open for 4% of the time, Pallas kernels for 0%

profile of v2, /device:TPU:1, one launch (start us, length us, event | category | flops | bytes accessed | tf_op | source)
XLA Modules:
  0.0 153.3 jit_solution(3074306009449103008)
XLA Ops:
  0.0 0.7 fusion.44
  1.2 38.4 %all_to_all.30 = bf16[16,20,384]{2,1,0:T(8,128)(2,1)S(1)} all-to-all(bf16[16,20,384]{2,1,0:T(8,128)(2,1)S(1)} %bitcast.95), channel_id=1, replica_groups=mesh['y'=4,'xh'=2,'core'=2,'zh'=8,'zl'=2,'xl'=2] {'zh','core'}, dimensions={0} | all-to-all | bytes 491520 | tf_op jit(solution)/shard_map/all_to_all | solution.py:39
  39.8 1.0 broadcast_in_dim.72
  40.8 3.5 %all-to-all-start.1 = ((bf16[4,160,768]{2,1,0:T(8,128)(2,1)}), bf16[4,160,768]{2,1,0:T(8,128)(2,1)S(1)}, u32[]{:S(2)}, u32[]{:S(2)}) async-start(bf16[4,160,768]{2,1,0:T(8,128)(2,1)} %broadcast_in_dim.72), calls=%async_computation.1 | async-start | bytes 1966080 | tf_op jit(solution)/shard_map/all_to_all | solution.py:39
  44.5 1.9 %collective-permute-start.1 = (f32[3,8]{1,0:T(4,128)S(1)}, f32[3,8]{1,0:T(4,128)S(1)}, u32[]{:S(2)}, u32[]{:S(2)}) collective-permute-start(f32[3,8]{1,0:T(4,128)S(1)} %bitcast.100), channel_id=1, source_target_pairs={{0,32},{32,0},{1,33},{33,1},{2,34},{34,2},{3,35},{35,3},{4,36},{36... | collective-permute-start | bytes 296 | tf_op jit(solution)/shard_map/ppermute | solution.py:35
  46.5 1.2 constant_dynamic-update-slice_fusion
  47.8 2.4 %collective-permute-start = (bf16[384,1024]{1,0:T(8,128)(2,1)S(1)}, bf16[384,1024]{1,0:T(8,128)(2,1)}, u32[]{:S(2)}, u32[]{:S(2)}) collective-permute-start(bf16[384,1024]{1,0:T(8,128)(2,1)S(1)} %dynamic-slice_bitcast_fusion), channel_id=1, source_target_pairs={{0,32},{32,0},{1,33},{33,1},{2,34},{34,2},{3,35},{35,3},{4,36},{36... | collective-permute-start | bytes 2359304 | tf_op jit(solution)/shard_map/ppermute | solution.py:35
  50.7 1.6 %collective-permute-done = bf16[384,1024]{1,0:T(8,128)(2,1)} collective-permute-done((bf16[384,1024]{1,0:T(8,128)(2,1)S(1)}, bf16[384,1024]{1,0:T(8,128)(2,1)}, u32[]{:S(2)}, u32[]{:S(2)}) %collective-permute-start) | collective-permute-done | bytes 786464 | tf_op jit(solution)/shard_map/ppermute | solution.py:35
  52.3 2.2 %bitcast_select_fusion.1 = (bf16[384,1024]{1,0:T(8,128)(2,1)}, bf16[384,1024]{1,0:T(8,128)(2,1)S(1)}) fusion(bf16[384,1024]{1,0:T(8,128)(2,1)} %collective-permute-done, pred[]{:T(512)S(6)} %eq.20, bf16[2,384,1024]{2,1,0:T(8,128)(2,1)S(1)} %constant_dynamic-update-slice_fusion, s32[]{:T(128)S(6)} %select_n.70), kind=kLoop, calls=%fused_computation.13 | loop fusion | flops 786432 | bytes 3145733 | tf_op jit(solution)/shard_map/jit(_where)/select_n | solution.py:58
  54.4 2.2 %all-to-all-done.1 = bf16[4,160,768]{2,1,0:T(8,128)(2,1)S(1)} async-done(((bf16[4,160,768]{2,1,0:T(8,128)(2,1)}), bf16[4,160,768]{2,1,0:T(8,128)(2,1)S(1)}, u32[]{:S(2)}, u32[]{:S(2)}) %all-to-all-start.1) | async-done | bytes 983072 | tf_op jit(solution)/shard_map/all_to_all | solution.py:39
  56.6 1.4 fusion.10
  58.1 0.5 fusion.6
  58.6 0.5 fusion.8
  59.1 0.5 fusion.4
  59.5 0.5 fusion.2
  60.0 2.4 %multiply_convert_fusion = f16[640,1024]{1,0:T(8,128)(2,1)} fusion(f32[640,1024]{1,0:T(8,128)S(1)} %fusion.2, f32[640,1024]{1,0:T(8,128)S(1)} %fusion.4, f32[640,1024]{1,0:T(8,128)S(1)} %fusion.6, f32[640,1024]{1,0:T(8,128)S(1)} %fusion.8, f32[640,1024]{1,0:T(8,128)S(1)} %fusion.10, f32[1024]{0:T(1024)S(1)} %broadcast_bitcast_fusion.4, ...), kind=kOutput, calls=%fused_computation.1 | convolution fusion | flops 176291840 | bytes 14868480 | tf_op jit(solution)/shard_map/dot_general | solution.py:50
  62.4 6.8 %all-to-all-start.2 = ((f16[8,80,1024]{2,1,0:T(8,128)(2,1)}), f16[8,80,1024]{2,1,0:T(8,128)(2,1)S(1)}, u32[]{:S(2)}, u32[]{:S(2)}) async-start(f16[8,80,1024]{2,1,0:T(8,128)(2,1)} %bitcast.20), calls=%async_computation.2 | async-start | bytes 2621440 | tf_op jit(solution)/shard_map/all_to_all | solution.py:39
  69.3 2.0 %collective-permute-start.2 = (bf16[512,384]{1,0:T(8,128)(2,1)S(1)}, bf16[512,384]{1,0:T(8,128)(2,1)S(1)}, u32[]{:S(2)}, u32[]{:S(2)}) collective-permute-start(bf16[512,384]{1,0:T(8,128)(2,1)S(1)} %dynamic-slice_bitcast_fusion.1), channel_id=1, source_target_pairs={{0,32},{32,0},{1,33},{33,1},{2,34},{34,2},{3,35},{35,3},{4,36},{36... | collective-permute-start | bytes 1179656 | tf_op jit(solution)/shard_map/ppermute | solution.py:35
  71.4 2.3 %collective-permute-start.3 = (f32[4,3]{1,0:T(4,128)S(1)}, f32[4,3]{1,0:T(4,128)S(1)}, u32[]{:S(2)}, u32[]{:S(2)}) collective-permute-start(f32[4,3]{1,0:T(4,128)S(1)} %bitcast.101), channel_id=1, source_target_pairs={{0,32},{32,0},{1,33},{33,1},{2,34},{34,2},{3,35},{35,3},{4,36},{36... | collective-permute-start | bytes 152 | tf_op jit(solution)/shard_map/ppermute | solution.py:35
  73.8 0.7 collective-permute-done.3
  74.6 14.7 %all-to-all-done.2 = f16[8,80,1024]{2,1,0:T(8,128)(2,1)S(1)} async-done(((f16[8,80,1024]{2,1,0:T(8,128)(2,1)}), f16[8,80,1024]{2,1,0:T(8,128)(2,1)S(1)}, u32[]{:S(2)}, u32[]{:S(2)}) %all-to-all-start.2) | async-done | bytes 1310752 | tf_op jit(solution)/shard_map/all_to_all | solution.py:39
  89.7 0.9 broadcast_in_dim.79
  90.6 3.5 %all-to-all-start.3 = ((bf16[8,80,512]{2,1,0:T(8,128)(2,1)}), bf16[8,80,512]{2,1,0:T(8,128)(2,1)S(1)}, u32[]{:S(2)}, u32[]{:S(2)}) async-start(bf16[8,80,512]{2,1,0:T(8,128)(2,1)} %broadcast_in_dim.79), calls=%async_computation.3 | async-start | bytes 1310720 | tf_op jit(solution)/shard_map/all_to_all | solution.py:39
  94.4 11.5 %all-to-all-done.3 = bf16[8,80,512]{2,1,0:T(8,128)(2,1)S(1)} async-done(((bf16[8,80,512]{2,1,0:T(8,128)(2,1)}), bf16[8,80,512]{2,1,0:T(8,128)(2,1)S(1)}, u32[]{:S(2)}, u32[]{:S(2)}) %all-to-all-start.3) | async-done | bytes 655392 | tf_op jit(solution)/shard_map/all_to_all | solution.py:39
  106.0 0.4 fusion.16
  106.4 0.4 fusion.19
  107.2 0.7 add_convert_fusion
  107.9 13.8 %all_to_all.31 = bf16[4,160,768]{2,1,0:T(8,128)(2,1)S(1)} all-to-all(bf16[4,160,768]{2,1,0:T(8,128)(2,1)S(1)} %bitcast.89), channel_id=1, replica_groups=mesh['y'=4,'xh'=2,'core'=2,'zh'=8,'zl'=2,'xl'=2] {'zl','xl'}, dimensions={0} | all-to-all | bytes 1966080 | tf_op jit(solution)/shard_map/all_to_all | solution.py:39
  121.8 0.8 copy.55
  122.6 7.1 %all-to-all-start.5 = ((bf16[16,20,384]{2,1,0:T(8,128)(2,1)}), bf16[16,20,384]{2,1,0:T(8,128)(2,1)S(1)}, u32[]{:S(2)}, u32[]{:S(2)}) async-start(bf16[16,20,384]{2,1,0:T(8,128)(2,1)} %bitcast.36), calls=%async_computation.5 | async-start | bytes 589824 | tf_op jit(solution)/shard_map/all_to_all | solution.py:39
  129.7 22.6 %all-to-all-done.5 = bf16[16,20,384]{2,1,0:T(8,128)(2,1)S(1)} async-done(((bf16[16,20,384]{2,1,0:T(8,128)(2,1)}), bf16[16,20,384]{2,1,0:T(8,128)(2,1)S(1)}, u32[]{:S(2)}, u32[]{:S(2)}) %all-to-all-start.5) | async-done | bytes 245792 | tf_op jit(solution)/shard_map/all_to_all | solution.py:39
  152.3 0.9 fusion
  (59 shorter events, 3.0 us)
Async XLA Ops:
  0.0 1.0 copy-start
  1.0 43.4 %copy-start.5 = (f32[2,3,4]{2,0,1:T(2,128)S(1)}, f32[2,3,4]{2,0,1:T(2,128)}, u32[]{:S(2)}) copy-start(f32[2,3,4]{2,0,1:T(2,128)} %param.15) | copy-start | bytes 292
  1.0 43.4 %copy-start.6 = (f32[2,3,4]{2,0,1:T(2,128)S(1)}, f32[2,3,4]{2,0,1:T(2,128)}, u32[]{:S(2)}) copy-start(f32[2,3,4]{2,0,1:T(2,128)} %param.14) | copy-start | bytes 292
  1.0 45.4 %copy-start.2 = (bf16[2,384,512]{2,1,0:T(8,128)(2,1)S(1)}, bf16[2,384,512]{2,1,0:T(8,128)(2,1)}, u32[]{:S(2)}) copy-start(bf16[2,384,512]{2,1,0:T(8,128)(2,1)} %param.12) | copy-start | bytes 2359300
  40.8 15.8 %all-to-all-start.1 = ((bf16[4,160,768]{2,1,0:T(8,128)(2,1)}), bf16[4,160,768]{2,1,0:T(8,128)(2,1)S(1)}, u32[]{:S(2)}, u32[]{:S(2)}) async-start(bf16[4,160,768]{2,1,0:T(8,128)(2,1)} %broadcast_in_dim.72), calls=%async_computation.1 | async-start | bytes 1966080 | tf_op jit(solution)/shard_map/all_to_all | solution.py:39
  44.5 5.8 %collective-permute-start.1 = (f32[3,8]{1,0:T(4,128)S(1)}, f32[3,8]{1,0:T(4,128)S(1)}, u32[]{:S(2)}, u32[]{:S(2)}) collective-permute-start(f32[3,8]{1,0:T(4,128)S(1)} %bitcast.100), channel_id=1, source_target_pairs={{0,32},{32,0},{1,33},{33,1},{2,34},{34,2},{3,35},{35,3},{4,36},{36... | collective-permute-start | bytes 296 | tf_op jit(solution)/shard_map/ppermute | solution.py:35
  47.8 4.4 %collective-permute-start = (bf16[384,1024]{1,0:T(8,128)(2,1)S(1)}, bf16[384,1024]{1,0:T(8,128)(2,1)}, u32[]{:S(2)}, u32[]{:S(2)}) collective-permute-start(bf16[384,1024]{1,0:T(8,128)(2,1)S(1)} %dynamic-slice_bitcast_fusion), channel_id=1, source_target_pairs={{0,32},{32,0},{1,33},{33,1},{2,34},{34,2},{3,35},{35,3},{4,36},{36... | collective-permute-start | bytes 2359304 | tf_op jit(solution)/shard_map/ppermute | solution.py:35
  54.4 3.6 %copy-start.1 = (bf16[384,1024]{1,0:T(8,128)(2,1)S(1)}, bf16[384,1024]{1,0:T(8,128)(2,1)}, u32[]{:S(2)}) copy-start(bf16[384,1024]{1,0:T(8,128)(2,1)} %get-tuple-element.5) | copy-start | bytes 2359300
  62.4 6.8 %copy-start.3 = (bf16[2,512,384]{2,1,0:T(8,128)(2,1)S(1)}, bf16[2,512,384]{2,1,0:T(8,128)(2,1)}, u32[]{:S(2)}) copy-start(bf16[2,512,384]{2,1,0:T(8,128)(2,1)} %param.16) | copy-start | bytes 2359300
  62.4 8.8 %copy-start.4 = (f32[2,4,3]{1,0,2:T(2,128)S(1)}, f32[2,4,3]{1,0,2:T(2,128)}, u32[]{:S(2)}) copy-start(f32[2,4,3]{1,0,2:T(2,128)} %param.17) | copy-start | bytes 292
  62.4 26.9 %all-to-all-start.2 = ((f16[8,80,1024]{2,1,0:T(8,128)(2,1)}), f16[8,80,1024]{2,1,0:T(8,128)(2,1)S(1)}, u32[]{:S(2)}, u32[]{:S(2)}) async-start(f16[8,80,1024]{2,1,0:T(8,128)(2,1)} %bitcast.20), calls=%async_computation.2 | async-start | bytes 2621440 | tf_op jit(solution)/shard_map/all_to_all | solution.py:39
  69.3 25.0 %collective-permute-start.2 = (bf16[512,384]{1,0:T(8,128)(2,1)S(1)}, bf16[512,384]{1,0:T(8,128)(2,1)S(1)}, u32[]{:S(2)}, u32[]{:S(2)}) collective-permute-start(bf16[512,384]{1,0:T(8,128)(2,1)S(1)} %dynamic-slice_bitcast_fusion.1), channel_id=1, source_target_pairs={{0,32},{32,0},{1,33},{33,1},{2,34},{34,2},{3,35},{35,3},{4,36},{36... | collective-permute-start | bytes 1179656 | tf_op jit(solution)/shard_map/ppermute | solution.py:35
  71.4 3.1 %collective-permute-start.3 = (f32[4,3]{1,0:T(4,128)S(1)}, f32[4,3]{1,0:T(4,128)S(1)}, u32[]{:S(2)}, u32[]{:S(2)}) collective-permute-start(f32[4,3]{1,0:T(4,128)S(1)} %bitcast.101), channel_id=1, source_target_pairs={{0,32},{32,0},{1,33},{33,1},{2,34},{34,2},{3,35},{35,3},{4,36},{36... | collective-permute-start | bytes 152 | tf_op jit(solution)/shard_map/ppermute | solution.py:35
  90.6 15.3 %all-to-all-start.3 = ((bf16[8,80,512]{2,1,0:T(8,128)(2,1)}), bf16[8,80,512]{2,1,0:T(8,128)(2,1)S(1)}, u32[]{:S(2)}, u32[]{:S(2)}) async-start(bf16[8,80,512]{2,1,0:T(8,128)(2,1)} %broadcast_in_dim.79), calls=%async_computation.3 | async-start | bytes 1310720 | tf_op jit(solution)/shard_map/all_to_all | solution.py:39
  107.8 21.8 %copy-start.7 = (s32[64,2]{0,1:T(2,128)S(1)}, s32[64,2]{0,1:T(2,128)}, u32[]{:S(2)}) copy-start(s32[64,2]{0,1:T(2,128)} %param.10) | copy-start | bytes 1540
  107.8 21.8 %copy-start.8 = (f32[64,2]{0,1:T(2,128)S(1)}, f32[64,2]{0,1:T(2,128)}, u32[]{:S(2)}) copy-start(f32[64,2]{0,1:T(2,128)} %param.11) | copy-start | bytes 1540
  122.6 29.7 %all-to-all-start.5 = ((bf16[16,20,384]{2,1,0:T(8,128)(2,1)}), bf16[16,20,384]{2,1,0:T(8,128)(2,1)S(1)}, u32[]{:S(2)}, u32[]{:S(2)}) async-start(bf16[16,20,384]{2,1,0:T(8,128)(2,1)} %bitcast.36), calls=%async_computation.5 | async-start | bytes 589824 | tf_op jit(solution)/shard_map/all_to_all | solution.py:39

commit v3 on v2

v3 whole, which is shorter than its diff:
```python
import jax
import jax.numpy as jnp
from jax import lax
from jax.experimental import pallas as pl
from jax.experimental.pallas import tpu as pltpu
from jax.sharding import Mesh, PartitionSpec as P

EXPW = 2
CAP = 20
SB = 128
COL = ("y", "xh", "core")
BLK = ("zh", "zl", "xl")
SIZES = {"y": 4, "xh": 2, "core": 2, "zh": 8, "zl": 2, "xl": 2}
ZH = SIZES["zh"]
NEAR = SIZES["zl"] * SIZES["xl"]
GROUP = SIZES["y"] * SIZES["xh"]
F32 = jnp.float32
BF16 = jnp.bfloat16
SHIFT = 64.0


def dispatch(route_ids, route_gates):
    expert_ids = jnp.arange(EXPW, dtype=jnp.int32)
    matches = route_ids[:, :, None] == expert_ids[None, None, :]
    chosen = jnp.any(matches, axis=1)
    combine_weights = jnp.sum(
        jnp.where(matches, route_gates[:, :, None], jnp.zeros((), route_gates.dtype)), axis=1
    )
    slot_index = jnp.cumsum(chosen.astype(jnp.int32), axis=0) - 1
    onehot = chosen[:, :, None] & (
        slot_index[:, :, None] == jnp.arange(CAP, dtype=jnp.int32)[None, None, :]
    )
    return (onehot, combine_weights)


def swap(value):
    return lax.ppermute(value, "core", [(0, 1), (1, 0)])


def trade(value, axes):
    return lax.all_to_all(value, axes, 0, 0, tiled=True)


def gather(value, axes, count):
    return trade(jnp.broadcast_to(value[None], (count,) + value.shape), axes)


def pick(array, index):
    return lax.dynamic_index_in_dim(array, index, 0, keepdims=False)


def scale_row(read, blocks):
    return jnp.concatenate([jnp.full((1, SB), read(block), F32) for block in blocks], axis=1)


def gate_up_kernel(core_ref, gs_ref, us_ref, rs_ref, x_ref, gw_ref, uw_ref, rw_ref, o_ref):
    core = core_ref[0]
    depth, units = gw_ref.shape[1], gw_ref.shape[2]
    ks, ns = depth // SB, units // SB
    chunk = 2 * SB
    for which, (own_scale, own_weight) in enumerate(((gs_ref, gw_ref), (us_ref, uw_ref))):
        for n in range(units // chunk):
            columns = slice(n * chunk, (n + 1) * chunk)
            blocks = (2 * n, 2 * n + 1)
            total = None
            for other in (0, 1):
                base = (core if other == 0 else 1 - core) * depth
                for k in range(ks):
                    offset = pl.multiple_of(base + k * SB, SB)
                    rows = x_ref[0, :, pl.ds(offset, SB)]
                    if other == 0:
                        weight = own_weight[0, k * SB : (k + 1) * SB, columns]
                        row = scale_row(lambda c: own_scale[core, k, c] * SHIFT, blocks)
                    else:
                        first = which * depth + k * SB
                        weight = rw_ref[first : first + SB, columns]
                        place = (which * ks + k) * ns
                        row = scale_row(lambda c: rs_ref[0, place + c] * SHIFT, blocks)
                    product = jnp.dot(rows, weight, preferred_element_type=F32) * row
                    total = product if total is None else total + product
            left = which * units + n * chunk
            o_ref[:, :, left : left + chunk] = total.reshape(o_ref.shape[:2] + (chunk,))


def gate_up(core_index, portion, gate_weight, up_weight, other, gate_scale, up_scale, other_scale):
    near, near_rows, width2 = portion.shape
    _, depth, units = gate_weight.shape
    per = GROUP // near
    smem = pl.BlockSpec(memory_space=pltpu.SMEM)
    return pl.pallas_call(
        gate_up_kernel,
        grid_spec=pltpu.PrefetchScalarGridSpec(
            num_scalar_prefetch=1,
            grid=(near,),
            in_specs=[
                smem,
                smem,
                smem,
                pl.BlockSpec((1, near_rows, width2), lambda i, c: (i, 0, 0)),
                pl.BlockSpec((1, depth, units), lambda i, c: (c[0], 0, 0)),
                pl.BlockSpec((1, depth, units), lambda i, c: (c[0], 0, 0)),
                pl.BlockSpec((2 * depth, units), lambda i, c: (0, 0)),
            ],
            out_specs=pl.BlockSpec((per, near_rows // per, 2 * units), lambda i, c: (i, 0, 0)),
        ),
        out_shape=jax.ShapeDtypeStruct((GROUP, near_rows // per, 2 * units), F32),
        compiler_params=pltpu.CompilerParams(vmem_limit_bytes=24 * 1024 * 1024),
        cost_estimate=pl.CostEstimate(
            flops=2 * near * near_rows * width2 * 2 * units,
            bytes_accessed=near * near_rows * (2 * width2 + 8 * units) + 8 * depth * units,
            transcendentals=0,
        ),
        name="gate_up",
    )(core_index, gate_scale, up_scale, other_scale, portion, gate_weight, up_weight, other)


def down_kernel(core_ref, ds_ref, rs_ref, h_ref, dw_ref, rw_ref, o_ref):
    core = core_ref[0]
    depth, width = dw_ref.shape[1], dw_ref.shape[2]
    ks, ns = depth // SB, width // SB
    rows = h_ref.shape[0] * h_ref.shape[1]
    start = rs_ref.shape[1] - ks * ns
    for other in (0, 1):
        total = None
        for k in range(ks):
            cut = slice(k * SB, (k + 1) * SB)
            hidden = h_ref[:, :, cut].reshape(rows, SB)
            if other == 0:
                weight = dw_ref[0, cut, :]
                row = scale_row(lambda c: ds_ref[core, k, c], range(ns))
            else:
                weight = rw_ref[cut, :]
                row = scale_row(lambda c: rs_ref[0, start + k * ns + c], range(ns))
            product = jnp.dot(hidden, weight, preferred_element_type=F32) * row
            total = product if total is None else total + product
        base = pl.multiple_of((core if other == 0 else 1 - core) * width, SB)
        o_ref[0, :, pl.ds(base, width)] = total.astype(o_ref.dtype)


def down_project(core_index, hidden, down_weight, other, down_scale, other_scale):
    _, some_rows, depth = hidden.shape
    width = down_weight.shape[2]
    per = GROUP // NEAR
    smem = pl.BlockSpec(memory_space=pltpu.SMEM)
    return pl.pallas_call(
        down_kernel,
        grid_spec=pltpu.PrefetchScalarGridSpec(
            num_scalar_prefetch=1,
            grid=(NEAR,),
            in_specs=[
                smem,
                smem,
                pl.BlockSpec((per, some_rows, depth), lambda i, c: (i, 0, 0)),
                pl.BlockSpec((1, depth, width), lambda i, c: (c[0], 0, 0)),
                pl.BlockSpec((depth, width), lambda i, c: (0, 0)),
            ],
            out_specs=pl.BlockSpec((1, per * some_rows, 2 * width), lambda i, c: (i, 0, 0)),
        ),
        out_shape=jax.ShapeDtypeStruct((NEAR, per * some_rows, 2 * width), BF16),
        compiler_params=pltpu.CompilerParams(vmem_limit_bytes=24 * 1024 * 1024),
        cost_estimate=pl.CostEstimate(
            flops=4 * GROUP * some_rows * depth * width,
            bytes_accessed=GROUP * some_rows * (2 * depth + 4 * width) + 4 * depth * width,
            transcendentals=0,
        ),
        name="down_project",
    )(core_index, down_scale, other_scale, hidden, down_weight, other)


def shards(
    tokens,
    route_ids,
    route_gates,
    gate_weight,
    up_weight,
    gate_scale,
    up_scale,
    down_weight,
    down_scale,
):
    core = lax.axis_index("core")
    width = tokens.shape[1]
    hidden_width = gate_weight.shape[2]
    near_rows = ZH * CAP
    onehot, combine_weights = dispatch(route_ids, route_gates)
    slot_rows = jnp.einsum(
        "tec,td->ecd", onehot.astype(BF16), tokens, preferred_element_type=F32
    ).astype(BF16)
    packed = slot_rows.reshape(2, 4, CAP // 4 * width)
    far = jnp.broadcast_to(packed[None], (ZH,) + packed.shape).reshape(2 * ZH, 4, -1)
    far = trade(far, ("zh", "core")).reshape(ZH, 2, CAP, width)
    far = far.transpose(0, 2, 1, 3).reshape(near_rows, 2 * width)
    portion = gather(far, ("zl", "xl"), NEAR)

    other = 1 - core
    other_gate_up = swap(jnp.concatenate([pick(gate_weight, other), pick(up_weight, other)], axis=0))
    scales = [pick(scale, other).reshape(1, -1) for scale in (gate_scale, up_scale, down_scale)]
    other_scales = swap(jnp.concatenate(scales, axis=1))
    core_index = jnp.reshape(core, (1,)).astype(jnp.int32)

    partial_sums = gate_up(
        core_index,
        portion,
        gate_weight,
        up_weight,
        other_gate_up,
        gate_scale,
        up_scale,
        other_scales,
    ).astype(jnp.float16)
    received = trade(partial_sums, ("y", "xh"))
    summed = jnp.sum(received.astype(F32), axis=0) * (1.0 / SHIFT)
    hidden = (jax.nn.silu(summed[:, :hidden_width]) * summed[:, hidden_width:]).astype(BF16)
    hidden, other_down = lax.optimization_barrier((hidden, pick(down_weight, other)))
    other_down = swap(other_down)
    hidden = gather(hidden, ("y", "xh"), GROUP)
    down = down_project(core_index, hidden, down_weight, other_down, down_scale, other_scales)
    down = trade(down, ("zl", "xl"))
    down = jnp.sum(down.astype(F32), axis=0).astype(BF16)
    down = down.reshape(ZH, CAP, 2, width).transpose(0, 2, 1, 3).reshape(2 * ZH, 4, -1)
    down = trade(down, ("zh", "core")).reshape(ZH, 2, 4, -1)
    expert_out = jnp.sum(down.astype(F32), axis=0).reshape(2, CAP, width)

    combine = onehot.astype(F32) * combine_weights[:, :, None]
    mixed = jnp.einsum("tec,ecd->td", combine, expert_out, precision=lax.Precision.HIGHEST)
    return mixed.astype(BF16)


def solution(mesh):
    parts = Mesh(mesh.devices.reshape(tuple(SIZES.values())), tuple(SIZES))
    in_specs = (
        P(BLK, COL),
        P(BLK, None),
        P(BLK, None),
        P(None, COL, BLK),
        P(None, COL, BLK),
        P(None, COL, BLK),
        P(None, COL, BLK),
        P(None, BLK, COL),
        P(None, BLK, COL),
    )
    return jax.shard_map(
        shards, mesh=parts, in_specs=in_specs, out_specs=P(BLK, COL), check_vma=False
    )
```

time: 154 us -> 149 us (0.968)
  matrix products: 8.7 us -> 1.07 us
  Pallas kernels: 0 us -> 5.79 us
  blocking collectives: 52.2 us -> 49.5 us
  waiting for transfers between devices: 53.3 us -> 54.9 us
    dot_general x10 -> x0, matrix products: 7.63 us -> none  [blocked(): product = jnp.dot(rows[:, cut], weight[cut], preferred_element_type=F32)]
    pallas_call x0 -> x2, Pallas kernels: none -> 5.79 us  [the longest x1 3.44 us: gate_up(): pl.pallas_call(gate_up_kernel, grid_spec=pltpu.PrefetchScalarGridSpec(num...]
    all_to_all x2, blocking collectives: 52.2 us -> 49.5 us  [trade(): return lax.all_to_all(value, axes, 0, 0, tiled=True)]
    select_n x4 -> x0, other arithmetic: 2.25 us -> none  [the longest x3 2.18 us: both_cores(): first = jnp.where(core == 0, own, other)]
    all_to_all x4, waiting for transfers between devices: 51 us -> 52.9 us  [trade(): return lax.all_to_all(value, axes, 0, 0, tiled=True)]
    ppermute x4 -> x3, starting transfers between devices: 8.63 us -> 7.64 us  [swap(): return lax.ppermute(value, 'core', [(0, 1), (1, 0)])]
  transfers between devices with their start and end apart: 8 -> 7, of which waited for: 6 -> 6; matrix products, arithmetic and copies ran while one was open for 4% -> 1% of each run, Pallas kernels for 0% -> 0%
where the time goes in v3:
time: 149 us
  waiting for transfers between devices  54.9 us (37%)
  blocking collectives  49.5 us (33%)
  starting transfers between devices  29.4 us (20%)
  Pallas kernels  5.79 us (4%)
  local copies, waits for them, and re-layouts  4.14 us (3%)
  other arithmetic  3.8 us (3%)
    all_to_all x4, waiting for transfers between devices, trade(): return lax.all_to_all(value, axes, 0, 0, tiled=True)  52.9 us
    all_to_all x2, blocking collectives, trade(): return lax.all_to_all(value, axes, 0, 0, tiled=True)  49.5 us
    all_to_all x4, starting transfers between devices, trade(): return lax.all_to_all(value, axes, 0, 0, tiled=True)  21.7 us
    ppermute x3, starting transfers between devices, swap(): return lax.ppermute(value, 'core', [(0, 1), (1, 0)])  7.64 us
    pallas_call x1, Pallas kernels, gate_up(): pl.pallas_call(gate_up_kernel, grid_spec=pltpu.PrefetchScalarGridSpec(num...  3.44 us
  transfers between devices with their start and end apart: 7, of which 6 were waited for; matrix products, arithmetic and copies ran while one was open for 1% of the time, Pallas kernels for 0%

profile of v3, /device:TPU:1, one launch (start us, length us, event | category | flops | bytes accessed | tf_op | source)
XLA Modules:
  0.0 148.8 jit_solution(11007095299456675894)
XLA Ops:
  0.0 0.7 fusion.13
  0.7 0.1 copy.36
  1.0 0.1 convolution_convert_fusion
  1.2 36.4 %all_to_all.30 = bf16[16,4,1920]{2,1,0:T(4,128)(2,1)S(1)} all-to-all(bf16[16,4,1920]{2,1,0:T(4,128)(2,1)S(1)} %bitcast.26), channel_id=1, replica_groups=mesh['y'=4,'xh'=2,'core'=2,'zh'=8,'zl'=2,'xl'=2] {'zh','core'}, dimensions={0} | all-to-all | bytes 491520 | tf_op jit(solution)/shard_map/all_to_all | solution.py:41
  37.7 0.2 reshape.54
  37.8 0.2 copy.39
  38.1 1.0 broadcast_in_dim.44
  39.1 3.5 %all-to-all-start.1 = ((bf16[4,160,768]{2,1,0:T(8,128)(2,1)}), bf16[4,160,768]{2,1,0:T(8,128)(2,1)S(1)}, u32[]{:S(2)}, u32[]{:S(2)}) async-start(bf16[4,160,768]{2,1,0:T(8,128)(2,1)} %broadcast_in_dim.44), calls=%async_computation.1 | async-start | bytes 1966080 | tf_op jit(solution)/shard_map/all_to_all | solution.py:41
  42.8 1.0 pad_maximum_fusion
  43.7 1.9 %collective-permute-start.1 = (bf16[768,512]{1,0:T(8,128)(2,1)}, bf16[768,512]{1,0:T(8,128)(2,1)S(1)}, u32[]{:S(2)}, u32[]{:S(2)}) collective-permute-start(bf16[768,512]{1,0:T(8,128)(2,1)} %pad_maximum_fusion), channel_id=1, source_target_pairs={{0,32},{32,0},{1,33},{33,1},{2,34},{34,2},{3,35},{35,3},{4,36},{36... | collective-permute-start | bytes 2359304 | tf_op jit(solution)/shard_map/ppermute | solution.py:37
  46.1 2.4 %collective-permute-start = (f32[1,36]{1,0:T(1,128)S(1)}, f32[1,36]{1,0:T(1,128)S(1)}, u32[]{:S(2)}, u32[]{:S(2)}) collective-permute-start(f32[1,36]{1,0:T(1,128)S(1)} %pad_maximum_fusion.1), channel_id=1, source_target_pairs={{0,32},{32,0},{1,33},{33,1},{2,34},{34,2},{3,35},{35,3},{4,36},{36... | collective-permute-start | bytes 440 | tf_op jit(solution)/shard_map/ppermute | solution.py:37
  48.6 0.8 collective-permute-done.rs_ref
  49.3 5.9 %all-to-all-done.1.x_ref = bf16[4,160,768]{2,1,0:T(8,128)(2,1)S(1)} async-done(((bf16[4,160,768]{2,1,0:T(8,128)(2,1)}), bf16[4,160,768]{2,1,0:T(8,128)(2,1)S(1)}, u32[]{:S(2)}, u32[]{:S(2)}) %all-to-all-start.1) | async-done | bytes 983072 | tf_op jit(solution)/shard_map/all_to_all | solution.py:41
  55.3 3.4 %gate_up.1 = f32[8,80,1024]{2,1,0:T(8,128)S(1)} custom-call(s32[1]{0:T(128)} %bitcast.core_ref, f32[2,3,4]{2,1,0:T(4,128)S(1)} %copy.40.gs_ref, f32[2,3,4]{2,1,0:T(4,128)S(1)} %copy.41.us_ref, f32[1,36]{1,0:T(1,128)S(1)} %collective-permute-done.rs_ref, bf16[4,160,768]{2,1,0:T(8,128)(2,1)S(1)} %all-to-all-done.1.x_ref, bf16[2,384,512]{2,1,0:T(8,128)(2,1)S(1)} %copy-done.1, ...), custom_call_target="tpu_custom_call" | custom-call | flops 1006632960 | bytes 5177344 | tf_op jit(solution)/shard_map/gate_up/pallas_call | solution.py:90
  58.7 1.3 convert_element_type.34
  60.0 6.8 %all-to-all-start.2 = ((f16[8,80,1024]{2,1,0:T(8,128)(2,1)}), f16[8,80,1024]{2,1,0:T(8,128)(2,1)S(1)}, u32[]{:S(2)}, u32[]{:S(2)}) async-start(f16[8,80,1024]{2,1,0:T(8,128)(2,1)} %convert_element_type.34), calls=%async_computation.2 | async-start | bytes 2621440 | tf_op jit(solution)/shard_map/all_to_all | solution.py:41
  66.9 19.5 %all-to-all-done.2 = f16[8,80,1024]{2,1,0:T(8,128)(2,1)S(1)} async-done(((f16[8,80,1024]{2,1,0:T(8,128)(2,1)}), f16[8,80,1024]{2,1,0:T(8,128)(2,1)S(1)}, u32[]{:S(2)}, u32[]{:S(2)}) %all-to-all-start.2) | async-done | bytes 1310752 | tf_op jit(solution)/shard_map/all_to_all | solution.py:41
  86.4 0.3 convert_reduce_fusion
  86.8 0.9 broadcast_in_dim.45
  87.7 3.5 %all-to-all-start.3 = ((bf16[8,80,512]{2,1,0:T(8,128)(2,1)}), bf16[8,80,512]{2,1,0:T(8,128)(2,1)S(1)}, u32[]{:S(2)}, u32[]{:S(2)}) async-start(bf16[8,80,512]{2,1,0:T(8,128)(2,1)} %broadcast_in_dim.45), calls=%async_computation.3 | async-start | bytes 1310720 | tf_op jit(solution)/shard_map/all_to_all | solution.py:41
  91.2 3.3 %collective-permute-start.2 = (bf16[512,384]{1,0:T(8,128)(2,1)S(1)}, bf16[512,384]{1,0:T(8,128)(2,1)S(1)}, u32[]{:S(2)}, u32[]{:S(2)}) collective-permute-start(bf16[512,384]{1,0:T(8,128)(2,1)S(1)} %dynamic-slice_bitcast_fusion), channel_id=1, source_target_pairs={{0,32},{32,0},{1,33},{33,1},{2,34},{34,2},{3,35},{35,3},{4,36},{36... | collective-permute-start | bytes 1179656 | tf_op jit(solution)/shard_map/ppermute | solution.py:37
  94.6 0.1 copy.42.ds_ref
  94.7 1.2 collective-permute-done.2.rw_ref
  95.9 6.9 %all-to-all-done.3.h_ref = bf16[8,80,512]{2,1,0:T(8,128)(2,1)S(1)} async-done(((bf16[8,80,512]{2,1,0:T(8,128)(2,1)}), bf16[8,80,512]{2,1,0:T(8,128)(2,1)S(1)}, u32[]{:S(2)}, u32[]{:S(2)}) %all-to-all-start.3) | async-done | bytes 655392 | tf_op jit(solution)/shard_map/all_to_all | solution.py:41
  102.8 2.4 %down_project.1 = bf16[4,160,768]{2,1,0:T(8,128)(2,1)S(1)} custom-call(s32[1]{0:T(128)} %bitcast.core_ref, f32[2,4,3]{2,1,0:T(4,128)S(1)} %copy.42.ds_ref, f32[1,36]{1,0:T(1,128)S(1)} %collective-permute-done.rs_ref, bf16[8,80,512]{2,1,0:T(8,128)(2,1)S(1)} %all-to-all-done.3.h_ref, bf16[2,512,384]{2,1,0:T(8,128)(2,1)S(1)} %copy-done.3, ...), custom_call_target="tpu_custom_call" | custom-call | flops 503316480 | bytes 2424832 | tf_op jit(solution)/shard_map/down_project/pallas_call | solution.py:145
  105.1 13.1 %all_to_all.31 = bf16[4,160,768]{2,1,0:T(8,128)(2,1)S(1)} all-to-all(bf16[4,160,768]{2,1,0:T(8,128)(2,1)S(1)} %down_project.1), channel_id=1, replica_groups=mesh['y'=4,'xh'=2,'core'=2,'zh'=8,'zl'=2,'xl'=2] {'zl','xl'}, dimensions={0} | all-to-all | bytes 1966080 | tf_op jit(solution)/shard_map/all_to_all | solution.py:41
  118.2 0.1 reduce_sum.41
  118.5 0.8 reshape.56
  119.3 7.9 %all-to-all-start.5 = ((bf16[16,4,1920]{2,1,0:T(4,128)(2,1)}), bf16[16,4,1920]{2,1,0:T(4,128)(2,1)S(1)}, u32[]{:S(2)}, u32[]{:S(2)}) async-start(bf16[16,4,1920]{2,1,0:T(4,128)(2,1)} %reshape.56), calls=%async_computation.5 | async-start | bytes 491520 | tf_op jit(solution)/shard_map/all_to_all | solution.py:41
  127.2 20.5 %all-to-all-done.5 = bf16[16,4,1920]{2,1,0:T(4,128)(2,1)S(1)} async-done(((bf16[16,4,1920]{2,1,0:T(4,128)(2,1)}), bf16[16,4,1920]{2,1,0:T(4,128)(2,1)S(1)}, u32[]{:S(2)}, u32[]{:S(2)}) %all-to-all-start.5) | async-done | bytes 245792 | tf_op jit(solution)/shard_map/all_to_all | solution.py:41
  147.7 0.1 convert_reduce_fusion.1
  147.9 0.9 fusion
  (43 shorter events, 1.2 us)
Async XLA Ops:
  0.0 1.0 copy-start
  38.1 4.6 %copy-start.1 = (bf16[2,384,512]{2,1,0:T(8,128)(2,1)S(1)}, bf16[2,384,512]{2,1,0:T(8,128)(2,1)}, u32[]{:S(2)}) copy-start(bf16[2,384,512]{2,1,0:T(8,128)(2,1)} %gw_ref.1) | copy-start | bytes 2359300
  38.1 4.6 %copy-start.2 = (bf16[2,384,512]{2,1,0:T(8,128)(2,1)S(1)}, bf16[2,384,512]{2,1,0:T(8,128)(2,1)}, u32[]{:S(2)}) copy-start(bf16[2,384,512]{2,1,0:T(8,128)(2,1)} %uw_ref.1) | copy-start | bytes 2359300
  39.1 16.2 %all-to-all-start.1 = ((bf16[4,160,768]{2,1,0:T(8,128)(2,1)}), bf16[4,160,768]{2,1,0:T(8,128)(2,1)S(1)}, u32[]{:S(2)}, u32[]{:S(2)}) async-start(bf16[4,160,768]{2,1,0:T(8,128)(2,1)} %broadcast_in_dim.44), calls=%async_computation.1 | async-start | bytes 1966080 | tf_op jit(solution)/shard_map/all_to_all | solution.py:41
  42.7 3.0 %copy-start.5 = (f32[2,3,4]{2,0,1:T(2,128)S(1)}, f32[2,3,4]{2,0,1:T(2,128)}, u32[]{:S(2)}) copy-start(f32[2,3,4]{2,0,1:T(2,128)} %param.14) | copy-start | bytes 292
  42.7 3.0 %copy-start.6 = (f32[2,3,4]{2,0,1:T(2,128)S(1)}, f32[2,3,4]{2,0,1:T(2,128)}, u32[]{:S(2)}) copy-start(f32[2,3,4]{2,0,1:T(2,128)} %param.15) | copy-start | bytes 292
  42.7 3.2 %copy-start.4 = (f32[2,4,3]{1,0,2:T(2,128)S(1)}, f32[2,4,3]{1,0,2:T(2,128)}, u32[]{:S(2)}) copy-start(f32[2,4,3]{1,0,2:T(2,128)} %param.17) | copy-start | bytes 292
  43.7 5.6 %collective-permute-start.1 = (bf16[768,512]{1,0:T(8,128)(2,1)}, bf16[768,512]{1,0:T(8,128)(2,1)S(1)}, u32[]{:S(2)}, u32[]{:S(2)}) collective-permute-start(bf16[768,512]{1,0:T(8,128)(2,1)} %pad_maximum_fusion), channel_id=1, source_target_pairs={{0,32},{32,0},{1,33},{33,1},{2,34},{34,2},{3,35},{35,3},{4,36},{36... | collective-permute-start | bytes 2359304 | tf_op jit(solution)/shard_map/ppermute | solution.py:37
  46.1 3.2 %collective-permute-start = (f32[1,36]{1,0:T(1,128)S(1)}, f32[1,36]{1,0:T(1,128)S(1)}, u32[]{:S(2)}, u32[]{:S(2)}) collective-permute-start(f32[1,36]{1,0:T(1,128)S(1)} %pad_maximum_fusion.1), channel_id=1, source_target_pairs={{0,32},{32,0},{1,33},{33,1},{2,34},{34,2},{3,35},{35,3},{4,36},{36... | collective-permute-start | bytes 440 | tf_op jit(solution)/shard_map/ppermute | solution.py:37
  60.0 6.8 %copy-start.3 = (bf16[2,512,384]{2,1,0:T(8,128)(2,1)S(1)}, bf16[2,512,384]{2,1,0:T(8,128)(2,1)}, u32[]{:S(2)}) copy-start(bf16[2,512,384]{2,1,0:T(8,128)(2,1)} %dw_ref.1) | copy-start | bytes 2359300
  60.0 26.4 %all-to-all-start.2 = ((f16[8,80,1024]{2,1,0:T(8,128)(2,1)}), f16[8,80,1024]{2,1,0:T(8,128)(2,1)S(1)}, u32[]{:S(2)}, u32[]{:S(2)}) async-start(f16[8,80,1024]{2,1,0:T(8,128)(2,1)} %convert_element_type.34), calls=%async_computation.2 | async-start | bytes 2621440 | tf_op jit(solution)/shard_map/all_to_all | solution.py:41
  87.7 15.1 %all-to-all-start.3 = ((bf16[8,80,512]{2,1,0:T(8,128)(2,1)}), bf16[8,80,512]{2,1,0:T(8,128)(2,1)S(1)}, u32[]{:S(2)}, u32[]{:S(2)}) async-start(bf16[8,80,512]{2,1,0:T(8,128)(2,1)} %broadcast_in_dim.45), calls=%async_computation.3 | async-start | bytes 1310720 | tf_op jit(solution)/shard_map/all_to_all | solution.py:41
  91.2 4.7 %collective-permute-start.2 = (bf16[512,384]{1,0:T(8,128)(2,1)S(1)}, bf16[512,384]{1,0:T(8,128)(2,1)S(1)}, u32[]{:S(2)}, u32[]{:S(2)}) collective-permute-start(bf16[512,384]{1,0:T(8,128)(2,1)S(1)} %dynamic-slice_bitcast_fusion), channel_id=1, source_target_pairs={{0,32},{32,0},{1,33},{33,1},{2,34},{34,2},{3,35},{35,3},{4,36},{36... | collective-permute-start | bytes 1179656 | tf_op jit(solution)/shard_map/ppermute | solution.py:37
  118.2 9.0 %copy-start.7 = (s32[64,2]{0,1:T(2,128)S(1)}, s32[64,2]{0,1:T(2,128)}, u32[]{:S(2)}) copy-start(s32[64,2]{0,1:T(2,128)} %param.10) | copy-start | bytes 1540
  118.2 9.0 %copy-start.8 = (f32[64,2]{0,1:T(2,128)S(1)}, f32[64,2]{0,1:T(2,128)}, u32[]{:S(2)}) copy-start(f32[64,2]{0,1:T(2,128)} %param.11) | copy-start | bytes 1540
  119.3 28.4 %all-to-all-start.5 = ((bf16[16,4,1920]{2,1,0:T(4,128)(2,1)}), bf16[16,4,1920]{2,1,0:T(4,128)(2,1)S(1)}, u32[]{:S(2)}, u32[]{:S(2)}) async-start(bf16[16,4,1920]{2,1,0:T(4,128)(2,1)} %reshape.56), calls=%async_computation.5 | async-start | bytes 491520 | tf_op jit(solution)/shard_map/all_to_all | solution.py:41

commit v4 on v3

--- a/solution.py
+++ b/solution.py
@@ -49,16 +49,20 @@
     return lax.dynamic_index_in_dim(array, index, 0, keepdims=False)
 
 
+def flat_scales(scales, expert):
+    return jnp.concatenate([pick(scale, expert).reshape(1, -1) for scale in scales], axis=1)
+
+
 def scale_row(read, blocks):
     return jnp.concatenate([jnp.full((1, SB), read(block), F32) for block in blocks], axis=1)
 
 
-def gate_up_kernel(core_ref, gs_ref, us_ref, rs_ref, x_ref, gw_ref, uw_ref, rw_ref, o_ref):
+def gate_up_kernel(core_ref, os_ref, rs_ref, x_ref, gw_ref, uw_ref, rw_ref, o_ref):
     core = core_ref[0]
     depth, units = gw_ref.shape[1], gw_ref.shape[2]
     ks, ns = depth // SB, units // SB
     chunk = 2 * SB
-    for which, (own_scale, own_weight) in enumerate(((gs_ref, gw_ref), (us_ref, uw_ref))):
+    for which, own_weight in enumerate((gw_ref, uw_ref)):
         for n in range(units // chunk):
             columns = slice(n * chunk, (n + 1) * chunk)
             blocks = (2 * n, 2 * n + 1)
@@ -68,13 +72,13 @@
                 for k in range(ks):
                     offset = pl.multiple_of(base + k * SB, SB)
                     rows = x_ref[0, :, pl.ds(offset, SB)]
+                    place = (which * ks + k) * ns
                     if other == 0:
                         weight = own_weight[0, k * SB : (k + 1) * SB, columns]
-                        row = scale_row(lambda c: own_scale[core, k, c] * SHIFT, blocks)
+                        row = scale_row(lambda c: os_ref[0, place + c] * SHIFT, blocks)
                     else:
                         first = which * depth + k * SB
                         weight = rw_ref[first : first + SB, columns]
-                        place = (which * ks + k) * ns
                         row = scale_row(lambda c: rs_ref[0, place + c] * SHIFT, blocks)
                     product = jnp.dot(rows, weight, preferred_element_type=F32) * row
                     total = product if total is None else total + product
@@ -82,7 +86,7 @@
             o_ref[:, :, left : left + chunk] = total.reshape(o_ref.shape[:2] + (chunk,))
 
 
-def gate_up(core_index, portion, gate_weight, up_weight, other, gate_scale, up_scale, other_scale):
+def gate_up(core_index, portion, gate_weight, up_weight, other, own_scales, other_scales):
     near, near_rows, width2 = portion.shape
     _, depth, units = gate_weight.shape
     per = GROUP // near
@@ -95,7 +99,6 @@
             in_specs=[
                 smem,
                 smem,
-                smem,
                 pl.BlockSpec((1, near_rows, width2), lambda i, c: (i, 0, 0)),
                 pl.BlockSpec((1, depth, units), lambda i, c: (c[0], 0, 0)),
                 pl.BlockSpec((1, depth, units), lambda i, c: (c[0], 0, 0)),
@@ -111,10 +114,10 @@
             transcendentals=0,
         ),
         name="gate_up",
-    )(core_index, gate_scale, up_scale, other_scale, portion, gate_weight, up_weight, other)
-
-
-def down_kernel(core_ref, ds_ref, rs_ref, h_ref, dw_ref, rw_ref, o_ref):
+    )(core_index, own_scales, other_scales, portion, gate_weight, up_weight, other)
+
+
+def down_kernel(core_ref, os_ref, rs_ref, h_ref, dw_ref, rw_ref, o_ref):
     core = core_ref[0]
     depth, width = dw_ref.shape[1], dw_ref.shape[2]
     ks, ns = depth // SB, width // SB
@@ -127,7 +130,7 @@
             hidden = h_ref[:, :, cut].reshape(rows, SB)
             if other == 0:
                 weight = dw_ref[0, cut, :]
-                row = scale_row(lambda c: ds_ref[core, k, c], range(ns))
+                row = scale_row(lambda c: os_ref[0, start + k * ns + c], range(ns))
             else:
                 weight = rw_ref[cut, :]
                 row = scale_row(lambda c: rs_ref[0, start + k * ns + c], range(ns))
@@ -137,7 +140,7 @@
         o_ref[0, :, pl.ds(base, width)] = total.astype(o_ref.dtype)
 
 
-def down_project(core_index, hidden, down_weight, other, down_scale, other_scale):
+def down_project(core_index, hidden, down_weight, other, own_scales, other_scales):
     _, some_rows, depth = hidden.shape
     width = down_weight.shape[2]
     per = GROUP // NEAR
@@ -164,7 +167,7 @@
             transcendentals=0,
         ),
         name="down_project",
-    )(core_index, down_scale, other_scale, hidden, down_weight, other)
+    )(core_index, own_scales, other_scales, hidden, down_weight, other)
 
 
 def shards(
@@ -190,38 +193,41 @@
     far = jnp.broadcast_to(packed[None], (ZH,) + packed.shape).reshape(2 * ZH, 4, -1)
     far = trade(far, ("zh", "core")).reshape(ZH, 2, CAP, width)
     far = far.transpose(0, 2, 1, 3).reshape(near_rows, 2 * width)
+    other = 1 - core
+    core_index = jnp.reshape(core, (1,)).astype(jnp.int32)
+    scales = (gate_scale, up_scale, down_scale)
+    own_scales = flat_scales(scales, core)
+    other_scales = swap(flat_scales(scales, other))
+    other_gate_up = swap(jnp.concatenate([pick(gate_weight, other), pick(up_weight, other)], axis=0))
+    other_down = swap(pick(down_weight, other))
+    combine = onehot.astype(F32) * combine_weights[:, :, None]
+    (
+        far,
+        core_index,
+        own_scales,
+        other_scales,
+        other_gate_up,
+        other_down,
+        combine,
+    ) = lax.optimization_barrier(
+        (far, core_index, own_scales, other_scales, other_gate_up, other_down, combine)
+    )
     portion = gather(far, ("zl", "xl"), NEAR)
 
-    other = 1 - core
-    other_gate_up = swap(jnp.concatenate([pick(gate_weight, other), pick(up_weight, other)], axis=0))
-    scales = [pick(scale, other).reshape(1, -1) for scale in (gate_scale, up_scale, down_scale)]
-    other_scales = swap(jnp.concatenate(scales, axis=1))
-    core_index = jnp.reshape(core, (1,)).astype(jnp.int32)
-
     partial_sums = gate_up(
-        core_index,
-        portion,
-        gate_weight,
-        up_weight,
-        other_gate_up,
-        gate_scale,
-        up_scale,
-        other_scales,
+        core_index, portion, gate_weight, up_weight, other_gate_up, own_scales, other_scales
     ).astype(jnp.float16)
     received = trade(partial_sums, ("y", "xh"))
     summed = jnp.sum(received.astype(F32), axis=0) * (1.0 / SHIFT)
     hidden = (jax.nn.silu(summed[:, :hidden_width]) * summed[:, hidden_width:]).astype(BF16)
-    hidden, other_down = lax.optimization_barrier((hidden, pick(down_weight, other)))
-    other_down = swap(other_down)
     hidden = gather(hidden, ("y", "xh"), GROUP)
-    down = down_project(core_index, hidden, down_weight, other_down, down_scale, other_scales)
+    down = down_project(core_index, hidden, down_weight, other_down, own_scales, other_scales)
     down = trade(down, ("zl", "xl"))
     down = jnp.sum(down.astype(F32), axis=0).astype(BF16)
     down = down.reshape(ZH, CAP, 2, width).transpose(0, 2, 1, 3).reshape(2 * ZH, 4, -1)
     down = trade(down, ("zh", "core")).reshape(ZH, 2, 4, -1)
     expert_out = jnp.sum(down.astype(F32), axis=0).reshape(2, CAP, width)
 
-    combine = onehot.astype(F32) * combine_weights[:, :, None]
     mixed = jnp.einsum("tec,ecd->td", combine, expert_out, precision=lax.Precision.HIGHEST)
     return mixed.astype(BF16)
 

time: 149 us -> 145 us (0.973)
  blocking collectives: 49.5 us -> 97.8 us
  waiting for transfers between devices: 54.9 us -> 10.6 us
  starting transfers between devices: 29.4 us -> 22.9 us
  other arithmetic: 3.8 us -> 1.93 us
    all_to_all x2 -> x5, blocking collectives: 49.5 us -> 97.8 us  [trade(): return lax.all_to_all(value, axes, 0, 0, tiled=True)]
    all_to_all x4 -> x1, waiting for transfers between devices: 52.9 us -> 10.5 us  [trade(): return lax.all_to_all(value, axes, 0, 0, tiled=True)]
    all_to_all x4 -> x1, starting transfers between devices: 21.7 us -> 16.6 us  [trade(): return lax.all_to_all(value, axes, 0, 0, tiled=True)]
    ppermute x3, waiting for transfers between devices: 2.01 us -> 0.01 us  [swap(): return lax.ppermute(value, 'core', [(0, 1), (1, 0)])]
    squeeze x2, local copies, waits for them, and re-layouts: 0.11 us -> 2.03 us  [pick(): return lax.dynamic_index_in_dim(array, index, 0, keepdims=False)]
    broadcast_in_dim x2, local copies, waits for them, and re-layouts: 1.91 us -> 0.11 us  [gather(): return trade(jnp.broadcast_to(value[None], (count,) + value.shape), axes)]
  transfers between devices with their start and end apart: 7 -> 4, of which waited for: 6 -> 1; matrix products, arithmetic and copies ran while one was open for 1% -> 2% of each run, Pallas kernels for 0% -> 0%
where the time goes in v4:
time: 145 us
  blocking collectives  97.8 us (67%)
  starting transfers between devices  22.9 us (16%)
  waiting for transfers between devices  10.6 us (7%)
  Pallas kernels  5.6 us (4%)
  local copies, waits for them, and re-layouts  4.53 us (3%)
  other arithmetic  1.93 us (1%)
    all_to_all x5, blocking collectives, trade(): return lax.all_to_all(value, axes, 0, 0, tiled=True)  97.8 us
    all_to_all x1, starting transfers between devices, trade(): return lax.all_to_all(value, axes, 0, 0, tiled=True)  16.6 us
    all_to_all x1, waiting for transfers between devices, trade(): return lax.all_to_all(value, axes, 0, 0, tiled=True)  10.5 us
    ppermute x3, starting transfers between devices, swap(): return lax.ppermute(value, 'core', [(0, 1), (1, 0)])  6.33 us
    pallas_call x1, Pallas kernels, gate_up(): pl.pallas_call(gate_up_kernel, grid_spec=pltpu.PrefetchScalarGridSpec(num...  3.31 us
  transfers between devices with their start and end apart: 4, of which 1 were waited for; matrix products, arithmetic and copies ran while one was open for 2% of the time, Pallas kernels for 0%

profile of v4, /device:TPU:1, one launch (start us, length us, event | category | flops | bytes accessed | tf_op | source)
XLA Modules:
  0.0 144.7 jit_solution(4942622686009541336)
XLA Ops:
  0.0 0.7 fusion.8
  0.7 0.1 copy.30
  0.8 0.1 reduce_window_sum.11
  1.0 0.1 convolution_convert_fusion
  1.2 0.8 broadcast_in_dim.21
  1.9 16.6 %all-to-all-start = ((bf16[16,4,1920]{2,1,0:T(4,128)(2,1)}), bf16[16,4,1920]{2,1,0:T(4,128)(2,1)S(1)}, u32[]{:S(2)}, u32[]{:S(2)}) async-start(bf16[16,4,1920]{2,1,0:T(4,128)(2,1)} %bitcast.1), calls=%async_computation | async-start | bytes 491520 | tf_op jit(solution)/shard_map/all_to_all | solution.py:41
  18.6 1.2 dynamic-slice_bitcast_fusion.1
  19.9 2.0 %collective-permute-start.1 = (bf16[768,512]{1,0:T(8,128)(2,1)S(1)}, bf16[768,512]{1,0:T(8,128)(2,1)S(1)}, u32[]{:S(2)}, u32[]{:S(2)}) collective-permute-start(bf16[768,512]{1,0:T(8,128)(2,1)S(1)} %pad_maximum_fusion), channel_id=1, source_target_pairs={{0,32},{32,0},{1,33},{33,1},{2,34},{34,2},{3,35},{35,3},{4,36},{36... | collective-permute-start | bytes 2359304 | tf_op jit(solution)/shard_map/ppermute | solution.py:37
  22.0 0.1 copy.34
  22.1 0.1 reshape.73
  22.2 0.1 reshape.71
  22.4 2.3 %collective-permute-start = (f32[1,36]{1,0:T(1,128)S(1)}, f32[1,36]{1,0:T(1,128)S(1)}, u32[]{:S(2)}, u32[]{:S(2)}) collective-permute-start(f32[1,36]{1,0:T(1,128)S(1)} %pad_maximum_fusion.2), channel_id=1, source_target_pairs={{0,32},{32,0},{1,33},{33,1},{2,34},{34,2},{3,35},{35,3},{4,36},{36... | collective-permute-start | bytes 440 | tf_op jit(solution)/shard_map/ppermute | solution.py:37
  24.8 0.8 dynamic-slice_bitcast_fusion
  25.5 2.0 %collective-permute-start.2 = (bf16[512,384]{1,0:T(8,128)(2,1)}, bf16[512,384]{1,0:T(8,128)(2,1)S(1)}, u32[]{:S(2)}, u32[]{:S(2)}) collective-permute-start(bf16[512,384]{1,0:T(8,128)(2,1)} %dynamic-slice_bitcast_fusion), channel_id=1, source_target_pairs={{0,32},{32,0},{1,33},{33,1},{2,34},{34,2},{3,35},{35,3},{4,36},{36... | collective-permute-start | bytes 1179656 | tf_op jit(solution)/shard_map/ppermute | solution.py:37
  27.6 0.1 copy.33
  27.6 0.1 reshape.70
  28.0 10.5 %all-to-all-done = bf16[16,4,1920]{2,1,0:T(4,128)(2,1)S(1)} async-done(((bf16[16,4,1920]{2,1,0:T(4,128)(2,1)}), bf16[16,4,1920]{2,1,0:T(4,128)(2,1)S(1)}, u32[]{:S(2)}, u32[]{:S(2)}) %all-to-all-start) | async-done | bytes 245792 | tf_op jit(solution)/shard_map/all_to_all | solution.py:41
  38.6 0.2 reshape.65
  38.7 0.2 copy.32
  39.1 16.1 %all_to_all.30.x_ref = bf16[4,160,768]{2,1,0:T(8,128)(2,1)S(1)} all-to-all(bf16[4,160,768]{2,1,0:T(8,128)(2,1)S(1)} %broadcast_in_dim.24), channel_id=1, replica_groups=mesh['y'=4,'xh'=2,'core'=2,'zh'=8,'zl'=2,'xl'=2] {'zl','xl'}, dimensions={0} | all-to-all | bytes 1966080 | tf_op jit(solution)/shard_map/all_to_all | solution.py:41
  55.2 3.3 %gate_up.1 = f32[8,80,1024]{2,1,0:T(8,128)S(1)} custom-call(s32[1]{0:T(128)} %bitcast.3.core_ref, f32[1,36]{1,0:T(1,128)S(1)} %pad_maximum_fusion.1.os_ref, f32[1,36]{1,0:T(1,128)S(1)} %collective-permute-done.rs_ref, bf16[4,160,768]{2,1,0:T(8,128)(2,1)S(1)} %all_to_all.30.x_ref, bf16[2,384,512]{2,1,0:T(8,128)(2,1)S(1)} %copy-done.2, ...), custom_call_target="tpu_custom_call" | custom-call | flops 1006632960 | bytes 5177344 | tf_op jit(solution)/shard_map/gate_up/pallas_call | solution.py:94
  58.5 0.2 convert_element_type.34
  58.7 26.1 %all_to_all.31 = f16[8,80,1024]{2,1,0:T(8,128)(2,1)S(1)} all-to-all(f16[8,80,1024]{2,1,0:T(8,128)(2,1)S(1)} %convert_element_type.34), channel_id=1, replica_groups=mesh['y'=4,'xh'=2,'core'=2,'zh'=8,'zl'=2,'xl'=2] {'y','xh'}, dimensions={0} | all-to-all | bytes 2621440 | tf_op jit(solution)/shard_map/all_to_all | solution.py:41
  84.8 0.3 convert_reduce_fusion
  85.3 13.8 %all_to_all.32.h_ref = bf16[8,80,512]{2,1,0:T(8,128)(2,1)S(1)} all-to-all(bf16[8,80,512]{2,1,0:T(8,128)(2,1)S(1)} %broadcast_in_dim.25), channel_id=1, replica_groups=mesh['y'=4,'xh'=2,'core'=2,'zh'=8,'zl'=2,'xl'=2] {'y','xh'}, dimensions={0} | all-to-all | bytes 1310720 | tf_op jit(solution)/shard_map/all_to_all | solution.py:41
  99.1 2.3 %down_project.1 = bf16[4,160,768]{2,1,0:T(8,128)(2,1)S(1)} custom-call(s32[1]{0:T(128)} %bitcast.3.core_ref, f32[1,36]{1,0:T(1,128)S(1)} %pad_maximum_fusion.1.os_ref, f32[1,36]{1,0:T(1,128)S(1)} %collective-permute-done.rs_ref, bf16[8,80,512]{2,1,0:T(8,128)(2,1)S(1)} %all_to_all.32.h_ref, bf16[2,512,384]{2,1,0:T(8,128)(2,1)S(1)} %copy-done.1, ...), custom_call_target="tpu_custom_call" | custom-call | flops 503316480 | bytes 2424832 | tf_op jit(solution)/shard_map/down_project/pallas_call | solution.py:148
  101.4 12.9 %all_to_all.33 = bf16[4,160,768]{2,1,0:T(8,128)(2,1)S(1)} all-to-all(bf16[4,160,768]{2,1,0:T(8,128)(2,1)S(1)} %down_project.1), channel_id=1, replica_groups=mesh['y'=4,'xh'=2,'core'=2,'zh'=8,'zl'=2,'xl'=2] {'zl','xl'}, dimensions={0} | all-to-all | bytes 1966080 | tf_op jit(solution)/shard_map/all_to_all | solution.py:41
  114.3 0.1 reduce_sum.41
  114.6 0.1 reshape.75
  114.7 28.9 %all_to_all.34 = bf16[16,4,1920]{2,1,0:T(4,128)(2,1)S(1)} all-to-all(bf16[16,4,1920]{2,1,0:T(4,128)(2,1)S(1)} %reshape.75), channel_id=1, replica_groups=mesh['y'=4,'xh'=2,'core'=2,'zh'=8,'zl'=2,'xl'=2] {'zh','core'}, dimensions={0} | all-to-all | bytes 491520 | tf_op jit(solution)/shard_map/all_to_all | solution.py:41
  143.6 0.1 convert_reduce_fusion.1
  143.8 0.9 fusion
  (43 shorter events, 1.1 us)
Async XLA Ops:
  0.0 1.0 copy-start
  1.9 36.6 %all-to-all-start = ((bf16[16,4,1920]{2,1,0:T(4,128)(2,1)}), bf16[16,4,1920]{2,1,0:T(4,128)(2,1)S(1)}, u32[]{:S(2)}, u32[]{:S(2)}) async-start(bf16[16,4,1920]{2,1,0:T(4,128)(2,1)} %bitcast.1), calls=%async_computation | async-start | bytes 491520 | tf_op jit(solution)/shard_map/all_to_all | solution.py:41
  18.5 3.4 %copy-start.4 = (f32[2,4,3]{1,0,2:T(2,128)S(1)}, f32[2,4,3]{1,0,2:T(2,128)}, u32[]{:S(2)}) copy-start(f32[2,4,3]{1,0,2:T(2,128)} %param.17) | copy-start | bytes 292
  18.5 3.6 %copy-start.5 = (f32[2,3,4]{2,0,1:T(2,128)S(1)}, f32[2,3,4]{2,0,1:T(2,128)}, u32[]{:S(2)}) copy-start(f32[2,3,4]{2,0,1:T(2,128)} %param.14) | copy-start | bytes 292
  18.6 3.6 %copy-start.6 = (f32[2,3,4]{2,0,1:T(2,128)S(1)}, f32[2,3,4]{2,0,1:T(2,128)}, u32[]{:S(2)}) copy-start(f32[2,3,4]{2,0,1:T(2,128)} %param.15) | copy-start | bytes 292
  18.6 6.2 %copy-start.1 = (bf16[2,512,384]{2,1,0:T(8,128)(2,1)S(1)}, bf16[2,512,384]{2,1,0:T(8,128)(2,1)}, u32[]{:S(2)}) copy-start(bf16[2,512,384]{2,1,0:T(8,128)(2,1)} %dw_ref.1) | copy-start | bytes 2359300
  19.8 8.2 %copy-start.7 = (f32[64,2]{0,1:T(2,128)S(1)}, f32[64,2]{0,1:T(2,128)}, u32[]{:S(2)}) copy-start(f32[64,2]{0,1:T(2,128)} %param.11) | copy-start | bytes 1540
  19.8 8.1 %copy-start.8 = (s32[64,2]{0,1:T(2,128)S(1)}, s32[64,2]{0,1:T(2,128)}, u32[]{:S(2)}) copy-start(s32[64,2]{0,1:T(2,128)} %param.10) | copy-start | bytes 1540
  19.9 19.1 %collective-permute-start.1 = (bf16[768,512]{1,0:T(8,128)(2,1)S(1)}, bf16[768,512]{1,0:T(8,128)(2,1)S(1)}, u32[]{:S(2)}, u32[]{:S(2)}) collective-permute-start(bf16[768,512]{1,0:T(8,128)(2,1)S(1)} %pad_maximum_fusion), channel_id=1, source_target_pairs={{0,32},{32,0},{1,33},{33,1},{2,34},{34,2},{3,35},{35,3},{4,36},{36... | collective-permute-start | bytes 2359304 | tf_op jit(solution)/shard_map/ppermute | solution.py:37
  22.4 16.5 %collective-permute-start = (f32[1,36]{1,0:T(1,128)S(1)}, f32[1,36]{1,0:T(1,128)S(1)}, u32[]{:S(2)}, u32[]{:S(2)}) collective-permute-start(f32[1,36]{1,0:T(1,128)S(1)} %pad_maximum_fusion.2), channel_id=1, source_target_pairs={{0,32},{32,0},{1,33},{33,1},{2,34},{34,2},{3,35},{35,3},{4,36},{36... | collective-permute-start | bytes 440 | tf_op jit(solution)/shard_map/ppermute | solution.py:37
  25.5 13.4 %collective-permute-start.2 = (bf16[512,384]{1,0:T(8,128)(2,1)}, bf16[512,384]{1,0:T(8,128)(2,1)S(1)}, u32[]{:S(2)}, u32[]{:S(2)}) collective-permute-start(bf16[512,384]{1,0:T(8,128)(2,1)} %dynamic-slice_bitcast_fusion), channel_id=1, source_target_pairs={{0,32},{32,0},{1,33},{33,1},{2,34},{34,2},{3,35},{35,3},{4,36},{36... | collective-permute-start | bytes 1179656 | tf_op jit(solution)/shard_map/ppermute | solution.py:37
  39.0 16.2 %copy-start.2 = (bf16[2,384,512]{2,1,0:T(8,128)(2,1)S(1)}, bf16[2,384,512]{2,1,0:T(8,128)(2,1)}, u32[]{:S(2)}) copy-start(bf16[2,384,512]{2,1,0:T(8,128)(2,1)} %gw_ref.1) | copy-start | bytes 2359300
  39.0 16.2 %copy-start.3 = (bf16[2,384,512]{2,1,0:T(8,128)(2,1)S(1)}, bf16[2,384,512]{2,1,0:T(8,128)(2,1)}, u32[]{:S(2)}) copy-start(bf16[2,384,512]{2,1,0:T(8,128)(2,1)} %uw_ref.1) | copy-start | bytes 2359300

commit v5 on v4

v5 whole, which is shorter than its diff:
```python
import jax
import jax.numpy as jnp
from jax import lax
from jax.experimental import pallas as pl
from jax.experimental.pallas import tpu as pltpu
from jax.sharding import Mesh, PartitionSpec as P

EXPW = 2
CAP = 20
SB = 128
COL = ("y", "xh", "core")
BLK = ("zh", "zl", "xl")
SIZES = {"y": 4, "xh": 2, "core": 2, "zh": 8, "zl": 2, "xl": 2}
ZH = SIZES["zh"]
NEAR = SIZES["zl"] * SIZES["xl"]
GROUP = SIZES["y"] * SIZES["xh"]
F32 = jnp.float32
BF16 = jnp.bfloat16
SHIFT = 64.0


def dispatch(route_ids, route_gates):
    expert_ids = jnp.arange(EXPW, dtype=jnp.int32)
    matches = route_ids[:, :, None] == expert_ids[None, None, :]
    chosen = jnp.any(matches, axis=1)
    combine_weights = jnp.sum(
        jnp.where(matches, route_gates[:, :, None], jnp.zeros((), route_gates.dtype)), axis=1
    )
    slot_index = jnp.cumsum(chosen.astype(jnp.int32), axis=0) - 1
    onehot = chosen[:, :, None] & (
        slot_index[:, :, None] == jnp.arange(CAP, dtype=jnp.int32)[None, None, :]
    )
    return (onehot, combine_weights)


def swap(value):
    return lax.ppermute(value, "core", [(0, 1), (1, 0)])


def trade(value, axes):
    return lax.all_to_all(value, axes, 0, 0, tiled=True)


def gather(value, axes, count):
    return trade(jnp.broadcast_to(value[None], (count,) + value.shape), axes)


def pick(array, index):
    return lax.dynamic_index_in_dim(array, index, 0, keepdims=False)


def flat_scales(scales, expert):
    return jnp.concatenate([pick(scale, expert).reshape(1, -1) for scale in scales], axis=1)


def scale_row(read, blocks):
    return jnp.concatenate([jnp.full((1, SB), read(block), F32) for block in blocks], axis=1)


def gate_up_kernel(core_ref, os_ref, rs_ref, x_ref, gw_ref, uw_ref, rw_ref, o_ref):
    core = core_ref[0]
    near, _, _, depth = x_ref.shape
    units = gw_ref.shape[2]
    ks, ns = depth // SB, units // SB
    chunk = 2 * SB
    per = o_ref.shape[0] // near
    for i in range(near):
        for which, own_weight in enumerate((gw_ref, uw_ref)):
            for n in range(units // chunk):
                columns = slice(n * chunk, (n + 1) * chunk)
                blocks = (2 * n, 2 * n + 1)
                total = None
                for part, scale_ref in ((core, os_ref), (1 - core, rs_ref)):
                    for k in range(ks):
                        cut = slice(k * SB, (k + 1) * SB)
                        rows = x_ref[i, part, :, cut]
                        if scale_ref is os_ref:
                            weight = own_weight[0, cut, columns]
                        else:
                            first = which * depth + k * SB
                            weight = rw_ref[first : first + SB, columns]
                        place = (which * ks + k) * ns
                        row = scale_row(lambda c: scale_ref[0, place + c] * SHIFT, blocks)
                        product = jnp.dot(rows, weight, preferred_element_type=F32) * row
                        total = product if total is None else total + product
                left = which * units + n * chunk
                o_ref[i * per : (i + 1) * per, :, left : left + chunk] = total.reshape(
                    (per, o_ref.shape[1], chunk)
                )


def whole(shape):
    return pl.BlockSpec(shape, lambda i, c: (0,) * len(shape))


def expert_part(shape):
    return pl.BlockSpec((1,) + shape[1:], lambda i, c: (c[0],) + (0,) * (len(shape) - 1))


def gate_up(core_index, portion, gate_weight, up_weight, other, own_scales, other_scales):
    near, _, near_rows, depth = portion.shape
    units = gate_weight.shape[2]
    out = (GROUP, near * near_rows // GROUP, 2 * units)
    smem = pl.BlockSpec(memory_space=pltpu.SMEM)
    return pl.pallas_call(
        gate_up_kernel,
        grid_spec=pltpu.PrefetchScalarGridSpec(
            num_scalar_prefetch=1,
            grid=(1,),
            in_specs=[
                smem,
                smem,
                whole(portion.shape),
                expert_part(gate_weight.shape),
                expert_part(up_weight.shape),
                whole(other.shape),
            ],
            out_specs=whole(out),
        ),
        out_shape=jax.ShapeDtypeStruct(out, F32),
        compiler_params=pltpu.CompilerParams(vmem_limit_bytes=32 * 1024 * 1024),
        cost_estimate=pl.CostEstimate(
            flops=8 * near * near_rows * depth * units,
            bytes_accessed=near * near_rows * (4 * depth + 8 * units) + 8 * depth * units,
            transcendentals=0,
        ),
        name="gate_up",
    )(core_index, own_scales, other_scales, portion, gate_weight, up_weight, other)


def down_kernel(core_ref, os_ref, rs_ref, h_ref, dw_ref, rw_ref, o_ref):
    core = core_ref[0]
    near, _, rows, width = o_ref.shape
    depth = h_ref.shape[2]
    ks, ns = depth // SB, width // SB
    start = rs_ref.shape[1] - ks * ns
    per = h_ref.shape[0] // near
    for i in range(near):
        for part, scale_ref in ((core, os_ref), (1 - core, rs_ref)):
            total = None
            for k in range(ks):
                cut = slice(k * SB, (k + 1) * SB)
                hidden = h_ref[i * per : (i + 1) * per, :, cut].reshape(rows, SB)
                weight = dw_ref[0, cut, :] if scale_ref is os_ref else rw_ref[cut, :]
                row = scale_row(lambda c: scale_ref[0, start + k * ns + c], range(ns))
                product = jnp.dot(hidden, weight, preferred_element_type=F32) * row
                total = product if total is None else total + product
            o_ref[i, part] = total.astype(o_ref.dtype)


def down_project(core_index, hidden, down_weight, other, own_scales, other_scales):
    _, some_rows, depth = hidden.shape
    width = down_weight.shape[2]
    rows = GROUP * some_rows
    out = (NEAR, 2, rows // NEAR, width)
    smem = pl.BlockSpec(memory_space=pltpu.SMEM)
    return pl.pallas_call(
        down_kernel,
        grid_spec=pltpu.PrefetchScalarGridSpec(
            num_scalar_prefetch=1,
            grid=(1,),
            in_specs=[
                smem,
                smem,
                whole(hidden.shape),
                expert_part(down_weight.shape),
                whole(other.shape),
            ],
            out_specs=whole(out),
        ),
        out_shape=jax.ShapeDtypeStruct(out, BF16),
        compiler_params=pltpu.CompilerParams(vmem_limit_bytes=32 * 1024 * 1024),
        cost_estimate=pl.CostEstimate(
            flops=4 * rows * depth * width,
            bytes_accessed=rows * (2 * depth + 4 * width) + 4 * depth * width,
            transcendentals=0,
        ),
        name="down_project",
    )(core_index, own_scales, other_scales, hidden, down_weight, other)


def shards(
    tokens,
    route_ids,
    route_gates,
    gate_weight,
    up_weight,
    gate_scale,
    up_scale,
    down_weight,
    down_scale,
):
    core = lax.axis_index("core")
    width = tokens.shape[1]
    hidden_width = gate_weight.shape[2]
    near_rows = ZH * CAP
    onehot, combine_weights = dispatch(route_ids, route_gates)
    slot_rows = jnp.einsum(
        "tec,td->ecd", onehot.astype(BF16), tokens, preferred_element_type=F32
    ).astype(BF16)
    packed = slot_rows.reshape(8, -1)
    far = gather(packed, "zh", ZH).reshape(ZH, 2, CAP, width)
    far = far.transpose(1, 0, 2, 3).reshape(2, near_rows, width)

    other = 1 - core
    core_index = jnp.reshape(core, (1,)).astype(jnp.int32)
    scales = (gate_scale, up_scale, down_scale)
    own_scales = flat_scales(scales, core)
    other_scales = swap(flat_scales(scales, other))
    other_gate_up = swap(jnp.concatenate([pick(gate_weight, other), pick(up_weight, other)], axis=0))
    other_down = swap(pick(down_weight, other))
    combine = onehot.astype(F32) * combine_weights[:, :, None]
    (
        far,
        core_index,
        own_scales,
        other_scales,
        other_gate_up,
        other_down,
        combine,
    ) = lax.optimization_barrier(
        (far, core_index, own_scales, other_scales, other_gate_up, other_down, combine)
    )
    portion = jnp.broadcast_to(far[None], (NEAR,) + far.shape).reshape(2 * NEAR, near_rows, width)
    portion = trade(portion, ("zl", "xl", "core")).reshape(NEAR, 2, near_rows, width)

    partial_sums = gate_up(
        core_index, portion, gate_weight, up_weight, other_gate_up, own_scales, other_scales
    ).astype(jnp.float16)
    received = trade(partial_sums, ("y", "xh"))
    summed = jnp.sum(received.astype(F32), axis=0) * (1.0 / SHIFT)
    hidden = (jax.nn.silu(summed[:, :hidden_width]) * summed[:, hidden_width:]).astype(BF16)
    hidden = gather(hidden, ("y", "xh"), GROUP)
    down = down_project(core_index, hidden, down_weight, other_down, own_scales, other_scales)
    down = trade(down.reshape(2 * NEAR, near_rows, width), ("zl", "xl", "core"))
    down = jnp.sum(down.reshape(NEAR, 2, near_rows, width).astype(F32), axis=0).astype(BF16)
    down = down.reshape(2, ZH, CAP, width).transpose(1, 0, 2, 3).reshape(ZH, 8, -1)
    down = trade(down, "zh")
    expert_out = jnp.sum(down.astype(F32), axis=0).reshape(2, CAP, width)

    mixed = jnp.einsum("tec,ecd->td", combine, expert_out, precision=lax.Precision.HIGHEST)
    return mixed.astype(BF16)


def solution(mesh):
    parts = Mesh(mesh.devices.reshape(tuple(SIZES.values())), tuple(SIZES))
    in_specs = (
        P(BLK, COL),
        P(BLK, None),
        P(BLK, None),
        P(None, COL, BLK),
        P(None, COL, BLK),
        P(None, COL, BLK),
        P(None, COL, BLK),
        P(None, BLK, COL),
        P(None, BLK, COL),
    )
    return jax.shard_map(
        shards, mesh=parts, in_specs=in_specs, out_specs=P(BLK, COL), check_vma=False
    )
```

time: 145 us -> 143 us (0.986)
  the two profiles are of different devices: /device:TPU:1 before, /device:TPU:2 now
where the time goes in v5:
time: 143 us; the launch traced here: 142 us
  blocking collectives  97.1 us (68%)
  starting transfers between devices  21.3 us (15%)
  waiting for transfers between devices  11.3 us (8%)
  local copies, waits for them, and re-layouts  4.76 us (3%)
  Pallas kernels  4.52 us (3%)
  other arithmetic  1.94 us (1%)
    all_to_all x5, blocking collectives, trade(): return lax.all_to_all(value, axes, 0, 0, tiled=True)  97.1 us
    all_to_all x1, starting transfers between devices, trade(): return lax.all_to_all(value, axes, 0, 0, tiled=True)  15.1 us
    all_to_all x1, waiting for transfers between devices, trade(): return lax.all_to_all(value, axes, 0, 0, tiled=True)  11.3 us
    ppermute x3, starting transfers between devices, swap(): return lax.ppermute(value, 'core', [(0, 1), (1, 0)])  6.23 us
  transfers between devices with their start and end apart: 4, of which 1 were waited for; matrix products, arithmetic and copies ran while one was open for 2% of the time, Pallas kernels for 0%

profile of v5, /device:TPU:2, one launch (start us, length us, event | category | flops | bytes accessed | tf_op | source)
XLA Modules:
  0.0 142.3 jit_solution(17549842933435985064)
XLA Ops:
  0.0 0.7 fusion.8
  0.7 0.1 copy.35
  0.8 0.1 reduce_window_sum.11
  1.0 0.1 convolution_convert_fusion
  1.2 0.7 broadcast_in_dim.21
  1.9 15.1 %all-to-all-start = ((bf16[8,8,1920]{2,1,0:T(8,128)(2,1)}), bf16[8,8,1920]{2,1,0:T(8,128)(2,1)S(1)}, u32[]{:S(2)}, u32[]{:S(2)}) async-start(bf16[8,8,1920]{2,1,0:T(8,128)(2,1)} %broadcast_in_dim.21), calls=%async_computation | async-start | bytes 491520 | tf_op jit(solution)/shard_map/all_to_all | solution.py:41
  17.0 1.2 dynamic-slice_bitcast_fusion.1
  18.4 1.9 %collective-permute-start.1 = (bf16[768,512]{1,0:T(8,128)(2,1)S(1)}, bf16[768,512]{1,0:T(8,128)(2,1)S(1)}, u32[]{:S(2)}, u32[]{:S(2)}) collective-permute-start(bf16[768,512]{1,0:T(8,128)(2,1)S(1)} %pad_maximum_fusion), channel_id=1, source_target_pairs={{0,32},{32,0},{1,33},{33,1},{2,34},{34,2},{3,35},{35,3},{4,36},{36... | collective-permute-start | bytes 2359304 | tf_op jit(solution)/shard_map/ppermute | solution.py:37
  20.3 0.1 copy.39
  20.4 0.1 reshape.78
  20.8 2.4 %collective-permute-start = (f32[1,36]{1,0:T(1,128)S(1)}, f32[1,36]{1,0:T(1,128)S(1)}, u32[]{:S(2)}, u32[]{:S(2)}) collective-permute-start(f32[1,36]{1,0:T(1,128)S(1)} %pad_maximum_fusion.2), channel_id=1, source_target_pairs={{0,32},{32,0},{1,33},{33,1},{2,34},{34,2},{3,35},{35,3},{4,36},{36... | collective-permute-start | bytes 440 | tf_op jit(solution)/shard_map/ppermute | solution.py:37
  23.2 0.8 dynamic-slice_bitcast_fusion
  24.0 1.9 %collective-permute-start.2 = (bf16[512,384]{1,0:T(8,128)(2,1)}, bf16[512,384]{1,0:T(8,128)(2,1)S(1)}, u32[]{:S(2)}, u32[]{:S(2)}) collective-permute-start(bf16[512,384]{1,0:T(8,128)(2,1)} %dynamic-slice_bitcast_fusion), channel_id=1, source_target_pairs={{0,32},{32,0},{1,33},{33,1},{2,34},{34,2},{3,35},{35,3},{4,36},{36... | collective-permute-start | bytes 1179656 | tf_op jit(solution)/shard_map/ppermute | solution.py:37
  25.9 0.1 copy.38
  26.0 0.1 reshape.75
  26.4 11.3 %all-to-all-done = bf16[8,8,1920]{2,1,0:T(8,128)(2,1)S(1)} async-done(((bf16[8,8,1920]{2,1,0:T(8,128)(2,1)}), bf16[8,8,1920]{2,1,0:T(8,128)(2,1)S(1)}, u32[]{:S(2)}, u32[]{:S(2)}) %all-to-all-start) | async-done | bytes 245792 | tf_op jit(solution)/shard_map/all_to_all | solution.py:41
  37.7 0.2 reshape.70
  37.9 0.2 copy.37
  38.2 0.1 broadcast_in_dim.24
  38.3 16.6 %all_to_all.30 = bf16[8,160,384]{2,1,0:T(8,128)(2,1)S(1)} all-to-all(bf16[8,160,384]{2,1,0:T(8,128)(2,1)S(1)} %bitcast.28), channel_id=1, replica_groups=mesh['y'=4,'xh'=2,'core'=2,'zh'=8,'zl'=2,'xl'=2] {'zl','xl','core'}, dimensions={0} | all-to-all | bytes 1966080 | tf_op jit(solution)/shard_map/all_to_all | solution.py:41
  54.8 2.8 %gate_up.1 = f32[8,80,1024]{2,1,0:T(8,128)S(1)} custom-call(s32[1]{0:T(128)} %bitcast.3.core_ref, f32[1,36]{1,0:T(1,128)S(1)} %pad_maximum_fusion.1.os_ref, f32[1,36]{1,0:T(1,128)S(1)} %collective-permute-done.rs_ref, bf16[4,2,160,384]{3,2,1,0:T(8,128)(2,1)S(1)} %bitcast.26, bf16[2,384,512]{2,1,0:T(8,128)(2,1)S(1)} %copy-done.2, ...), custom_call_target="tpu_custom_call" | custom-call | flops 1006632960 | bytes 5177344 | tf_op jit(solution)/shard_map/gate_up/pallas_call | solution.py:105
  57.6 0.2 convert_element_type.31
  57.9 25.7 %all_to_all.31 = f16[8,80,1024]{2,1,0:T(8,128)(2,1)S(1)} all-to-all(f16[8,80,1024]{2,1,0:T(8,128)(2,1)S(1)} %convert_element_type.31), channel_id=1, replica_groups=mesh['y'=4,'xh'=2,'core'=2,'zh'=8,'zl'=2,'xl'=2] {'y','xh'}, dimensions={0} | all-to-all | bytes 2621440 | tf_op jit(solution)/shard_map/all_to_all | solution.py:41
  83.6 0.3 convert_reduce_fusion
  84.0 14.4 %all_to_all.32.h_ref = bf16[8,80,512]{2,1,0:T(8,128)(2,1)S(1)} all-to-all(bf16[8,80,512]{2,1,0:T(8,128)(2,1)S(1)} %broadcast_in_dim.25), channel_id=1, replica_groups=mesh['y'=4,'xh'=2,'core'=2,'zh'=8,'zl'=2,'xl'=2] {'y','xh'}, dimensions={0} | all-to-all | bytes 1310720 | tf_op jit(solution)/shard_map/all_to_all | solution.py:41
  98.5 1.8 %down_project.1 = bf16[4,2,160,384]{3,2,1,0:T(8,128)(2,1)S(1)} custom-call(s32[1]{0:T(128)} %bitcast.3.core_ref, f32[1,36]{1,0:T(1,128)S(1)} %pad_maximum_fusion.1.os_ref, f32[1,36]{1,0:T(1,128)S(1)} %collective-permute-done.rs_ref, bf16[8,80,512]{2,1,0:T(8,128)(2,1)S(1)} %all_to_all.32.h_ref, bf16[2,512,384]{2,1,0:T(8,128)(2,1)S(1)} %copy-done.1, ...), custom_call_target="tpu_custom_call" | custom-call | flops 503316480 | bytes 2424832 | tf_op jit(solution)/shard_map/down_project/pallas_call | solution.py:157
  100.2 17.3 %all_to_all.33 = bf16[8,160,384]{2,1,0:T(8,128)(2,1)S(1)} all-to-all(bf16[8,160,384]{2,1,0:T(8,128)(2,1)S(1)} %bitcast.25), channel_id=1, replica_groups=mesh['y'=4,'xh'=2,'core'=2,'zh'=8,'zl'=2,'xl'=2] {'zl','xl','core'}, dimensions={0} | all-to-all | bytes 1966080 | tf_op jit(solution)/shard_map/all_to_all | solution.py:41
  117.5 0.2 reduce_sum.41
  117.7 0.2 copy.41
  118.0 0.2 reshape.84
  118.2 23.1 %all_to_all.34 = bf16[8,8,1920]{2,1,0:T(8,128)(2,1)S(1)} all-to-all(bf16[8,8,1920]{2,1,0:T(8,128)(2,1)S(1)} %reshape.84), channel_id=1, replica_groups=mesh['y'=4,'xh'=2,'core'=2,'zh'=8,'zl'=2,'xl'=2] {'zh'}, dimensions={0} | all-to-all | bytes 491520 | tf_op jit(solution)/shard_map/all_to_all | solution.py:41
  141.4 0.9 fusion
  (43 shorter events, 1.0 us)
Async XLA Ops:
  0.0 1.0 copy-start
  1.9 35.8 %all-to-all-start = ((bf16[8,8,1920]{2,1,0:T(8,128)(2,1)}), bf16[8,8,1920]{2,1,0:T(8,128)(2,1)S(1)}, u32[]{:S(2)}, u32[]{:S(2)}) async-start(bf16[8,8,1920]{2,1,0:T(8,128)(2,1)} %broadcast_in_dim.21), calls=%async_computation | async-start | bytes 491520 | tf_op jit(solution)/shard_map/all_to_all | solution.py:41
  17.0 3.3 %copy-start.4 = (f32[2,4,3]{1,0,2:T(2,128)S(1)}, f32[2,4,3]{1,0,2:T(2,128)}, u32[]{:S(2)}) copy-start(f32[2,4,3]{1,0,2:T(2,128)} %param.17) | copy-start | bytes 292
  17.0 3.5 %copy-start.5 = (f32[2,3,4]{2,0,1:T(2,128)S(1)}, f32[2,3,4]{2,0,1:T(2,128)}, u32[]{:S(2)}) copy-start(f32[2,3,4]{2,0,1:T(2,128)} %param.14) | copy-start | bytes 292
  17.0 3.5 %copy-start.6 = (f32[2,3,4]{2,0,1:T(2,128)S(1)}, f32[2,3,4]{2,0,1:T(2,128)}, u32[]{:S(2)}) copy-start(f32[2,3,4]{2,0,1:T(2,128)} %param.15) | copy-start | bytes 292
  17.0 6.2 %copy-start.1 = (bf16[2,512,384]{2,1,0:T(8,128)(2,1)S(1)}, bf16[2,512,384]{2,1,0:T(8,128)(2,1)}, u32[]{:S(2)}) copy-start(bf16[2,512,384]{2,1,0:T(8,128)(2,1)} %dw_ref.1) | copy-start | bytes 2359300
  18.3 8.1 %copy-start.7 = (f32[64,2]{0,1:T(2,128)S(1)}, f32[64,2]{0,1:T(2,128)}, u32[]{:S(2)}) copy-start(f32[64,2]{0,1:T(2,128)} %param.11) | copy-start | bytes 1540
  18.3 8.0 %copy-start.8 = (s32[64,2]{0,1:T(2,128)S(1)}, s32[64,2]{0,1:T(2,128)}, u32[]{:S(2)}) copy-start(s32[64,2]{0,1:T(2,128)} %param.10) | copy-start | bytes 1540
  18.4 19.7 %collective-permute-start.1 = (bf16[768,512]{1,0:T(8,128)(2,1)S(1)}, bf16[768,512]{1,0:T(8,128)(2,1)S(1)}, u32[]{:S(2)}, u32[]{:S(2)}) collective-permute-start(bf16[768,512]{1,0:T(8,128)(2,1)S(1)} %pad_maximum_fusion), channel_id=1, source_target_pairs={{0,32},{32,0},{1,33},{33,1},{2,34},{34,2},{3,35},{35,3},{4,36},{36... | collective-permute-start | bytes 2359304 | tf_op jit(solution)/shard_map/ppermute | solution.py:37
  20.8 17.3 %collective-permute-start = (f32[1,36]{1,0:T(1,128)S(1)}, f32[1,36]{1,0:T(1,128)S(1)}, u32[]{:S(2)}, u32[]{:S(2)}) collective-permute-start(f32[1,36]{1,0:T(1,128)S(1)} %pad_maximum_fusion.2), channel_id=1, source_target_pairs={{0,32},{32,0},{1,33},{33,1},{2,34},{34,2},{3,35},{35,3},{4,36},{36... | collective-permute-start | bytes 440 | tf_op jit(solution)/shard_map/ppermute | solution.py:37
  24.0 14.1 %collective-permute-start.2 = (bf16[512,384]{1,0:T(8,128)(2,1)}, bf16[512,384]{1,0:T(8,128)(2,1)S(1)}, u32[]{:S(2)}, u32[]{:S(2)}) collective-permute-start(bf16[512,384]{1,0:T(8,128)(2,1)} %dynamic-slice_bitcast_fusion), channel_id=1, source_target_pairs={{0,32},{32,0},{1,33},{33,1},{2,34},{34,2},{3,35},{35,3},{4,36},{36... | collective-permute-start | bytes 1179656 | tf_op jit(solution)/shard_map/ppermute | solution.py:37
  38.2 16.7 %copy-start.2 = (bf16[2,384,512]{2,1,0:T(8,128)(2,1)S(1)}, bf16[2,384,512]{2,1,0:T(8,128)(2,1)}, u32[]{:S(2)}) copy-start(bf16[2,384,512]{2,1,0:T(8,128)(2,1)} %gw_ref.1) | copy-start | bytes 2359300
  38.2 16.7 %copy-start.3 = (bf16[2,384,512]{2,1,0:T(8,128)(2,1)S(1)}, bf16[2,384,512]{2,1,0:T(8,128)(2,1)}, u32[]{:S(2)}) copy-start(bf16[2,384,512]{2,1,0:T(8,128)(2,1)} %uw_ref.1) | copy-start | bytes 2359300

commit v6 on v5

--- a/solution.py
+++ b/solution.py
@@ -59,8 +59,8 @@
 
 def gate_up_kernel(core_ref, os_ref, rs_ref, x_ref, gw_ref, uw_ref, rw_ref, o_ref):
     core = core_ref[0]
-    near, _, _, depth = x_ref.shape
-    units = gw_ref.shape[2]
+    near = x_ref.shape[0]
+    depth, units = gw_ref.shape[1:]
     ks, ns = depth // SB, units // SB
     chunk = 2 * SB
     per = o_ref.shape[0] // near
@@ -73,7 +73,7 @@
                 for part, scale_ref in ((core, os_ref), (1 - core, rs_ref)):
                     for k in range(ks):
                         cut = slice(k * SB, (k + 1) * SB)
-                        rows = x_ref[i, part, :, cut]
+                        rows = x_ref[i, :, pl.ds(pl.multiple_of(part * depth + k * SB, SB), SB)]
                         if scale_ref is os_ref:
                             weight = own_weight[0, cut, columns]
                         else:
@@ -98,8 +98,8 @@
 
 
 def gate_up(core_index, portion, gate_weight, up_weight, other, own_scales, other_scales):
-    near, _, near_rows, depth = portion.shape
-    units = gate_weight.shape[2]
+    near, near_rows, _ = portion.shape
+    depth, units = gate_weight.shape[1:]
     out = (GROUP, near * near_rows // GROUP, 2 * units)
     smem = pl.BlockSpec(memory_space=pltpu.SMEM)
     return pl.pallas_call(
@@ -130,8 +130,8 @@
 
 def down_kernel(core_ref, os_ref, rs_ref, h_ref, dw_ref, rw_ref, o_ref):
     core = core_ref[0]
-    near, _, rows, width = o_ref.shape
-    depth = h_ref.shape[2]
+    near, rows, _ = o_ref.shape
+    depth, width = rw_ref.shape
     ks, ns = depth // SB, width // SB
     start = rs_ref.shape[1] - ks * ns
     per = h_ref.shape[0] // near
@@ -145,14 +145,14 @@
                 row = scale_row(lambda c: scale_ref[0, start + k * ns + c], range(ns))
                 product = jnp.dot(hidden, weight, preferred_element_type=F32) * row
                 total = product if total is None else total + product
-            o_ref[i, part] = total.astype(o_ref.dtype)
+            o_ref[i, :, pl.ds(pl.multiple_of(part * width, SB), width)] = total.astype(o_ref.dtype)
 
 
 def down_project(core_index, hidden, down_weight, other, own_scales, other_scales):
     _, some_rows, depth = hidden.shape
     width = down_weight.shape[2]
     rows = GROUP * some_rows
-    out = (NEAR, 2, rows // NEAR, width)
+    out = (NEAR, rows // NEAR, 2 * width)
     smem = pl.BlockSpec(memory_space=pltpu.SMEM)
     return pl.pallas_call(
         down_kernel,
@@ -191,16 +191,23 @@
     down_scale,
 ):
     core = lax.axis_index("core")
+    zero = core == 0
     width = tokens.shape[1]
     hidden_width = gate_weight.shape[2]
     near_rows = ZH * CAP
+    other_tokens = swap(tokens)
     onehot, combine_weights = dispatch(route_ids, route_gates)
+    own = jnp.where(zero, onehot[:, 0], onehot[:, 1]).astype(BF16)
+    both = [jnp.where(zero, tokens, other_tokens), jnp.where(zero, other_tokens, tokens)]
     slot_rows = jnp.einsum(
-        "tec,td->ecd", onehot.astype(BF16), tokens, preferred_element_type=F32
+        "tc,td->cd", own, jnp.concatenate(both, axis=1), preferred_element_type=F32
     ).astype(BF16)
-    packed = slot_rows.reshape(8, -1)
-    far = gather(packed, "zh", ZH).reshape(ZH, 2, CAP, width)
-    far = far.transpose(1, 0, 2, 3).reshape(2, near_rows, width)
+    slot_rows, gate_weight, up_weight, down_weight, gate_scale, up_scale, down_scale = (
+        lax.optimization_barrier(
+            (slot_rows, gate_weight, up_weight, down_weight, gate_scale, up_scale, down_scale)
+        )
+    )
+    far = gather(slot_rows.reshape(8, -1), "zh", ZH).reshape(near_rows, 2 * width)
 
     other = 1 - core
     core_index = jnp.reshape(core, (1,)).astype(jnp.int32)
@@ -210,19 +217,32 @@
     other_gate_up = swap(jnp.concatenate([pick(gate_weight, other), pick(up_weight, other)], axis=0))
     other_down = swap(pick(down_weight, other))
     combine = onehot.astype(F32) * combine_weights[:, :, None]
+    own_combine = jnp.where(zero, combine[:, 0], combine[:, 1])
+    other_combine = jnp.where(zero, combine[:, 1], combine[:, 0])
     (
         far,
+        zero,
         core_index,
         own_scales,
         other_scales,
         other_gate_up,
         other_down,
-        combine,
+        own_combine,
+        other_combine,
     ) = lax.optimization_barrier(
-        (far, core_index, own_scales, other_scales, other_gate_up, other_down, combine)
-    )
-    portion = jnp.broadcast_to(far[None], (NEAR,) + far.shape).reshape(2 * NEAR, near_rows, width)
-    portion = trade(portion, ("zl", "xl", "core")).reshape(NEAR, 2, near_rows, width)
+        (
+            far,
+            zero,
+            core_index,
+            own_scales,
+            other_scales,
+            other_gate_up,
+            other_down,
+            own_combine,
+            other_combine,
+        )
+    )
+    portion = gather(far, ("zl", "xl"), NEAR)
 
     partial_sums = gate_up(
         core_index, portion, gate_weight, up_weight, other_gate_up, own_scales, other_scales
@@ -232,13 +252,14 @@
     hidden = (jax.nn.silu(summed[:, :hidden_width]) * summed[:, hidden_width:]).astype(BF16)
     hidden = gather(hidden, ("y", "xh"), GROUP)
     down = down_project(core_index, hidden, down_weight, other_down, own_scales, other_scales)
-    down = trade(down.reshape(2 * NEAR, near_rows, width), ("zl", "xl", "core"))
-    down = jnp.sum(down.reshape(NEAR, 2, near_rows, width).astype(F32), axis=0).astype(BF16)
-    down = down.reshape(2, ZH, CAP, width).transpose(1, 0, 2, 3).reshape(ZH, 8, -1)
-    down = trade(down, "zh")
-    expert_out = jnp.sum(down.astype(F32), axis=0).reshape(2, CAP, width)
-
-    mixed = jnp.einsum("tec,ecd->td", combine, expert_out, precision=lax.Precision.HIGHEST)
+    down = trade(down, ("zl", "xl"))
+    down = jnp.sum(down.astype(F32), axis=0).astype(BF16)
+    down = trade(down.reshape(ZH, 8, -1), "zh")
+    out = jnp.sum(down.astype(F32), axis=0).reshape(CAP, 2 * width)
+    first, second = out[:, :width], out[:, width:]
+    given = swap(jnp.where(zero, second, first))
+    mixed = jnp.dot(own_combine, jnp.where(zero, first, second), precision=lax.Precision.HIGHEST)
+    mixed = mixed + jnp.dot(other_combine, given, precision=lax.Precision.HIGHEST)
     return mixed.astype(BF16)
 
 

time: 143 us -> 142 us (level)
  the two profiles are of different devices: /device:TPU:2 before, /device:TPU:1 now
where the time goes in v6:
time: 142 us; the launch traced here: 141 us
  blocking collectives  82.5 us (58%)
  starting transfers between devices  33.4 us (24%)
  waiting for transfers between devices  10.8 us (8%)
  Pallas kernels  4.51 us (3%)
  other arithmetic  4.26 us (3%)
  local copies, waits for them, and re-layouts  4.17 us (3%)
    all_to_all x5, blocking collectives, trade(): return lax.all_to_all(value, axes, 0, 0, tiled=True)  82.5 us
    ppermute x5, starting transfers between devices, swap(): return lax.ppermute(value, 'core', [(0, 1), (1, 0)])  24 us
    all_to_all x1, waiting for transfers between devices, trade(): return lax.all_to_all(value, axes, 0, 0, tiled=True)  9.95 us
    all_to_all x1, starting transfers between devices, trade(): return lax.all_to_all(value, axes, 0, 0, tiled=True)  9.44 us
  transfers between devices with their start and end apart: 6, of which 2 were waited for; matrix products, arithmetic and copies ran while one was open for 4% of the time, Pallas kernels for 0%

profile of v6, /device:TPU:1, one launch (start us, length us, event | category | flops | bytes accessed | tf_op | source)
XLA Modules:
  0.0 141.3 jit_solution(17166320720960790473)
XLA Ops:
  0.0 8.9 %collective-permute-start = (bf16[64,384]{1,0:T(8,128)(2,1)}, bf16[64,384]{1,0:T(8,128)(2,1)S(1)}, u32[]{:S(2)}, u32[]{:S(2)}) collective-permute-start(bf16[64,384]{1,0:T(8,128)(2,1)} %param.9), channel_id=1, source_target_pairs={{0,32},{32,0},{1,33},{33,1},{2,34},{34,2},{3,35},{35,3},{4,36},{36... | collective-permute-start | bytes 147464 | tf_op jit(solution)/shard_map/ppermute | solution.py:37
  8.9 0.7 fusion.14
  9.6 0.1 copy.20
  9.7 0.1 reduce_window_sum.11
  9.9 0.7 select_reduce_fusion
  10.6 0.8 broadcast_select_fusion.1
  11.5 0.1 convolution_convert_fusion
  11.6 0.7 broadcast_in_dim.21
  12.3 9.4 %all-to-all-start = ((bf16[8,8,1920]{2,1,0:T(8,128)(2,1)}), bf16[8,8,1920]{2,1,0:T(8,128)(2,1)S(1)}, u32[]{:S(2)}, u32[]{:S(2)}) async-start(bf16[8,8,1920]{2,1,0:T(8,128)(2,1)} %broadcast_in_dim.21), calls=%async_computation | async-start | bytes 491520 | tf_op jit(solution)/shard_map/all_to_all | solution.py:41
  21.8 1.1 dynamic-slice_bitcast_fusion.1
  23.0 0.9 pad_maximum_fusion
  23.9 2.2 %collective-permute-start.2 = (bf16[768,512]{1,0:T(8,128)(2,1)}, bf16[768,512]{1,0:T(8,128)(2,1)S(1)}, u32[]{:S(2)}, u32[]{:S(2)}) collective-permute-start(bf16[768,512]{1,0:T(8,128)(2,1)} %pad_maximum_fusion), channel_id=1, source_target_pairs={{0,32},{32,0},{1,33},{33,1},{2,34},{34,2},{3,35},{35,3},{4,36},{36... | collective-permute-start | bytes 2359304 | tf_op jit(solution)/shard_map/ppermute | solution.py:37
  26.1 0.8 dynamic-slice_bitcast_fusion
  26.9 2.1 %collective-permute-start.3 = (bf16[512,384]{1,0:T(8,128)(2,1)}, bf16[512,384]{1,0:T(8,128)(2,1)S(1)}, u32[]{:S(2)}, u32[]{:S(2)}) collective-permute-start(bf16[512,384]{1,0:T(8,128)(2,1)} %dynamic-slice_bitcast_fusion), channel_id=1, source_target_pairs={{0,32},{32,0},{1,33},{33,1},{2,34},{34,2},{3,35},{35,3},{4,36},{36... | collective-permute-start | bytes 1179656 | tf_op jit(solution)/shard_map/ppermute | solution.py:37
  29.9 2.2 %collective-permute-start.1 = (f32[1,36]{1,0:T(1,128)S(1)}, f32[1,36]{1,0:T(1,128)S(1)}, u32[]{:S(2)}, u32[]{:S(2)}) collective-permute-start(f32[1,36]{1,0:T(1,128)S(1)} %pad_maximum_fusion.2), channel_id=1, source_target_pairs={{0,32},{32,0},{1,33},{33,1},{2,34},{34,2},{3,35},{35,3},{4,36},{36... | collective-permute-start | bytes 440 | tf_op jit(solution)/shard_map/ppermute | solution.py:37
  32.2 9.9 %all-to-all-done = bf16[8,8,1920]{2,1,0:T(8,128)(2,1)S(1)} async-done(((bf16[8,8,1920]{2,1,0:T(8,128)(2,1)}), bf16[8,8,1920]{2,1,0:T(8,128)(2,1)S(1)}, u32[]{:S(2)}, u32[]{:S(2)}) %all-to-all-start) | async-done | bytes 245792 | tf_op jit(solution)/shard_map/all_to_all | solution.py:41
  42.1 0.2 reshape.58
  42.5 14.5 %all_to_all.30.x_ref = bf16[4,160,768]{2,1,0:T(8,128)(2,1)S(1)} all-to-all(bf16[4,160,768]{2,1,0:T(8,128)(2,1)S(1)} %broadcast_in_dim.24), channel_id=1, replica_groups=mesh['y'=4,'xh'=2,'core'=2,'zh'=8,'zl'=2,'xl'=2] {'zl','xl'}, dimensions={0} | all-to-all | bytes 1966080 | tf_op jit(solution)/shard_map/all_to_all | solution.py:41
  57.0 2.8 %gate_up.1 = f32[8,80,1024]{2,1,0:T(8,128)S(1)} custom-call(s32[1]{0:T(128)} %bitcast.1.core_ref, f32[1,36]{1,0:T(1,128)S(1)} %pad_maximum_fusion.1.os_ref, f32[1,36]{1,0:T(1,128)S(1)} %collective-permute-done.1.rs_ref, bf16[4,160,768]{2,1,0:T(8,128)(2,1)S(1)} %all_to_all.30.x_ref, bf16[2,384,512]{2,1,0:T(8,128)(2,1)S(1)} %copy-done.1, ...), custom_call_target="tpu_custom_call" | custom-call | flops 1006632960 | bytes 5177344 | tf_op jit(solution)/shard_map/gate_up/pallas_call | solution.py:105
  59.8 0.2 convert_element_type.31
  60.0 23.6 %all_to_all.31 = f16[8,80,1024]{2,1,0:T(8,128)(2,1)S(1)} all-to-all(f16[8,80,1024]{2,1,0:T(8,128)(2,1)S(1)} %convert_element_type.31), channel_id=1, replica_groups=mesh['y'=4,'xh'=2,'core'=2,'zh'=8,'zl'=2,'xl'=2] {'y','xh'}, dimensions={0} | all-to-all | bytes 2621440 | tf_op jit(solution)/shard_map/all_to_all | solution.py:41
  83.6 0.3 convert_reduce_fusion
  84.0 12.5 %all_to_all.32.h_ref = bf16[8,80,512]{2,1,0:T(8,128)(2,1)S(1)} all-to-all(bf16[8,80,512]{2,1,0:T(8,128)(2,1)S(1)} %broadcast_in_dim.25), channel_id=1, replica_groups=mesh['y'=4,'xh'=2,'core'=2,'zh'=8,'zl'=2,'xl'=2] {'y','xh'}, dimensions={0} | all-to-all | bytes 1310720 | tf_op jit(solution)/shard_map/all_to_all | solution.py:41
  96.6 1.8 %down_project.1 = bf16[4,160,768]{2,1,0:T(8,128)(2,1)S(1)} custom-call(s32[1]{0:T(128)} %bitcast.1.core_ref, f32[1,36]{1,0:T(1,128)S(1)} %pad_maximum_fusion.1.os_ref, f32[1,36]{1,0:T(1,128)S(1)} %collective-permute-done.1.rs_ref, bf16[8,80,512]{2,1,0:T(8,128)(2,1)S(1)} %all_to_all.32.h_ref, bf16[2,512,384]{2,1,0:T(8,128)(2,1)S(1)} %copy-done, ...), custom_call_target="tpu_custom_call" | custom-call | flops 503316480 | bytes 2424832 | tf_op jit(solution)/shard_map/down_project/pallas_call | solution.py:157
  98.4 12.5 %all_to_all.33 = bf16[4,160,768]{2,1,0:T(8,128)(2,1)S(1)} all-to-all(bf16[4,160,768]{2,1,0:T(8,128)(2,1)S(1)} %down_project.1), channel_id=1, replica_groups=mesh['y'=4,'xh'=2,'core'=2,'zh'=8,'zl'=2,'xl'=2] {'zl','xl'}, dimensions={0} | all-to-all | bytes 1966080 | tf_op jit(solution)/shard_map/all_to_all | solution.py:41
  110.8 0.1 reduce_sum.41
  111.0 0.2 reshape.66
  111.2 19.4 %all_to_all.34 = bf16[8,8,1920]{2,1,0:T(8,128)(2,1)S(1)} all-to-all(bf16[8,8,1920]{2,1,0:T(8,128)(2,1)S(1)} %reshape.66), channel_id=1, replica_groups=mesh['y'=4,'xh'=2,'core'=2,'zh'=8,'zl'=2,'xl'=2] {'zh'}, dimensions={0} | all-to-all | bytes 491520 | tf_op jit(solution)/shard_map/all_to_all | solution.py:41
  130.7 8.6 %collective-permute-start.4 = (f32[20,384]{1,0:T(8,128)S(1)}, f32[20,384]{1,0:T(8,128)S(1)}, u32[]{:S(2)}, u32[]{:S(2)}) collective-permute-start(f32[20,384]{1,0:T(8,128)S(1)} %slice_select_fusion), channel_id=1, source_target_pairs={{0,32},{32,0},{1,33},{33,1},{2,34},{34,2},{3,35},{35,3},{4,36},{36... | collective-permute-start | bytes 92168 | tf_op jit(solution)/shard_map/ppermute | solution.py:37
  139.3 0.8 collective-permute-done.4
  140.1 0.3 fusion.20
  140.4 0.9 fusion
  (42 shorter events, 1.3 us)
Async XLA Ops:
  0.0 21.8 %copy-start.1 = (bf16[2,384,512]{2,1,0:T(8,128)(2,1)S(1)}, bf16[2,384,512]{2,1,0:T(8,128)(2,1)}, u32[]{:S(2)}) copy-start(bf16[2,384,512]{2,1,0:T(8,128)(2,1)} %gw_ref) | copy-start | bytes 2359300
  0.0 10.6 %collective-permute-start = (bf16[64,384]{1,0:T(8,128)(2,1)}, bf16[64,384]{1,0:T(8,128)(2,1)S(1)}, u32[]{:S(2)}, u32[]{:S(2)}) collective-permute-start(bf16[64,384]{1,0:T(8,128)(2,1)} %param.9), channel_id=1, source_target_pairs={{0,32},{32,0},{1,33},{33,1},{2,34},{34,2},{3,35},{35,3},{4,36},{36... | collective-permute-start | bytes 147464 | tf_op jit(solution)/shard_map/ppermute | solution.py:37
  12.3 29.8 %all-to-all-start = ((bf16[8,8,1920]{2,1,0:T(8,128)(2,1)}), bf16[8,8,1920]{2,1,0:T(8,128)(2,1)S(1)}, u32[]{:S(2)}, u32[]{:S(2)}) async-start(bf16[8,8,1920]{2,1,0:T(8,128)(2,1)} %broadcast_in_dim.21), calls=%async_computation | async-start | bytes 491520 | tf_op jit(solution)/shard_map/all_to_all | solution.py:41
  21.8 4.3 %copy-start = (bf16[2,512,384]{2,1,0:T(8,128)(2,1)S(1)}, bf16[2,512,384]{2,1,0:T(8,128)(2,1)}, u32[]{:S(2)}) copy-start(bf16[2,512,384]{2,1,0:T(8,128)(2,1)} %dw_ref) | copy-start | bytes 2359300
  22.9 6.1 %copy-start.3 = (f32[2,4,3]{1,0,2:T(2,128)S(1)}, f32[2,4,3]{1,0,2:T(2,128)}, u32[]{:S(2)}) copy-start(f32[2,4,3]{1,0,2:T(2,128)} %param.17) | copy-start | bytes 292
  22.9 6.5 %copy-start.4 = (f32[2,3,4]{2,0,1:T(2,128)S(1)}, f32[2,3,4]{2,0,1:T(2,128)}, u32[]{:S(2)}) copy-start(f32[2,3,4]{2,0,1:T(2,128)} %param.14) | copy-start | bytes 292
  23.0 6.5 %copy-start.5 = (f32[2,3,4]{2,0,1:T(2,128)S(1)}, f32[2,3,4]{2,0,1:T(2,128)}, u32[]{:S(2)}) copy-start(f32[2,3,4]{2,0,1:T(2,128)} %param.15) | copy-start | bytes 292
  23.9 18.5 %collective-permute-start.2 = (bf16[768,512]{1,0:T(8,128)(2,1)}, bf16[768,512]{1,0:T(8,128)(2,1)S(1)}, u32[]{:S(2)}, u32[]{:S(2)}) collective-permute-start(bf16[768,512]{1,0:T(8,128)(2,1)} %pad_maximum_fusion), channel_id=1, source_target_pairs={{0,32},{32,0},{1,33},{33,1},{2,34},{34,2},{3,35},{35,3},{4,36},{36... | collective-permute-start | bytes 2359304 | tf_op jit(solution)/shard_map/ppermute | solution.py:37
  26.9 15.4 %collective-permute-start.3 = (bf16[512,384]{1,0:T(8,128)(2,1)}, bf16[512,384]{1,0:T(8,128)(2,1)S(1)}, u32[]{:S(2)}, u32[]{:S(2)}) collective-permute-start(bf16[512,384]{1,0:T(8,128)(2,1)} %dynamic-slice_bitcast_fusion), channel_id=1, source_target_pairs={{0,32},{32,0},{1,33},{33,1},{2,34},{34,2},{3,35},{35,3},{4,36},{36... | collective-permute-start | bytes 1179656 | tf_op jit(solution)/shard_map/ppermute | solution.py:37
  29.9 12.4 %collective-permute-start.1 = (f32[1,36]{1,0:T(1,128)S(1)}, f32[1,36]{1,0:T(1,128)S(1)}, u32[]{:S(2)}, u32[]{:S(2)}) collective-permute-start(f32[1,36]{1,0:T(1,128)S(1)} %pad_maximum_fusion.2), channel_id=1, source_target_pairs={{0,32},{32,0},{1,33},{33,1},{2,34},{34,2},{3,35},{35,3},{4,36},{36... | collective-permute-start | bytes 440 | tf_op jit(solution)/shard_map/ppermute | solution.py:37
  42.4 14.6 %copy-start.2 = (bf16[2,384,512]{2,1,0:T(8,128)(2,1)S(1)}, bf16[2,384,512]{2,1,0:T(8,128)(2,1)}, u32[]{:S(2)}) copy-start(bf16[2,384,512]{2,1,0:T(8,128)(2,1)} %uw_ref) | copy-start | bytes 2359300
  130.7 9.4 %collective-permute-start.4 = (f32[20,384]{1,0:T(8,128)S(1)}, f32[20,384]{1,0:T(8,128)S(1)}, u32[]{:S(2)}, u32[]{:S(2)}) collective-permute-start(f32[20,384]{1,0:T(8,128)S(1)} %slice_select_fusion), channel_id=1, source_target_pairs={{0,32},{32,0},{1,33},{33,1},{2,34},{34,2},{3,35},{35,3},{4,36},{36... | collective-permute-start | bytes 92168 | tf_op jit(solution)/shard_map/ppermute | solution.py:37

commit v7 on v6

--- a/solution.py
+++ b/solution.py
@@ -19,18 +19,26 @@
 SHIFT = 64.0
 
 
-def dispatch(route_ids, route_gates):
+def matching(route_ids):
     expert_ids = jnp.arange(EXPW, dtype=jnp.int32)
-    matches = route_ids[:, :, None] == expert_ids[None, None, :]
-    chosen = jnp.any(matches, axis=1)
-    combine_weights = jnp.sum(
-        jnp.where(matches, route_gates[:, :, None], jnp.zeros((), route_gates.dtype)), axis=1
-    )
+    return route_ids[:, :, None] == expert_ids[None, None, :]
+
+
+def dispatch(route_ids):
+    chosen = jnp.any(matching(route_ids), axis=1)
     slot_index = jnp.cumsum(chosen.astype(jnp.int32), axis=0) - 1
-    onehot = chosen[:, :, None] & (
+    return chosen[:, :, None] & (
         slot_index[:, :, None] == jnp.arange(CAP, dtype=jnp.int32)[None, None, :]
     )
-    return (onehot, combine_weights)
+
+
+def combine_weights(route_ids, route_gates):
+    return jnp.sum(
+        jnp.where(
+            matching(route_ids), route_gates[:, :, None], jnp.zeros((), route_gates.dtype)
+        ),
+        axis=1,
+    )
 
 
 def swap(value):
@@ -58,7 +66,6 @@
 
 
 def gate_up_kernel(core_ref, os_ref, rs_ref, x_ref, gw_ref, uw_ref, rw_ref, o_ref):
-    core = core_ref[0]
     near = x_ref.shape[0]
     depth, units = gw_ref.shape[1:]
     ks, ns = depth // SB, units // SB
@@ -70,10 +77,11 @@
                 columns = slice(n * chunk, (n + 1) * chunk)
                 blocks = (2 * n, 2 * n + 1)
                 total = None
-                for part, scale_ref in ((core, os_ref), (1 - core, rs_ref)):
+                for part, scale_ref in enumerate((os_ref, rs_ref)):
                     for k in range(ks):
                         cut = slice(k * SB, (k + 1) * SB)
-                        rows = x_ref[i, :, pl.ds(pl.multiple_of(part * depth + k * SB, SB), SB)]
+                        start = part * depth + k * SB
+                        rows = x_ref[i, :, start : start + SB]
                         if scale_ref is os_ref:
                             weight = own_weight[0, cut, columns]
                         else:
@@ -129,14 +137,13 @@
 
 
 def down_kernel(core_ref, os_ref, rs_ref, h_ref, dw_ref, rw_ref, o_ref):
-    core = core_ref[0]
     near, rows, _ = o_ref.shape
     depth, width = rw_ref.shape
     ks, ns = depth // SB, width // SB
     start = rs_ref.shape[1] - ks * ns
     per = h_ref.shape[0] // near
     for i in range(near):
-        for part, scale_ref in ((core, os_ref), (1 - core, rs_ref)):
+        for part, scale_ref in enumerate((os_ref, rs_ref)):
             total = None
             for k in range(ks):
                 cut = slice(k * SB, (k + 1) * SB)
@@ -145,7 +152,7 @@
                 row = scale_row(lambda c: scale_ref[0, start + k * ns + c], range(ns))
                 product = jnp.dot(hidden, weight, preferred_element_type=F32) * row
                 total = product if total is None else total + product
-            o_ref[i, :, pl.ds(pl.multiple_of(part * width, SB), width)] = total.astype(o_ref.dtype)
+            o_ref[i, :, part * width : (part + 1) * width] = total.astype(o_ref.dtype)
 
 
 def down_project(core_index, hidden, down_weight, other, own_scales, other_scales):
@@ -196,32 +203,56 @@
     hidden_width = gate_weight.shape[2]
     near_rows = ZH * CAP
     other_tokens = swap(tokens)
-    onehot, combine_weights = dispatch(route_ids, route_gates)
+    onehot = dispatch(route_ids)
     own = jnp.where(zero, onehot[:, 0], onehot[:, 1]).astype(BF16)
-    both = [jnp.where(zero, tokens, other_tokens), jnp.where(zero, other_tokens, tokens)]
-    slot_rows = jnp.einsum(
-        "tc,td->cd", own, jnp.concatenate(both, axis=1), preferred_element_type=F32
-    ).astype(BF16)
-    slot_rows, gate_weight, up_weight, down_weight, gate_scale, up_scale, down_scale = (
-        lax.optimization_barrier(
-            (slot_rows, gate_weight, up_weight, down_weight, gate_scale, up_scale, down_scale)
+    slot_rows = [
+        jnp.einsum("tc,td->cd", own, part, preferred_element_type=F32).astype(BF16)
+        for part in (tokens, other_tokens)
+    ]
+    slot_rows = jnp.concatenate(slot_rows, axis=1).reshape(8, -1)
+    (
+        slot_rows,
+        onehot,
+        route_ids,
+        route_gates,
+        gate_weight,
+        up_weight,
+        down_weight,
+        gate_scale,
+        up_scale,
+        down_scale,
+    ) = lax.optimization_barrier(
+        (
+            slot_rows,
+            onehot,
+            route_ids,
+            route_gates,
+            gate_weight,
+            up_weight,
+            down_weight,
+            gate_scale,
+            up_scale,
+            down_scale,
         )
     )
-    far = gather(slot_rows.reshape(8, -1), "zh", ZH).reshape(near_rows, 2 * width)
+    far = gather(slot_rows, "zh", ZH).reshape(near_rows, 2 * width)
 
     other = 1 - core
     core_index = jnp.reshape(core, (1,)).astype(jnp.int32)
+    sent = jnp.concatenate([pick(gate_weight, other), pick(up_weight, other)], axis=0)
+    sent_down, gate_scale, up_scale, down_scale = lax.optimization_barrier(
+        (pick(down_weight, other), gate_scale, up_scale, down_scale)
+    )
     scales = (gate_scale, up_scale, down_scale)
     own_scales = flat_scales(scales, core)
     other_scales = swap(flat_scales(scales, other))
-    other_gate_up = swap(jnp.concatenate([pick(gate_weight, other), pick(up_weight, other)], axis=0))
-    other_down = swap(pick(down_weight, other))
-    combine = onehot.astype(F32) * combine_weights[:, :, None]
+    other_gate_up = swap(sent)
+    other_down = swap(sent_down)
+    combine = onehot.astype(F32) * combine_weights(route_ids, route_gates)[:, :, None]
     own_combine = jnp.where(zero, combine[:, 0], combine[:, 1])
     other_combine = jnp.where(zero, combine[:, 1], combine[:, 0])
     (
         far,
-        zero,
         core_index,
         own_scales,
         other_scales,
@@ -232,7 +263,6 @@
     ) = lax.optimization_barrier(
         (
             far,
-            zero,
             core_index,
             own_scales,
             other_scales,
@@ -256,9 +286,8 @@
     down = jnp.sum(down.astype(F32), axis=0).astype(BF16)
     down = trade(down.reshape(ZH, 8, -1), "zh")
     out = jnp.sum(down.astype(F32), axis=0).reshape(CAP, 2 * width)
-    first, second = out[:, :width], out[:, width:]
-    given = swap(jnp.where(zero, second, first))
-    mixed = jnp.dot(own_combine, jnp.where(zero, first, second), precision=lax.Precision.HIGHEST)
+    given = swap(out[:, width:])
+    mixed = jnp.dot(own_combine, out[:, :width], precision=lax.Precision.HIGHEST)
     mixed = mixed + jnp.dot(other_combine, given, precision=lax.Precision.HIGHEST)
     return mixed.astype(BF16)
 

time: 142 us -> 141 us (level)
  other arithmetic: 4.26 us -> 2.75 us
where the time goes in v7:
time: 141 us
  blocking collectives  82.5 us (59%)
  starting transfers between devices  33.4 us (24%)
  waiting for transfers between devices  10.9 us (8%)
  Pallas kernels  4.5 us (3%)
  local copies, waits for them, and re-layouts  4.09 us (3%)
  other arithmetic  2.75 us (2%)
  matrix products  2.26 us (2%)
    all_to_all x5, blocking collectives, trade(): return lax.all_to_all(value, axes, 0, 0, tiled=True)  82.5 us
    ppermute x5, starting transfers between devices, swap(): return lax.ppermute(value, 'core', [(0, 1), (1, 0)])  24 us
    all_to_all x1, waiting for transfers between devices, trade(): return lax.all_to_all(value, axes, 0, 0, tiled=True)  10.1 us
    all_to_all x1, starting transfers between devices, trade(): return lax.all_to_all(value, axes, 0, 0, tiled=True)  9.45 us
  transfers between devices with their start and end apart: 6, of which 2 were waited for; matrix products, arithmetic and copies ran while one was open for 4% of the time, Pallas kernels for 0%

profile of v7, /device:TPU:1, one launch (start us, length us, event | category | flops | bytes accessed | tf_op | source)
XLA Modules:
  0.0 140.8 jit_solution(13688186925564973559)
XLA Ops:
  0.0 8.9 %collective-permute-start = (bf16[64,384]{1,0:T(8,128)(2,1)}, bf16[64,384]{1,0:T(8,128)(2,1)S(1)}, u32[]{:S(2)}, u32[]{:S(2)}) collective-permute-start(bf16[64,384]{1,0:T(8,128)(2,1)} %param.9), channel_id=1, source_target_pairs={{0,32},{32,0},{1,33},{33,1},{2,34},{34,2},{3,35},{35,3},{4,36},{36... | collective-permute-start | bytes 147464 | tf_op jit(solution)/shard_map/ppermute | solution.py:45
  8.9 0.7 compare_reduce_fusion
  9.7 0.1 copy.22
  9.8 0.1 reduce_window_sum.11
  9.9 0.9 convolution_convert_fusion.1
  10.9 0.1 convolution_convert_fusion
  11.1 0.7 broadcast_in_dim.14
  11.8 9.5 %all-to-all-start = ((bf16[8,8,1920]{2,1,0:T(8,128)(2,1)}), bf16[8,8,1920]{2,1,0:T(8,128)(2,1)S(1)}, u32[]{:S(2)}, u32[]{:S(2)}) async-start(bf16[8,8,1920]{2,1,0:T(8,128)(2,1)} %broadcast_in_dim.14), calls=%async_computation | async-start | bytes 491520 | tf_op jit(solution)/shard_map/all_to_all | solution.py:49
  21.2 1.8 %dynamic-slice_bitcast_fusion.2 = bf16[512,384]{1,0:T(8,128)(2,1)} fusion(bf16[2,512,384]{2,1,0:T(8,128)(2,1)} %dw_ref, s32[]{:T(128)S(6)} %select_n.51), kind=kLoop, calls=%fused_computation.9 | loop fusion | bytes 786436 | tf_op jit(solution)/shard_map/jit(dynamic_index_in_dim)/squeeze | solution.py:57
  23.0 0.1 copy.25
  23.5 0.9 pad_maximum_fusion
  24.4 2.2 %collective-permute-start.2 = (bf16[768,512]{1,0:T(8,128)(2,1)}, bf16[768,512]{1,0:T(8,128)(2,1)S(1)}, u32[]{:S(2)}, u32[]{:S(2)}) collective-permute-start(bf16[768,512]{1,0:T(8,128)(2,1)} %pad_maximum_fusion), channel_id=1, source_target_pairs={{0,32},{32,0},{1,33},{33,1},{2,34},{34,2},{3,35},{35,3},{4,36},{36... | collective-permute-start | bytes 2359304 | tf_op jit(solution)/shard_map/ppermute | solution.py:45
  26.7 2.1 %collective-permute-start.1 = (f32[1,36]{1,0:T(1,128)S(1)}, f32[1,36]{1,0:T(1,128)S(1)}, u32[]{:S(2)}, u32[]{:S(2)}) collective-permute-start(f32[1,36]{1,0:T(1,128)S(1)} %pad_maximum_fusion.3), channel_id=1, source_target_pairs={{0,32},{32,0},{1,33},{33,1},{2,34},{34,2},{3,35},{35,3},{4,36},{36... | collective-permute-start | bytes 440 | tf_op jit(solution)/shard_map/ppermute | solution.py:45
  28.8 2.2 %collective-permute-start.3 = (bf16[512,384]{1,0:T(8,128)(2,1)}, bf16[512,384]{1,0:T(8,128)(2,1)S(1)}, u32[]{:S(2)}, u32[]{:S(2)}) collective-permute-start(bf16[512,384]{1,0:T(8,128)(2,1)} %dynamic-slice_bitcast_fusion.2), channel_id=1, source_target_pairs={{0,32},{32,0},{1,33},{33,1},{2,34},{34,2},{3,35},{35,3},{4,36},{36... | collective-permute-start | bytes 1179656 | tf_op jit(solution)/shard_map/ppermute | solution.py:45
  31.1 0.1 copy.24
  31.5 10.1 %all-to-all-done = bf16[8,8,1920]{2,1,0:T(8,128)(2,1)S(1)} async-done(((bf16[8,8,1920]{2,1,0:T(8,128)(2,1)}), bf16[8,8,1920]{2,1,0:T(8,128)(2,1)S(1)}, u32[]{:S(2)}, u32[]{:S(2)}) %all-to-all-start) | async-done | bytes 245792 | tf_op jit(solution)/shard_map/all_to_all | solution.py:49
  41.6 0.2 reshape.63
  41.9 14.4 %all_to_all.30.x_ref = bf16[4,160,768]{2,1,0:T(8,128)(2,1)S(1)} all-to-all(bf16[4,160,768]{2,1,0:T(8,128)(2,1)S(1)} %broadcast_in_dim.21), channel_id=1, replica_groups=mesh['y'=4,'xh'=2,'core'=2,'zh'=8,'zl'=2,'xl'=2] {'zl','xl'}, dimensions={0} | all-to-all | bytes 1966080 | tf_op jit(solution)/shard_map/all_to_all | solution.py:49
  56.3 2.7 %gate_up.1 = f32[8,80,1024]{2,1,0:T(8,128)S(1)} custom-call(s32[1]{0:T(128)} %bitcast.1.core_ref, f32[1,36]{1,0:T(1,128)S(1)} %pad_maximum_fusion.2.os_ref, f32[1,36]{1,0:T(1,128)S(1)} %collective-permute-done.1.rs_ref, bf16[4,160,768]{2,1,0:T(8,128)(2,1)S(1)} %all_to_all.30.x_ref, bf16[2,384,512]{2,1,0:T(8,128)(2,1)S(1)} %copy-done.1, ...), custom_call_target="tpu_custom_call" | custom-call | flops 1006632960 | bytes 5177344 | tf_op jit(solution)/shard_map/gate_up/pallas_call | solution.py:113
  59.0 0.2 convert_element_type.35
  59.3 23.6 %all_to_all.31 = f16[8,80,1024]{2,1,0:T(8,128)(2,1)S(1)} all-to-all(f16[8,80,1024]{2,1,0:T(8,128)(2,1)S(1)} %convert_element_type.35), channel_id=1, replica_groups=mesh['y'=4,'xh'=2,'core'=2,'zh'=8,'zl'=2,'xl'=2] {'y','xh'}, dimensions={0} | all-to-all | bytes 2621440 | tf_op jit(solution)/shard_map/all_to_all | solution.py:49
  82.9 0.3 convert_reduce_fusion
  83.3 12.5 %all_to_all.32.h_ref = bf16[8,80,512]{2,1,0:T(8,128)(2,1)S(1)} all-to-all(bf16[8,80,512]{2,1,0:T(8,128)(2,1)S(1)} %broadcast_in_dim.22), channel_id=1, replica_groups=mesh['y'=4,'xh'=2,'core'=2,'zh'=8,'zl'=2,'xl'=2] {'y','xh'}, dimensions={0} | all-to-all | bytes 1310720 | tf_op jit(solution)/shard_map/all_to_all | solution.py:49
  95.8 1.8 %down_project.1 = bf16[4,160,768]{2,1,0:T(8,128)(2,1)S(1)} custom-call(s32[1]{0:T(128)} %bitcast.1.core_ref, f32[1,36]{1,0:T(1,128)S(1)} %pad_maximum_fusion.2.os_ref, f32[1,36]{1,0:T(1,128)S(1)} %collective-permute-done.1.rs_ref, bf16[8,80,512]{2,1,0:T(8,128)(2,1)S(1)} %all_to_all.32.h_ref, bf16[2,512,384]{2,1,0:T(8,128)(2,1)S(1)} %copy-done, ...), custom_call_target="tpu_custom_call" | custom-call | flops 503316480 | bytes 2424832 | tf_op jit(solution)/shard_map/down_project/pallas_call | solution.py:164
  97.6 12.7 %all_to_all.33 = bf16[4,160,768]{2,1,0:T(8,128)(2,1)S(1)} all-to-all(bf16[4,160,768]{2,1,0:T(8,128)(2,1)S(1)} %down_project.1), channel_id=1, replica_groups=mesh['y'=4,'xh'=2,'core'=2,'zh'=8,'zl'=2,'xl'=2] {'zl','xl'}, dimensions={0} | all-to-all | bytes 1966080 | tf_op jit(solution)/shard_map/all_to_all | solution.py:49
  110.2 0.1 reduce_sum.41
  110.4 0.2 reshape.71
  110.6 19.4 %all_to_all.34 = bf16[8,8,1920]{2,1,0:T(8,128)(2,1)S(1)} all-to-all(bf16[8,8,1920]{2,1,0:T(8,128)(2,1)S(1)} %reshape.71), channel_id=1, replica_groups=mesh['y'=4,'xh'=2,'core'=2,'zh'=8,'zl'=2,'xl'=2] {'zh'}, dimensions={0} | all-to-all | bytes 491520 | tf_op jit(solution)/shard_map/all_to_all | solution.py:49
  130.1 8.6 %collective-permute-start.4 = (f32[20,384]{1,0:T(8,128)S(1)}, f32[20,384]{1,0:T(8,128)S(1)}, u32[]{:S(2)}, u32[]{:S(2)}) collective-permute-start(f32[20,384]{1,0:T(8,128)S(1)} %slice.41), channel_id=1, source_target_pairs={{0,32},{32,0},{1,33},{33,1},{2,34},{34,2},{3,35},{35,3},{4,36},{36... | collective-permute-start | bytes 92168 | tf_op jit(solution)/shard_map/ppermute | solution.py:45
  138.7 0.8 collective-permute-done.4
  139.6 0.3 fusion.12
  139.9 0.9 fusion
  (47 shorter events, 1.2 us)
Async XLA Ops:
  0.0 23.0 %copy-start.3 = (f32[2,4,3]{1,0,2:T(2,128)S(1)}, f32[2,4,3]{1,0,2:T(2,128)}, u32[]{:S(2)}) copy-start(f32[2,4,3]{1,0,2:T(2,128)} %param.17) | copy-start | bytes 292
  0.0 23.2 %copy-start.5 = (f32[2,3,4]{2,0,1:T(2,128)S(1)}, f32[2,3,4]{2,0,1:T(2,128)}, u32[]{:S(2)}) copy-start(f32[2,3,4]{2,0,1:T(2,128)} %param.15) | copy-start | bytes 292
  0.0 23.2 %copy-start.4 = (f32[2,3,4]{2,0,1:T(2,128)S(1)}, f32[2,3,4]{2,0,1:T(2,128)}, u32[]{:S(2)}) copy-start(f32[2,3,4]{2,0,1:T(2,128)} %param.14) | copy-start | bytes 292
  0.0 23.4 %copy-start.2 = (bf16[2,384,512]{2,1,0:T(8,128)(2,1)S(1)}, bf16[2,384,512]{2,1,0:T(8,128)(2,1)}, u32[]{:S(2)}) copy-start(bf16[2,384,512]{2,1,0:T(8,128)(2,1)} %uw_ref) | copy-start | bytes 2359300
  0.0 23.4 %copy-start.1 = (bf16[2,384,512]{2,1,0:T(8,128)(2,1)S(1)}, bf16[2,384,512]{2,1,0:T(8,128)(2,1)}, u32[]{:S(2)}) copy-start(bf16[2,384,512]{2,1,0:T(8,128)(2,1)} %gw_ref) | copy-start | bytes 2359300
  0.0 10.8 %collective-permute-start = (bf16[64,384]{1,0:T(8,128)(2,1)}, bf16[64,384]{1,0:T(8,128)(2,1)S(1)}, u32[]{:S(2)}, u32[]{:S(2)}) collective-permute-start(bf16[64,384]{1,0:T(8,128)(2,1)} %param.9), channel_id=1, source_target_pairs={{0,32},{32,0},{1,33},{33,1},{2,34},{34,2},{3,35},{35,3},{4,36},{36... | collective-permute-start | bytes 147464 | tf_op jit(solution)/shard_map/ppermute | solution.py:45
  11.8 29.8 %all-to-all-start = ((bf16[8,8,1920]{2,1,0:T(8,128)(2,1)}), bf16[8,8,1920]{2,1,0:T(8,128)(2,1)S(1)}, u32[]{:S(2)}, u32[]{:S(2)}) async-start(bf16[8,8,1920]{2,1,0:T(8,128)(2,1)} %broadcast_in_dim.14), calls=%async_computation | async-start | bytes 491520 | tf_op jit(solution)/shard_map/all_to_all | solution.py:49
  23.4 7.6 %copy-start.6 = (s32[64,2]{0,1:T(2,128)S(1)}, s32[64,2]{0,1:T(2,128)}, u32[]{:S(2)}) copy-start(s32[64,2]{0,1:T(2,128)} %param.10) | copy-start | bytes 1540
  23.4 7.6 %copy-start.7 = (f32[64,2]{0,1:T(2,128)S(1)}, f32[64,2]{0,1:T(2,128)}, u32[]{:S(2)}) copy-start(f32[64,2]{0,1:T(2,128)} %param.11) | copy-start | bytes 1540
  24.4 17.4 %collective-permute-start.2 = (bf16[768,512]{1,0:T(8,128)(2,1)}, bf16[768,512]{1,0:T(8,128)(2,1)S(1)}, u32[]{:S(2)}, u32[]{:S(2)}) collective-permute-start(bf16[768,512]{1,0:T(8,128)(2,1)} %pad_maximum_fusion), channel_id=1, source_target_pairs={{0,32},{32,0},{1,33},{33,1},{2,34},{34,2},{3,35},{35,3},{4,36},{36... | collective-permute-start | bytes 2359304 | tf_op jit(solution)/shard_map/ppermute | solution.py:45
  26.7 15.1 %collective-permute-start.1 = (f32[1,36]{1,0:T(1,128)S(1)}, f32[1,36]{1,0:T(1,128)S(1)}, u32[]{:S(2)}, u32[]{:S(2)}) collective-permute-start(f32[1,36]{1,0:T(1,128)S(1)} %pad_maximum_fusion.3), channel_id=1, source_target_pairs={{0,32},{32,0},{1,33},{33,1},{2,34},{34,2},{3,35},{35,3},{4,36},{36... | collective-permute-start | bytes 440 | tf_op jit(solution)/shard_map/ppermute | solution.py:45
  28.8 13.0 %collective-permute-start.3 = (bf16[512,384]{1,0:T(8,128)(2,1)}, bf16[512,384]{1,0:T(8,128)(2,1)S(1)}, u32[]{:S(2)}, u32[]{:S(2)}) collective-permute-start(bf16[512,384]{1,0:T(8,128)(2,1)} %dynamic-slice_bitcast_fusion.2), channel_id=1, source_target_pairs={{0,32},{32,0},{1,33},{33,1},{2,34},{34,2},{3,35},{35,3},{4,36},{36... | collective-permute-start | bytes 1179656 | tf_op jit(solution)/shard_map/ppermute | solution.py:45
  83.2 12.6 %copy-start = (bf16[2,512,384]{2,1,0:T(8,128)(2,1)S(1)}, bf16[2,512,384]{2,1,0:T(8,128)(2,1)}, u32[]{:S(2)}) copy-start(bf16[2,512,384]{2,1,0:T(8,128)(2,1)} %dw_ref) | copy-start | bytes 2359300
  130.1 9.4 %collective-permute-start.4 = (f32[20,384]{1,0:T(8,128)S(1)}, f32[20,384]{1,0:T(8,128)S(1)}, u32[]{:S(2)}, u32[]{:S(2)}) collective-permute-start(f32[20,384]{1,0:T(8,128)S(1)} %slice.41), channel_id=1, source_target_pairs={{0,32},{32,0},{1,33},{33,1},{2,34},{34,2},{3,35},{35,3},{4,36},{36... | collective-permute-start | bytes 92168 | tf_op jit(solution)/shard_map/ppermute | solution.py:45

commit v8 on v7

--- a/solution.py
+++ b/solution.py
@@ -8,12 +8,15 @@
 EXPW = 2
 CAP = 20
 SB = 128
-COL = ("y", "xh", "core")
-BLK = ("zh", "zl", "xl")
-SIZES = {"y": 4, "xh": 2, "core": 2, "zh": 8, "zl": 2, "xl": 2}
-ZH = SIZES["zh"]
-NEAR = SIZES["zl"] * SIZES["xl"]
-GROUP = SIZES["y"] * SIZES["xh"]
+COL = ("ya", "yb", "xh", "core")
+BLK = ("za", "zb", "zc", "zl", "xl")
+FAR = ("zc", "zb", "za")
+NEIGHBOURS = ("xl", "zl")
+PLANE = ("ya", "yb", "xh")
+SIZES = dict.fromkeys(COL + BLK, 2)
+ZH = 2 ** len(FAR)
+NEAR = 2 ** len(NEIGHBOURS)
+GROUP = 2 ** len(PLANE)
 F32 = jnp.float32
 BF16 = jnp.bfloat16
 SHIFT = 64.0
@@ -235,7 +238,7 @@
             down_scale,
         )
     )
-    far = gather(slot_rows, "zh", ZH).reshape(near_rows, 2 * width)
+    far = gather(slot_rows, FAR, ZH).reshape(near_rows, 2 * width)
 
     other = 1 - core
     core_index = jnp.reshape(core, (1,)).astype(jnp.int32)
@@ -272,19 +275,19 @@
             other_combine,
         )
     )
-    portion = gather(far, ("zl", "xl"), NEAR)
+    portion = gather(far, NEIGHBOURS, NEAR)
 
     partial_sums = gate_up(
         core_index, portion, gate_weight, up_weight, other_gate_up, own_scales, other_scales
     ).astype(jnp.float16)
-    received = trade(partial_sums, ("y", "xh"))
+    received = trade(partial_sums, PLANE)
     summed = jnp.sum(received.astype(F32), axis=0) * (1.0 / SHIFT)
     hidden = (jax.nn.silu(summed[:, :hidden_width]) * summed[:, hidden_width:]).astype(BF16)
-    hidden = gather(hidden, ("y", "xh"), GROUP)
+    hidden = gather(hidden, PLANE, GROUP)
     down = down_project(core_index, hidden, down_weight, other_down, own_scales, other_scales)
-    down = trade(down, ("zl", "xl"))
+    down = trade(down, NEIGHBOURS)
     down = jnp.sum(down.astype(F32), axis=0).astype(BF16)
-    down = trade(down.reshape(ZH, 8, -1), "zh")
+    down = trade(down.reshape(ZH, 8, -1), FAR)
     out = jnp.sum(down.astype(F32), axis=0).reshape(CAP, 2 * width)
     given = swap(out[:, width:])
     mixed = jnp.dot(own_combine, out[:, :width], precision=lax.Precision.HIGHEST)

time: 141 us -> 138 us (0.979)
  waiting for transfers between devices: 10.9 us -> 3.46 us
  blocking collectives: 82.5 us -> 86.1 us
    all_to_all x1, waiting for transfers between devices: 10.1 us -> 2.6 us  [trade(): return lax.all_to_all(value, axes, 0, 0, tiled=True)]
    all_to_all x5, blocking collectives: 82.5 us -> 86.1 us  [trade(): return lax.all_to_all(value, axes, 0, 0, tiled=True)]
where the time goes in v8:
time: 138 us; the launch traced here: 137 us
  blocking collectives  86.1 us (62%)
  starting transfers between devices  33.6 us (24%)
  Pallas kernels  4.49 us (3%)
  local copies, waits for them, and re-layouts  4.09 us (3%)
  waiting for transfers between devices  3.46 us (3%)
  other arithmetic  2.75 us (2%)
  matrix products  2.26 us (2%)
    all_to_all x5, blocking collectives, trade(): return lax.all_to_all(value, axes, 0, 0, tiled=True)  86.1 us
    ppermute x5, starting transfers between devices, swap(): return lax.ppermute(value, 'core', [(0, 1), (1, 0)])  24.2 us
    all_to_all x1, starting transfers between devices, trade(): return lax.all_to_all(value, axes, 0, 0, tiled=True)  9.45 us
  transfers between devices with their start and end apart: 6, of which 2 were waited for; matrix products, arithmetic and copies ran while one was open for 4% of the time, Pallas kernels for 0%

profile of v8, /device:TPU:1, one launch (start us, length us, event | category | flops | bytes accessed | tf_op | source)
XLA Modules:
  0.0 137.0 jit_solution(2524393140076067523)
XLA Ops:
  0.0 8.9 %collective-permute-start = (bf16[64,384]{1,0:T(8,128)(2,1)}, bf16[64,384]{1,0:T(8,128)(2,1)S(1)}, u32[]{:S(2)}, u32[]{:S(2)}) collective-permute-start(bf16[64,384]{1,0:T(8,128)(2,1)} %param.9), channel_id=1, source_target_pairs={{0,32},{32,0},{1,33},{33,1},{2,34},{34,2},{3,35},{35,3},{4,36},{36... | collective-permute-start | bytes 147464 | tf_op jit(solution)/shard_map/ppermute | solution.py:48
  8.9 0.7 compare_reduce_fusion
  9.7 0.1 copy.22
  9.8 0.1 reduce_window_sum.11
  9.9 0.9 convolution_convert_fusion.1
  10.9 0.1 convolution_convert_fusion
  11.1 0.7 broadcast_in_dim.14
  11.8 9.5 %all-to-all-start = ((bf16[8,8,1920]{2,1,0:T(8,128)(2,1)}), bf16[8,8,1920]{2,1,0:T(8,128)(2,1)S(1)}, u32[]{:S(2)}, u32[]{:S(2)}) async-start(bf16[8,8,1920]{2,1,0:T(8,128)(2,1)} %broadcast_in_dim.14), calls=%async_computation | async-start | bytes 491520 | tf_op jit(solution)/shard_map/all_to_all | solution.py:52
  21.2 1.8 %dynamic-slice_bitcast_fusion.2 = bf16[512,384]{1,0:T(8,128)(2,1)} fusion(bf16[2,512,384]{2,1,0:T(8,128)(2,1)} %dw_ref, s32[]{:T(128)S(6)} %select_n.51), kind=kLoop, calls=%fused_computation.9 | loop fusion | bytes 786436 | tf_op jit(solution)/shard_map/jit(dynamic_index_in_dim)/squeeze | solution.py:60
  23.0 0.1 copy.25
  23.5 0.9 pad_maximum_fusion
  24.4 2.2 %collective-permute-start.2 = (bf16[768,512]{1,0:T(8,128)(2,1)}, bf16[768,512]{1,0:T(8,128)(2,1)S(1)}, u32[]{:S(2)}, u32[]{:S(2)}) collective-permute-start(bf16[768,512]{1,0:T(8,128)(2,1)} %pad_maximum_fusion), channel_id=1, source_target_pairs={{0,32},{32,0},{1,33},{33,1},{2,34},{34,2},{3,35},{35,3},{4,36},{36... | collective-permute-start | bytes 2359304 | tf_op jit(solution)/shard_map/ppermute | solution.py:48
  26.7 2.1 %collective-permute-start.1 = (f32[1,36]{1,0:T(1,128)S(1)}, f32[1,36]{1,0:T(1,128)S(1)}, u32[]{:S(2)}, u32[]{:S(2)}) collective-permute-start(f32[1,36]{1,0:T(1,128)S(1)} %pad_maximum_fusion.3), channel_id=1, source_target_pairs={{0,32},{32,0},{1,33},{33,1},{2,34},{34,2},{3,35},{35,3},{4,36},{36... | collective-permute-start | bytes 440 | tf_op jit(solution)/shard_map/ppermute | solution.py:48
  28.8 2.2 %collective-permute-start.3 = (bf16[512,384]{1,0:T(8,128)(2,1)}, bf16[512,384]{1,0:T(8,128)(2,1)S(1)}, u32[]{:S(2)}, u32[]{:S(2)}) collective-permute-start(bf16[512,384]{1,0:T(8,128)(2,1)} %dynamic-slice_bitcast_fusion.2), channel_id=1, source_target_pairs={{0,32},{32,0},{1,33},{33,1},{2,34},{34,2},{3,35},{35,3},{4,36},{36... | collective-permute-start | bytes 1179656 | tf_op jit(solution)/shard_map/ppermute | solution.py:48
  31.1 0.1 copy.24
  31.5 2.6 %all-to-all-done = bf16[8,8,1920]{2,1,0:T(8,128)(2,1)S(1)} async-done(((bf16[8,8,1920]{2,1,0:T(8,128)(2,1)}), bf16[8,8,1920]{2,1,0:T(8,128)(2,1)S(1)}, u32[]{:S(2)}, u32[]{:S(2)}) %all-to-all-start) | async-done | bytes 245792 | tf_op jit(solution)/shard_map/all_to_all | solution.py:52
  34.1 0.2 reshape.63
  34.4 18.0 %all_to_all.30.x_ref = bf16[4,160,768]{2,1,0:T(8,128)(2,1)S(1)} all-to-all(bf16[4,160,768]{2,1,0:T(8,128)(2,1)S(1)} %broadcast_in_dim.21), channel_id=1, replica_groups=mesh['ya'=2,'yb'=2,'xh'=2,'core'=2,'za'=2,'zb'=2,'zc'=2,'zl'=2,'xl'=2] {..., dimensions={0} | all-to-all | bytes 1966080 | tf_op jit(solution)/shard_map/all_to_all | solution.py:52
  52.5 2.7 %gate_up.1 = f32[8,80,1024]{2,1,0:T(8,128)S(1)} custom-call(s32[1]{0:T(128)} %bitcast.1.core_ref, f32[1,36]{1,0:T(1,128)S(1)} %pad_maximum_fusion.2.os_ref, f32[1,36]{1,0:T(1,128)S(1)} %collective-permute-done.1.rs_ref, bf16[4,160,768]{2,1,0:T(8,128)(2,1)S(1)} %all_to_all.30.x_ref, bf16[2,384,512]{2,1,0:T(8,128)(2,1)S(1)} %copy-done.1, ...), custom_call_target="tpu_custom_call" | custom-call | flops 1006632960 | bytes 5177344 | tf_op jit(solution)/shard_map/gate_up/pallas_call | solution.py:116
  55.2 0.2 convert_element_type.35
  55.5 23.4 %all_to_all.31 = f16[8,80,1024]{2,1,0:T(8,128)(2,1)S(1)} all-to-all(f16[8,80,1024]{2,1,0:T(8,128)(2,1)S(1)} %convert_element_type.35), channel_id=1, replica_groups=mesh['ya'=2,'yb'=2,'xh'=2,'core'=2,'za'=2,'zb'=2,'zc'=2,'zl'=2,'xl'=2] {..., dimensions={0} | all-to-all | bytes 2621440 | tf_op jit(solution)/shard_map/all_to_all | solution.py:52
  78.8 0.3 convert_reduce_fusion
  79.3 12.7 %all_to_all.32.h_ref = bf16[8,80,512]{2,1,0:T(8,128)(2,1)S(1)} all-to-all(bf16[8,80,512]{2,1,0:T(8,128)(2,1)S(1)} %broadcast_in_dim.22), channel_id=1, replica_groups=mesh['ya'=2,'yb'=2,'xh'=2,'core'=2,'za'=2,'zb'=2,'zc'=2,'zl'=2,'xl'=2] {..., dimensions={0} | all-to-all | bytes 1310720 | tf_op jit(solution)/shard_map/all_to_all | solution.py:52
  92.0 1.8 %down_project.1 = bf16[4,160,768]{2,1,0:T(8,128)(2,1)S(1)} custom-call(s32[1]{0:T(128)} %bitcast.1.core_ref, f32[1,36]{1,0:T(1,128)S(1)} %pad_maximum_fusion.2.os_ref, f32[1,36]{1,0:T(1,128)S(1)} %collective-permute-done.1.rs_ref, bf16[8,80,512]{2,1,0:T(8,128)(2,1)S(1)} %all_to_all.32.h_ref, bf16[2,512,384]{2,1,0:T(8,128)(2,1)S(1)} %copy-done, ...), custom_call_target="tpu_custom_call" | custom-call | flops 503316480 | bytes 2424832 | tf_op jit(solution)/shard_map/down_project/pallas_call | solution.py:167
  93.7 11.0 %all_to_all.33 = bf16[4,160,768]{2,1,0:T(8,128)(2,1)S(1)} all-to-all(bf16[4,160,768]{2,1,0:T(8,128)(2,1)S(1)} %down_project.1), channel_id=1, replica_groups=mesh['ya'=2,'yb'=2,'xh'=2,'core'=2,'za'=2,'zb'=2,'zc'=2,'zl'=2,'xl'=2] {..., dimensions={0} | all-to-all | bytes 1966080 | tf_op jit(solution)/shard_map/all_to_all | solution.py:52
  104.8 0.1 reduce_sum.41
  104.9 0.2 reshape.71
  105.1 21.0 %all_to_all.34 = bf16[8,8,1920]{2,1,0:T(8,128)(2,1)S(1)} all-to-all(bf16[8,8,1920]{2,1,0:T(8,128)(2,1)S(1)} %reshape.71), channel_id=1, replica_groups=mesh['ya'=2,'yb'=2,'xh'=2,'core'=2,'za'=2,'zb'=2,'zc'=2,'zl'=2,'xl'=2] {..., dimensions={0} | all-to-all | bytes 491520 | tf_op jit(solution)/shard_map/all_to_all | solution.py:52
  126.2 8.8 %collective-permute-start.4 = (f32[20,384]{1,0:T(8,128)S(1)}, f32[20,384]{1,0:T(8,128)S(1)}, u32[]{:S(2)}, u32[]{:S(2)}) collective-permute-start(f32[20,384]{1,0:T(8,128)S(1)} %slice.41), channel_id=1, source_target_pairs={{0,32},{32,0},{1,33},{33,1},{2,34},{34,2},{3,35},{35,3},{4,36},{36... | collective-permute-start | bytes 92168 | tf_op jit(solution)/shard_map/ppermute | solution.py:48
  135.0 0.8 collective-permute-done.4
  135.8 0.3 fusion.12
  136.1 0.9 fusion
  (47 shorter events, 1.2 us)
Async XLA Ops:
  0.0 23.0 %copy-start.3 = (f32[2,4,3]{1,0,2:T(2,128)S(1)}, f32[2,4,3]{1,0,2:T(2,128)}, u32[]{:S(2)}) copy-start(f32[2,4,3]{1,0,2:T(2,128)} %param.17) | copy-start | bytes 292
  0.0 23.2 %copy-start.5 = (f32[2,3,4]{2,0,1:T(2,128)S(1)}, f32[2,3,4]{2,0,1:T(2,128)}, u32[]{:S(2)}) copy-start(f32[2,3,4]{2,0,1:T(2,128)} %param.15) | copy-start | bytes 292
  0.0 23.2 %copy-start.4 = (f32[2,3,4]{2,0,1:T(2,128)S(1)}, f32[2,3,4]{2,0,1:T(2,128)}, u32[]{:S(2)}) copy-start(f32[2,3,4]{2,0,1:T(2,128)} %param.14) | copy-start | bytes 292
  0.0 23.4 %copy-start.2 = (bf16[2,384,512]{2,1,0:T(8,128)(2,1)S(1)}, bf16[2,384,512]{2,1,0:T(8,128)(2,1)}, u32[]{:S(2)}) copy-start(bf16[2,384,512]{2,1,0:T(8,128)(2,1)} %uw_ref) | copy-start | bytes 2359300
  0.0 23.4 %copy-start.1 = (bf16[2,384,512]{2,1,0:T(8,128)(2,1)S(1)}, bf16[2,384,512]{2,1,0:T(8,128)(2,1)}, u32[]{:S(2)}) copy-start(bf16[2,384,512]{2,1,0:T(8,128)(2,1)} %gw_ref) | copy-start | bytes 2359300
  0.0 10.8 %collective-permute-start = (bf16[64,384]{1,0:T(8,128)(2,1)}, bf16[64,384]{1,0:T(8,128)(2,1)S(1)}, u32[]{:S(2)}, u32[]{:S(2)}) collective-permute-start(bf16[64,384]{1,0:T(8,128)(2,1)} %param.9), channel_id=1, source_target_pairs={{0,32},{32,0},{1,33},{33,1},{2,34},{34,2},{3,35},{35,3},{4,36},{36... | collective-permute-start | bytes 147464 | tf_op jit(solution)/shard_map/ppermute | solution.py:48
  11.8 22.3 %all-to-all-start = ((bf16[8,8,1920]{2,1,0:T(8,128)(2,1)}), bf16[8,8,1920]{2,1,0:T(8,128)(2,1)S(1)}, u32[]{:S(2)}, u32[]{:S(2)}) async-start(bf16[8,8,1920]{2,1,0:T(8,128)(2,1)} %broadcast_in_dim.14), calls=%async_computation | async-start | bytes 491520 | tf_op jit(solution)/shard_map/all_to_all | solution.py:52
  23.4 7.6 %copy-start.6 = (s32[64,2]{0,1:T(2,128)S(1)}, s32[64,2]{0,1:T(2,128)}, u32[]{:S(2)}) copy-start(s32[64,2]{0,1:T(2,128)} %param.10) | copy-start | bytes 1540
  23.4 7.6 %copy-start.7 = (f32[64,2]{0,1:T(2,128)S(1)}, f32[64,2]{0,1:T(2,128)}, u32[]{:S(2)}) copy-start(f32[64,2]{0,1:T(2,128)} %param.11) | copy-start | bytes 1540
  24.4 9.9 %collective-permute-start.2 = (bf16[768,512]{1,0:T(8,128)(2,1)}, bf16[768,512]{1,0:T(8,128)(2,1)S(1)}, u32[]{:S(2)}, u32[]{:S(2)}) collective-permute-start(bf16[768,512]{1,0:T(8,128)(2,1)} %pad_maximum_fusion), channel_id=1, source_target_pairs={{0,32},{32,0},{1,33},{33,1},{2,34},{34,2},{3,35},{35,3},{4,36},{36... | collective-permute-start | bytes 2359304 | tf_op jit(solution)/shard_map/ppermute | solution.py:48
  26.7 7.6 %collective-permute-start.1 = (f32[1,36]{1,0:T(1,128)S(1)}, f32[1,36]{1,0:T(1,128)S(1)}, u32[]{:S(2)}, u32[]{:S(2)}) collective-permute-start(f32[1,36]{1,0:T(1,128)S(1)} %pad_maximum_fusion.3), channel_id=1, source_target_pairs={{0,32},{32,0},{1,33},{33,1},{2,34},{34,2},{3,35},{35,3},{4,36},{36... | collective-permute-start | bytes 440 | tf_op jit(solution)/shard_map/ppermute | solution.py:48
  28.8 5.5 %collective-permute-start.3 = (bf16[512,384]{1,0:T(8,128)(2,1)}, bf16[512,384]{1,0:T(8,128)(2,1)S(1)}, u32[]{:S(2)}, u32[]{:S(2)}) collective-permute-start(bf16[512,384]{1,0:T(8,128)(2,1)} %dynamic-slice_bitcast_fusion.2), channel_id=1, source_target_pairs={{0,32},{32,0},{1,33},{33,1},{2,34},{34,2},{3,35},{35,3},{4,36},{36... | collective-permute-start | bytes 1179656 | tf_op jit(solution)/shard_map/ppermute | solution.py:48
  79.1 12.8 %copy-start = (bf16[2,512,384]{2,1,0:T(8,128)(2,1)S(1)}, bf16[2,512,384]{2,1,0:T(8,128)(2,1)}, u32[]{:S(2)}) copy-start(bf16[2,512,384]{2,1,0:T(8,128)(2,1)} %dw_ref) | copy-start | bytes 2359300
  126.2 9.6 %collective-permute-start.4 = (f32[20,384]{1,0:T(8,128)S(1)}, f32[20,384]{1,0:T(8,128)S(1)}, u32[]{:S(2)}, u32[]{:S(2)}) collective-permute-start(f32[20,384]{1,0:T(8,128)S(1)} %slice.41), channel_id=1, source_target_pairs={{0,32},{32,0},{1,33},{33,1},{2,34},{34,2},{3,35},{35,3},{4,36},{36... | collective-permute-start | bytes 92168 | tf_op jit(solution)/shard_map/ppermute | solution.py:48

commit v9 on v8

--- a/solution.py
+++ b/solution.py
@@ -12,7 +12,7 @@
 BLK = ("za", "zb", "zc", "zl", "xl")
 FAR = ("zc", "zb", "za")
 NEIGHBOURS = ("xl", "zl")
-PLANE = ("ya", "yb", "xh")
+PLANE = ("xh", "yb", "ya")
 SIZES = dict.fromkeys(COL + BLK, 2)
 ZH = 2 ** len(FAR)
 NEAR = 2 ** len(NEIGHBOURS)
@@ -208,11 +208,9 @@
     other_tokens = swap(tokens)
     onehot = dispatch(route_ids)
     own = jnp.where(zero, onehot[:, 0], onehot[:, 1]).astype(BF16)
-    slot_rows = [
-        jnp.einsum("tc,td->cd", own, part, preferred_element_type=F32).astype(BF16)
-        for part in (tokens, other_tokens)
-    ]
-    slot_rows = jnp.concatenate(slot_rows, axis=1).reshape(8, -1)
+    both_tokens = jnp.concatenate([tokens, other_tokens], axis=1)
+    slot_rows = jnp.einsum("tc,td->cd", own, both_tokens, preferred_element_type=F32)
+    slot_rows = slot_rows.astype(BF16).reshape(8, -1)
     (
         slot_rows,
         onehot,

time: 138 us -> 138 us (level)
  transfers between devices with their start and end apart: 6 -> 6, of which waited for: 2 -> 3; matrix products, arithmetic and copies ran while one was open for 4% -> 4% of each run, Pallas kernels for 0% -> 0%
where the time goes in v9:
time: 138 us; the launch traced here: 137 us
  blocking collectives  87.2 us (63%)
  starting transfers between devices  33.6 us (24%)
  Pallas kernels  4.5 us (3%)
  local copies, waits for them, and re-layouts  4.1 us (3%)
  other arithmetic  2.74 us (2%)
  waiting for transfers between devices  2.74 us (2%)
  matrix products  2.14 us (2%)
    all_to_all x5, blocking collectives, trade(): return lax.all_to_all(value, axes, 0, 0, tiled=True)  87.2 us
    ppermute x5, starting transfers between devices, swap(): return lax.ppermute(value, 'core', [(0, 1), (1, 0)])  24.1 us
    all_to_all x1, starting transfers between devices, trade(): return lax.all_to_all(value, axes, 0, 0, tiled=True)  9.45 us
  transfers between devices with their start and end apart: 6, of which 3 were waited for; matrix products, arithmetic and copies ran while one was open for 4% of the time, Pallas kernels for 0%

profile of v9, /device:TPU:1, one launch (start us, length us, event | category | flops | bytes accessed | tf_op | source)
XLA Modules:
  0.0 137.2 jit_solution(2716454706865752539)
XLA Ops:
  0.0 8.9 %collective-permute-start = (bf16[64,384]{1,0:T(8,128)(2,1)}, bf16[64,384]{1,0:T(8,128)(2,1)S(1)}, u32[]{:S(2)}, u32[]{:S(2)}) collective-permute-start(bf16[64,384]{1,0:T(8,128)(2,1)} %param.9), channel_id=1, source_target_pairs={{0,32},{32,0},{1,33},{33,1},{2,34},{34,2},{3,35},{35,3},{4,36},{36... | collective-permute-start | bytes 147464 | tf_op jit(solution)/shard_map/ppermute | solution.py:48
  8.9 0.7 compare_reduce_fusion
  9.6 0.1 copy.22
  9.7 0.1 reduce_window_sum.11
  10.0 0.9 convolution_convert_fusion
  11.0 0.7 broadcast_in_dim.14
  11.7 9.5 %all-to-all-start = ((bf16[8,8,1920]{2,1,0:T(8,128)(2,1)}), bf16[8,8,1920]{2,1,0:T(8,128)(2,1)S(1)}, u32[]{:S(2)}, u32[]{:S(2)}) async-start(bf16[8,8,1920]{2,1,0:T(8,128)(2,1)} %broadcast_in_dim.14), calls=%async_computation | async-start | bytes 491520 | tf_op jit(solution)/shard_map/all_to_all | solution.py:52
  21.2 1.8 %dynamic-slice_bitcast_fusion.2 = bf16[512,384]{1,0:T(8,128)(2,1)} fusion(bf16[2,512,384]{2,1,0:T(8,128)(2,1)} %dw_ref, s32[]{:T(128)S(6)} %select_n.51), kind=kLoop, calls=%fused_computation.8 | loop fusion | bytes 786436 | tf_op jit(solution)/shard_map/jit(dynamic_index_in_dim)/squeeze | solution.py:60
  23.0 0.1 copy.25
  23.0 0.1 reshape.70
  23.4 0.9 pad_maximum_fusion
  24.4 2.5 %collective-permute-start.2 = (bf16[768,512]{1,0:T(8,128)(2,1)}, bf16[768,512]{1,0:T(8,128)(2,1)S(1)}, u32[]{:S(2)}, u32[]{:S(2)}) collective-permute-start(bf16[768,512]{1,0:T(8,128)(2,1)} %pad_maximum_fusion), channel_id=1, source_target_pairs={{0,32},{32,0},{1,33},{33,1},{2,34},{34,2},{3,35},{35,3},{4,36},{36... | collective-permute-start | bytes 2359304 | tf_op jit(solution)/shard_map/ppermute | solution.py:48
  27.0 1.9 %collective-permute-start.1 = (f32[1,36]{1,0:T(1,128)S(1)}, f32[1,36]{1,0:T(1,128)S(1)}, u32[]{:S(2)}, u32[]{:S(2)}) collective-permute-start(f32[1,36]{1,0:T(1,128)S(1)} %pad_maximum_fusion.2), channel_id=1, source_target_pairs={{0,32},{32,0},{1,33},{33,1},{2,34},{34,2},{3,35},{35,3},{4,36},{36... | collective-permute-start | bytes 440 | tf_op jit(solution)/shard_map/ppermute | solution.py:48
  28.9 2.4 %collective-permute-start.3 = (bf16[512,384]{1,0:T(8,128)(2,1)}, bf16[512,384]{1,0:T(8,128)(2,1)S(1)}, u32[]{:S(2)}, u32[]{:S(2)}) collective-permute-start(bf16[512,384]{1,0:T(8,128)(2,1)} %dynamic-slice_bitcast_fusion.2), channel_id=1, source_target_pairs={{0,32},{32,0},{1,33},{33,1},{2,34},{34,2},{3,35},{35,3},{4,36},{36... | collective-permute-start | bytes 1179656 | tf_op jit(solution)/shard_map/ppermute | solution.py:48
  31.4 0.1 copy.24
  31.8 1.8 %all-to-all-done = bf16[8,8,1920]{2,1,0:T(8,128)(2,1)S(1)} async-done(((bf16[8,8,1920]{2,1,0:T(8,128)(2,1)}), bf16[8,8,1920]{2,1,0:T(8,128)(2,1)S(1)}, u32[]{:S(2)}, u32[]{:S(2)}) %all-to-all-start) | async-done | bytes 245792 | tf_op jit(solution)/shard_map/all_to_all | solution.py:52
  33.6 0.2 reshape.63
  33.9 17.0 %all_to_all.30.x_ref = bf16[4,160,768]{2,1,0:T(8,128)(2,1)S(1)} all-to-all(bf16[4,160,768]{2,1,0:T(8,128)(2,1)S(1)} %broadcast_in_dim.21), channel_id=1, replica_groups=mesh['ya'=2,'yb'=2,'xh'=2,'core'=2,'za'=2,'zb'=2,'zc'=2,'zl'=2,'xl'=2] {..., dimensions={0} | all-to-all | bytes 1966080 | tf_op jit(solution)/shard_map/all_to_all | solution.py:52
  51.0 2.7 %gate_up.1 = f32[8,80,1024]{2,1,0:T(8,128)S(1)} custom-call(s32[1]{0:T(128)} %bitcast.1.core_ref, f32[1,36]{1,0:T(1,128)S(1)} %pad_maximum_fusion.1.os_ref, f32[1,36]{1,0:T(1,128)S(1)} %collective-permute-done.1.rs_ref, bf16[4,160,768]{2,1,0:T(8,128)(2,1)S(1)} %all_to_all.30.x_ref, bf16[2,384,512]{2,1,0:T(8,128)(2,1)S(1)} %copy-done.1, ...), custom_call_target="tpu_custom_call" | custom-call | flops 1006632960 | bytes 5177344 | tf_op jit(solution)/shard_map/gate_up/pallas_call | solution.py:116
  53.7 0.2 convert_element_type.31
  54.0 21.7 %all_to_all.31 = f16[8,80,1024]{2,1,0:T(8,128)(2,1)S(1)} all-to-all(f16[8,80,1024]{2,1,0:T(8,128)(2,1)S(1)} %convert_element_type.31), channel_id=1, replica_groups=mesh['ya'=2,'yb'=2,'xh'=2,'core'=2,'za'=2,'zb'=2,'zc'=2,'zl'=2,'xl'=2] {..., dimensions={0} | all-to-all | bytes 2621440 | tf_op jit(solution)/shard_map/all_to_all | solution.py:52
  75.7 0.3 convert_reduce_fusion
  76.2 13.0 %all_to_all.32.h_ref = bf16[8,80,512]{2,1,0:T(8,128)(2,1)S(1)} all-to-all(bf16[8,80,512]{2,1,0:T(8,128)(2,1)S(1)} %broadcast_in_dim.22), channel_id=1, replica_groups=mesh['ya'=2,'yb'=2,'xh'=2,'core'=2,'za'=2,'zb'=2,'zc'=2,'zl'=2,'xl'=2] {..., dimensions={0} | all-to-all | bytes 1310720 | tf_op jit(solution)/shard_map/all_to_all | solution.py:52
  89.2 1.8 %down_project.1 = bf16[4,160,768]{2,1,0:T(8,128)(2,1)S(1)} custom-call(s32[1]{0:T(128)} %bitcast.1.core_ref, f32[1,36]{1,0:T(1,128)S(1)} %pad_maximum_fusion.1.os_ref, f32[1,36]{1,0:T(1,128)S(1)} %collective-permute-done.1.rs_ref, bf16[8,80,512]{2,1,0:T(8,128)(2,1)S(1)} %all_to_all.32.h_ref, bf16[2,512,384]{2,1,0:T(8,128)(2,1)S(1)} %copy-done, ...), custom_call_target="tpu_custom_call" | custom-call | flops 503316480 | bytes 2424832 | tf_op jit(solution)/shard_map/down_project/pallas_call | solution.py:167
  90.9 11.8 %all_to_all.33 = bf16[4,160,768]{2,1,0:T(8,128)(2,1)S(1)} all-to-all(bf16[4,160,768]{2,1,0:T(8,128)(2,1)S(1)} %down_project.1), channel_id=1, replica_groups=mesh['ya'=2,'yb'=2,'xh'=2,'core'=2,'za'=2,'zb'=2,'zc'=2,'zl'=2,'xl'=2] {..., dimensions={0} | all-to-all | bytes 1966080 | tf_op jit(solution)/shard_map/all_to_all | solution.py:52
  102.7 0.1 reduce_sum.41
  102.9 0.2 reshape.71
  103.1 23.6 %all_to_all.34 = bf16[8,8,1920]{2,1,0:T(8,128)(2,1)S(1)} all-to-all(bf16[8,8,1920]{2,1,0:T(8,128)(2,1)S(1)} %reshape.71), channel_id=1, replica_groups=mesh['ya'=2,'yb'=2,'xh'=2,'core'=2,'za'=2,'zb'=2,'zc'=2,'zl'=2,'xl'=2] {..., dimensions={0} | all-to-all | bytes 491520 | tf_op jit(solution)/shard_map/all_to_all | solution.py:52
  126.8 8.4 %collective-permute-start.4 = (f32[20,384]{1,0:T(8,128)S(1)}, f32[20,384]{1,0:T(8,128)S(1)}, u32[]{:S(2)}, u32[]{:S(2)}) collective-permute-start(f32[20,384]{1,0:T(8,128)S(1)} %slice.41), channel_id=1, source_target_pairs={{0,32},{32,0},{1,33},{33,1},{2,34},{34,2},{3,35},{35,3},{4,36},{36... | collective-permute-start | bytes 92168 | tf_op jit(solution)/shard_map/ppermute | solution.py:48
  135.2 0.8 collective-permute-done.4
  136.0 0.3 fusion.17
  136.3 0.9 fusion
  (45 shorter events, 1.2 us)
Async XLA Ops:
  0.0 22.9 %copy-start.3 = (f32[2,4,3]{1,0,2:T(2,128)S(1)}, f32[2,4,3]{1,0,2:T(2,128)}, u32[]{:S(2)}) copy-start(f32[2,4,3]{1,0,2:T(2,128)} %param.17) | copy-start | bytes 292
  0.0 23.1 %copy-start.5 = (f32[2,3,4]{2,0,1:T(2,128)S(1)}, f32[2,3,4]{2,0,1:T(2,128)}, u32[]{:S(2)}) copy-start(f32[2,3,4]{2,0,1:T(2,128)} %param.15) | copy-start | bytes 292
  0.0 23.1 %copy-start.4 = (f32[2,3,4]{2,0,1:T(2,128)S(1)}, f32[2,3,4]{2,0,1:T(2,128)}, u32[]{:S(2)}) copy-start(f32[2,3,4]{2,0,1:T(2,128)} %param.14) | copy-start | bytes 292
  0.0 23.3 %copy-start.2 = (bf16[2,384,512]{2,1,0:T(8,128)(2,1)S(1)}, bf16[2,384,512]{2,1,0:T(8,128)(2,1)}, u32[]{:S(2)}) copy-start(bf16[2,384,512]{2,1,0:T(8,128)(2,1)} %uw_ref) | copy-start | bytes 2359300
  0.0 23.3 %copy-start.1 = (bf16[2,384,512]{2,1,0:T(8,128)(2,1)S(1)}, bf16[2,384,512]{2,1,0:T(8,128)(2,1)}, u32[]{:S(2)}) copy-start(bf16[2,384,512]{2,1,0:T(8,128)(2,1)} %gw_ref) | copy-start | bytes 2359300
  0.0 10.0 %collective-permute-start = (bf16[64,384]{1,0:T(8,128)(2,1)}, bf16[64,384]{1,0:T(8,128)(2,1)S(1)}, u32[]{:S(2)}, u32[]{:S(2)}) collective-permute-start(bf16[64,384]{1,0:T(8,128)(2,1)} %param.9), channel_id=1, source_target_pairs={{0,32},{32,0},{1,33},{33,1},{2,34},{34,2},{3,35},{35,3},{4,36},{36... | collective-permute-start | bytes 147464 | tf_op jit(solution)/shard_map/ppermute | solution.py:48
  11.7 21.9 %all-to-all-start = ((bf16[8,8,1920]{2,1,0:T(8,128)(2,1)}), bf16[8,8,1920]{2,1,0:T(8,128)(2,1)S(1)}, u32[]{:S(2)}, u32[]{:S(2)}) async-start(bf16[8,8,1920]{2,1,0:T(8,128)(2,1)} %broadcast_in_dim.14), calls=%async_computation | async-start | bytes 491520 | tf_op jit(solution)/shard_map/all_to_all | solution.py:52
  23.3 8.0 %copy-start.6 = (s32[64,2]{0,1:T(2,128)S(1)}, s32[64,2]{0,1:T(2,128)}, u32[]{:S(2)}) copy-start(s32[64,2]{0,1:T(2,128)} %param.10) | copy-start | bytes 1540
  23.3 8.0 %copy-start.7 = (f32[64,2]{0,1:T(2,128)S(1)}, f32[64,2]{0,1:T(2,128)}, u32[]{:S(2)}) copy-start(f32[64,2]{0,1:T(2,128)} %param.11) | copy-start | bytes 1540
  24.4 9.5 %collective-permute-start.2 = (bf16[768,512]{1,0:T(8,128)(2,1)}, bf16[768,512]{1,0:T(8,128)(2,1)S(1)}, u32[]{:S(2)}, u32[]{:S(2)}) collective-permute-start(bf16[768,512]{1,0:T(8,128)(2,1)} %pad_maximum_fusion), channel_id=1, source_target_pairs={{0,32},{32,0},{1,33},{33,1},{2,34},{34,2},{3,35},{35,3},{4,36},{36... | collective-permute-start | bytes 2359304 | tf_op jit(solution)/shard_map/ppermute | solution.py:48
  27.0 6.9 %collective-permute-start.1 = (f32[1,36]{1,0:T(1,128)S(1)}, f32[1,36]{1,0:T(1,128)S(1)}, u32[]{:S(2)}, u32[]{:S(2)}) collective-permute-start(f32[1,36]{1,0:T(1,128)S(1)} %pad_maximum_fusion.2), channel_id=1, source_target_pairs={{0,32},{32,0},{1,33},{33,1},{2,34},{34,2},{3,35},{35,3},{4,36},{36... | collective-permute-start | bytes 440 | tf_op jit(solution)/shard_map/ppermute | solution.py:48
  28.9 4.9 %collective-permute-start.3 = (bf16[512,384]{1,0:T(8,128)(2,1)}, bf16[512,384]{1,0:T(8,128)(2,1)S(1)}, u32[]{:S(2)}, u32[]{:S(2)}) collective-permute-start(bf16[512,384]{1,0:T(8,128)(2,1)} %dynamic-slice_bitcast_fusion.2), channel_id=1, source_target_pairs={{0,32},{32,0},{1,33},{33,1},{2,34},{34,2},{3,35},{35,3},{4,36},{36... | collective-permute-start | bytes 1179656 | tf_op jit(solution)/shard_map/ppermute | solution.py:48
  76.0 13.2 %copy-start = (bf16[2,512,384]{2,1,0:T(8,128)(2,1)S(1)}, bf16[2,512,384]{2,1,0:T(8,128)(2,1)}, u32[]{:S(2)}) copy-start(bf16[2,512,384]{2,1,0:T(8,128)(2,1)} %dw_ref) | copy-start | bytes 2359300
  126.8 9.2 %collective-permute-start.4 = (f32[20,384]{1,0:T(8,128)S(1)}, f32[20,384]{1,0:T(8,128)S(1)}, u32[]{:S(2)}, u32[]{:S(2)}) collective-permute-start(f32[20,384]{1,0:T(8,128)S(1)} %slice.41), channel_id=1, source_target_pairs={{0,32},{32,0},{1,33},{33,1},{2,34},{34,2},{3,35},{35,3},{4,36},{36... | collective-permute-start | bytes 92168 | tf_op jit(solution)/shard_map/ppermute | solution.py:48
